TPU v7x, 32 devices: a whole 2x2x4 slice. The times are simulated.
32 devices in a mesh: parts: 2 (over x), lon: 16 (over z, y, core).
Axes of the slice: x: 2, y: 2, z: 4, core: 2. Of those that a mesh axis runs over, the one named last changes fastest.
Arguments:
- ocean_state: bfloat16 [64, 512, 256], P('parts', 'lon'), parts along dimension 0, may hold values from -6 to 6
- land_sea: int32 [32, 512], replicated, may hold values 0 or 1
- conv_weight: bfloat16 [3, 9, 256, 256], replicated, may hold values from -0.125 to 0.125
- up_weight: bfloat16 [3, 256, 1024], replicated, may hold values from -0.375 to 0.375
- down_weight: bfloat16 [3, 1024, 256], replicated, may hold values from -0.1875 to 0.1875
Outputs:
- next_state: bfloat16 [64, 512, 256], P('parts', 'lon'), parts along dimension 0
There are 2 independent parts, one for each index of `parts`. A program takes and returns all parts, laid end to end along the dimension named above; an argument that names none is the same for every part. Nothing has to cross between parts.
All inputs are finite; a program needn't handle non-finite values.
Results may differ from a plain program's by a relative error of at most 0.009.
Values may be sent and summed in bfloat16 or wider, within the bound.
No kernel may reach another device: no remote copies, remote signals or barrier semaphores. Data moves between devices by JAX's collectives and lax.ppermute only.
A program may use at most 64 MiB of HBM per device.

v0:
```python
import functools

import jax
import jax.numpy as jnp
import numpy as np
from jax import lax
from jax.experimental import pallas as pl
from jax.experimental.pallas import tpu as pltpu
from jax.sharding import PartitionSpec as P

BF = jnp.bfloat16
F32 = jnp.float32
HALO = 16
DEEP = 14
RSQRT2 = np.float32(0.7071067811865476)


def conv_norm(layer, shifted, width, base, chunks, w_ref, nrm):
    dil = 2 ** (layer + 1)
    weight = w_ref[layer].reshape(-1, w_ref.shape[-1])
    at = 0
    for first, count, turned in chunks:
        taps = [(a, b) for a in range(3) for b in range(3)]
        if turned:
            taps = taps[::-1]
        size = count * width
        lhs = jnp.concatenate(
            [
                shifted[b, (first - base + (a - 1) * dil) * width : (first - base + (a - 1) * dil) * width + size]
                for a, b in taps
            ],
            axis=1,
        )
        conv = jnp.dot(lhs, weight, preferred_element_type=F32)
        mean = jnp.mean(conv, axis=-1, keepdims=True)
        centred = conv - mean
        var = jnp.mean(centred * centred, axis=-1, keepdims=True)
        nrm[at : at + size] = (centred * lax.rsqrt(var + 1e-05)).astype(BF)
        at += size


def mlp(layer, shifted, width, base, first, counts, up_ref, down_ref, mask_ref, nrm, store):
    at = 0
    row = first
    for count in counts:
        size = count * width
        pre = jnp.dot(nrm[at : at + size], up_ref[layer], preferred_element_type=F32)
        hidden = (0.5 * pre * (1.0 + lax.erf(pre * RSQRT2))).astype(BF)
        branch = jnp.dot(hidden, down_ref[layer], preferred_element_type=F32)
        centre = shifted[1, (row - base) * width : (row - base) * width + size].astype(F32)
        mask = mask_ref[row * width : row * width + size].astype(F32)
        mask = jnp.concatenate([mask, mask], axis=1)
        store(row, count, (mask * (centre + branch)).astype(BF))
        at += size
        row += count


def spread(shifted, width, at_row, values, start, dil):
    for b in range(3):
        lo = start + (b - 1) * dil
        shifted[b, at_row * width : (at_row + 1) * width] = values[lo : lo + width]


def spread_ref(shifted, width, at_row, ref, offset, start, dil):
    for b in range(3):
        lo = offset + start + (b - 1) * dil
        shifted[b, at_row * width : (at_row + 1) * width] = ref[lo : lo + width]


def south_kernel(
    left, own, right, m1, m2, m3, w, up, down, x1_tail, x2_tail, out, sh1, sh2, sh3, x1, x2, nrm
):
    for sh, rows, width in ((sh1, 2, 56), (sh2, 4, 48), (sh3, 8, 32)):
        for b in range(3):
            sh[b, : rows * width] = jnp.zeros((rows * width, 256), BF)
    for row in range(32):
        values = jnp.concatenate([left[row], own[row], right[row]], axis=0)
        spread(sh1, 56, row + 2, values, 4, 2)
    conv_norm(0, sh1, 56, -2, [(0, 8, False), (8, 8, False), (16, 8, False), (24, 6, False)], w, nrm)

    def store1(row, count, value):
        x1[row * 56 : (row + count) * 56] = value

    mlp(0, sh1, 56, -2, 0, [8, 8, 8, 6], up, down, m1, nrm, store1)
    x1_tail[...] = x1[22 * 56 : 30 * 56]
    for row in range(30):
        spread_ref(sh2, 48, row + 4, x1, row * 56, 4, 4)
    conv_norm(1, sh2, 48, -4, [(0, 10, False), (10, 8, False), (18, 8, False)], w, nrm)

    def store2(row, count, value):
        x2[row * 48 : (row + count) * 48] = value

    mlp(1, sh2, 48, -4, 0, [10, 8, 8], up, down, m2, nrm, store2)
    x2_tail[...] = x2[10 * 48 : 26 * 48]
    for row in range(26):
        spread_ref(sh3, 32, row + 8, x2, row * 48, 8, 8)
    conv_norm(2, sh3, 32, -8, [(0, 18, False)], w, nrm)

    def store3(row, count, value):
        out[row : row + count] = value.reshape(count, 32, 256)

    mlp(2, sh3, 32, -8, 0, [18], up, down, m3, nrm, store3)


def north_kernel(
    left, own, right, north, north_left, north_right, x1_tail, x2_tail, out_south,
    m1, m2, m3, w, up, down, out, sh1, sh2, sh3, x1, x2, nrm,
):
    out[0:18] = out_south[...]
    for row in range(4):
        values = jnp.concatenate([left[28 + row], own[28 + row], right[28 + row]], axis=0)
        spread(sh1, 56, row, values, 4, 2)
    for row in range(14):
        values = jnp.concatenate([north_left[row], north[row], north_right[row]], axis=0)
        spread(sh1, 56, row + 4, values, 4, 2)
    conv_norm(0, sh1, 56, 28, [(30, 2, False), (32, 12, True)], w, nrm)

    def store1(row, count, value):
        x1[(row - 30) * 56 : (row - 30 + count) * 56] = value

    mlp(0, sh1, 56, 28, 30, [8, 6], up, down, m1, nrm, store1)
    for row in range(8):
        spread_ref(sh2, 48, row, x1_tail, row * 56, 4, 4)
    for row in range(14):
        spread_ref(sh2, 48, row + 8, x1, row * 56, 4, 4)
    conv_norm(1, sh2, 48, 22, [(26, 6, False), (32, 8, True)], w, nrm)

    def store2(row, count, value):
        x2[(row - 26) * 48 : (row - 26 + count) * 48] = value

    mlp(1, sh2, 48, 22, 26, [14], up, down, m2, nrm, store2)
    for row in range(16):
        spread_ref(sh3, 32, row, x2_tail, row * 48, 8, 8)
    for row in range(14):
        spread_ref(sh3, 32, row + 16, x2, row * 48, 8, 8)
    conv_norm(2, sh3, 32, 10, [(18, 14, False)], w, nrm)

    def store3(row, count, value):
        out[row : row + count] = value.reshape(count, 32, 256)

    mlp(2, sh3, 32, 10, 18, [14], up, down, m3, nrm, store3)


def cost(cells):
    return pl.CostEstimate(
        flops=2 * cells * (9 * 256 * 256 + 2 * 256 * 1024), bytes_accessed=2**20, transcendentals=cells * 1024
    )


def call(kernel, name, outs, scratch_rows, cells, args):
    vmem = pl.BlockSpec(memory_space=pltpu.VMEM)
    r1, r2, r3, y1, y2, normed = scratch_rows
    return pl.pallas_call(
        kernel,
        name=name,
        out_shape=tuple(jax.ShapeDtypeStruct(shape, BF) for shape in outs),
        in_specs=[vmem] * len(args),
        out_specs=tuple(vmem for _ in outs),
        scratch_shapes=[
            pltpu.VMEM((3, r1 * 56, 256), BF),
            pltpu.VMEM((3, r2 * 48, 256), BF),
            pltpu.VMEM((3, r3 * 32, 256), BF),
            pltpu.VMEM((y1 * 56, 256), BF),
            pltpu.VMEM((y2 * 48, 256), BF),
            pltpu.VMEM((normed, 256), BF),
        ],
        compiler_params=pltpu.CompilerParams(vmem_limit_bytes=24 * 2**20),
        cost_estimate=cost(cells),
    )(*args)


def around(value, step):
    count = lax.axis_size("lon")
    return lax.ppermute(value, "lon", [(i, (i + step) % count) for i in range(count)])


def per_device(own, land_sea, w, up, down):
    count = lax.axis_size("lon")
    cols = own.shape[1]
    left = around(own[:, cols - HALO :], 1)
    right = around(own[:, :HALO], -1)
    strip = own[own.shape[0] - DEEP :][::-1, ::-1]
    north = lax.ppermute(strip, "lon", [(i, count - 1 - i) for i in range(count)])

    land = jnp.concatenate([land_sea, land_sea[::-1, ::-1][:DEEP]], axis=0).astype(BF)
    land = jnp.concatenate([land[:, -HALO:], land, land[:, :HALO]], axis=1)
    land = lax.dynamic_slice_in_dim(land, lax.axis_index("lon") * cols, cols + 2 * HALO, 1)

    def cells_mask(rows, margin):
        part = land[:rows, HALO - margin : HALO + cols + margin].reshape(-1, 1)
        return jnp.broadcast_to(part, (part.shape[0], 128))

    masks = (cells_mask(44, 12), cells_mask(40, 8), cells_mask(32, 0))
    weights = (w, up, down)
    x1_tail, x2_tail, out_south = call(
        south_kernel, "south", [(8 * 56, 256), (16 * 48, 256), (18, 32, 256)],
        (34, 34, 34, 30, 26, 30 * 56), 3504, (left, own, right, *masks, *weights),
    )
    north, x1_tail = lax.optimization_barrier((north, x1_tail))
    north_left = around(north[:, cols - HALO :], 1)
    north_right = around(north[:, :HALO], -1)
    (out,) = call(
        north_kernel, "north", [(32, 32, 256)], (18, 22, 30, 14, 14, 14 * 56), 1904,
        (left, own, right, north, north_left, north_right, x1_tail, x2_tail, out_south, *masks, *weights),
    )
    return out


def solution(mesh):
    in_specs = (P("parts", "lon", None), P(), P(), P(), P())
    out_specs = P("parts", "lon", None)
    return jax.shard_map(
        per_device, mesh=mesh, in_specs=in_specs, out_specs=out_specs, check_vma=False
    )
```

profile of v0, /device:TPU:0, one launch (start us, length us, event | category | flops | bytes accessed | tf_op | source)
XLA Modules:
  0.0 46.0 jit_solution(17082212975109305978)
XLA Ops:
  0.0 1.1 %fusion.5 = (bf16[32,16,256]{2,1,0:T(8,128)(2,1)S(1)}, bf16[32,16,256]{2,1,0:T(8,128)(2,1)S(1)}) fusion(bf16[32,32,256]{2,1,0:T(8,128)(2,1)} %own.3), kind=kLoop, calls=%fused_computation.11 | loop fusion | bytes 1048576 | tf_op jit(solution)/shard_map/slice | solution.py:181
  1.1 0.0 copy-start
  1.1 0.0 copy-start.2
  1.1 5.5 %collective-permute-start.1 = (bf16[32,16,256]{2,1,0:T(8,128)(2,1)S(1)}, bf16[32,16,256]{2,1,0:T(8,128)(2,1)S(1)}, u32[]{:S(2)}, u32[]{:S(2)}) collective-permute-start(bf16[32,16,256]{2,1,0:T(8,128)(2,1)S(1)} %get-tuple-element.15), channel_id=1, source_target_pairs={{0,15},{1,0},{2,1},{3,2},{4,3},{5,4},{6,5},{7,6},{8,7},{9,8},{10,9... | collective-permute-start | bytes 786440 | tf_op jit(solution)/shard_map/ppermute | solution.py:174
  6.6 0.0 collective-permute-start
  6.6 0.0 slice-done
  6.7 0.8 %rev.4 = bf16[14,32,256]{2,1,0:T(8,128)(2,1)} reverse(bf16[14,32,256]{2,1,0:T(8,128)(2,1)S(1)} %slice-done), dimensions={0,1} | reverse | bytes 458752 | tf_op jit(solution)/shard_map/rev | solution.py:182
  7.4 4.4 %collective-permute-start.2 = (bf16[14,32,256]{2,1,0:T(8,128)(2,1)}, bf16[14,32,256]{2,1,0:T(8,128)(2,1)S(1)}, u32[]{:S(2)}, u32[]{:S(2)}) collective-permute-start(bf16[14,32,256]{2,1,0:T(8,128)(2,1)} %rev.4), channel_id=1, source_target_pairs={{0,15},{1,14},{2,13},{3,12},{4,11},{5,10},{6,9},{7,8},{8,7},{9,6},... | collective-permute-start | bytes 688136 | tf_op jit(solution)/shard_map/ppermute | solution.py:183
  11.9 0.0 copy-done.4
  11.9 0.4 slice.40
  12.3 0.2 fusion.2
  12.4 0.1 slice.50
  12.5 0.1 slice.49
  12.6 0.1 slice.48
  12.7 0.1 broadcast_in_dim.25
  12.8 0.1 broadcast_in_dim.23
  12.8 0.1 broadcast_in_dim.21
  13.0 0.0 collective-permute-done.1.right
  13.0 3.6 %collective-permute-done.left = bf16[32,16,256]{2,1,0:T(8,128)(2,1)S(1)} collective-permute-done((bf16[32,16,256]{2,1,0:T(8,128)(2,1)S(1)}, bf16[32,16,256]{2,1,0:T(8,128)(2,1)S(1)}, u32[]{:S(2)}, u32[]{:S(2)}) %collective-permute-start) | collective-permute-done | bytes 262176 | tf_op jit(solution)/shard_map/ppermute | solution.py:174
  16.6 0.2 broadcast_in_dim.26.m3
  16.8 0.3 broadcast_in_dim.24.m2
  17.1 0.4 broadcast_in_dim.22.m1
  17.5 0.0 copy-start.1
  17.5 2.0 %copy-done.1 = bf16[3,9,256,256]{3,2,1,0:T(8,128)(2,1)S(1)} copy-done((bf16[3,9,256,256]{3,2,1,0:T(8,128)(2,1)S(1)}, bf16[3,9,256,256]{3,2,1,0:T(8,128)(2,1)}, u32[]{:S(2)}) %copy-start.1) | copy-done | bytes 3538968
  19.5 1.4 %copy-done.3 = bf16[3,1024,256]{2,1,0:T(8,128)(2,1)S(1)} copy-done((bf16[3,1024,256]{2,1,0:T(8,128)(2,1)S(1)}, bf16[3,1024,256]{2,1,0:T(8,128)(2,1)}, u32[]{:S(2)}) %copy-start.3) | copy-done | bytes 1572888
  20.9 9.8 %south.1 = (bf16[448,256]{1,0:T(8,128)(2,1)S(1)}, bf16[768,256]{1,0:T(8,128)(2,1)S(1)}, bf16[18,32,256]{2,1,0:T(8,128)(2,1)S(1)}) custom-call(bf16[32,16,256]{2,1,0:T(8,128)(2,1)S(1)} %collective-permute-done.left, bf16[32,32,256]{2,1,0:T(8,128)(2,1)S(1)} %copy-done, bf16[32,16,256]{2,1,0:T(8,128)(2,1)S(1)} %collective-permute-done.1.right, ...), custom_call_target="tpu_custom_call" | custom-call | flops 7807696896 | bytes 1048576 | tf_op jit(solution)/shard_map/south/pallas_call | solution.py:153
  30.7 0.0 collective-permute-done.2.north
  30.7 0.3 collective-permute-start.4
  31.0 0.3 collective-permute-start.3
  31.3 2.1 %collective-permute-done.4.north_right = bf16[14,16,256]{2,1,0:T(8,128)(2,1)S(1)} collective-permute-done((bf16[14,16,256]{2,1,0:T(8,128)(2,1)S(1)}, bf16[14,16,256]{2,1,0:T(8,128)(2,1)S(1)}, u32[]{:S(2)}, u32[]{:S(2)}) %collective-permute-start.4) | collective-permute-done | bytes 114720 | tf_op jit(solution)/shard_map/ppermute | solution.py:174
  33.4 4.6 %collective-permute-done.3.north_left = bf16[14,16,256]{2,1,0:T(8,128)(2,1)S(1)} collective-permute-done((bf16[14,16,256]{2,1,0:T(8,128)(2,1)S(1)}, bf16[14,16,256]{2,1,0:T(8,128)(2,1)S(1)}, u32[]{:S(2)}, u32[]{:S(2)}) %collective-permute-start.3) | collective-permute-done | bytes 114720 | tf_op jit(solution)/shard_map/ppermute | solution.py:174
  38.0 8.0 %north.1 = bf16[32,32,256]{2,1,0:T(8,128)(2,1)} custom-call(bf16[32,16,256]{2,1,0:T(8,128)(2,1)S(1)} %collective-permute-done.left, bf16[32,32,256]{2,1,0:T(8,128)(2,1)S(1)} %copy-done, bf16[32,16,256]{2,1,0:T(8,128)(2,1)S(1)} %collective-permute-done.1.right, bf16[14,32,256]{2,1,0:T(8,128)(2,1)S(1)} %collective-permute-done.2.north, ...), custom_call_target="tpu_custom_call" | custom-call | flops 4242538496 | bytes 1048576 | tf_op jit(solution)/shard_map/north/pallas_call | solution.py:153
  (9 shorter events, 0.0 us)
Async XLA Ops:
  0.0 6.6 %slice-start = ((bf16[32,32,256]{2,1,0:T(8,128)(2,1)}), bf16[14,32,256]{2,1,0:T(8,128)(2,1)S(1)}, s32[]{:S(2)}) async-start(bf16[32,32,256]{2,1,0:T(8,128)(2,1)} %own.3), calls=%async_computation | async-start | bytes 458752 | tf_op jit(solution)/shard_map/slice | solution.py:182
  0.0 11.9 %copy-start.4 = (s32[32,512]{1,0:T(8,128)S(1)}, s32[32,512]{1,0:T(8,128)}, u32[]{:S(2)}) copy-start(s32[32,512]{1,0:T(8,128)} %param.6) | copy-start | bytes 196612
  1.1 16.4 %copy-start = (bf16[32,32,256]{2,1,0:T(8,128)(2,1)S(1)}, bf16[32,32,256]{2,1,0:T(8,128)(2,1)}, u32[]{:S(2)}) copy-start(bf16[32,32,256]{2,1,0:T(8,128)(2,1)} %own.3) | copy-start | bytes 1572868
  1.1 16.4 %copy-start.2 = (bf16[3,256,1024]{2,1,0:T(8,128)(2,1)S(1)}, bf16[3,256,1024]{2,1,0:T(8,128)(2,1)}, u32[]{:S(2)}) copy-start(bf16[3,256,1024]{2,1,0:T(8,128)(2,1)} %up.3) | copy-start | bytes 4718596
  1.1 11.8 %collective-permute-start.1 = (bf16[32,16,256]{2,1,0:T(8,128)(2,1)S(1)}, bf16[32,16,256]{2,1,0:T(8,128)(2,1)S(1)}, u32[]{:S(2)}, u32[]{:S(2)}) collective-permute-start(bf16[32,16,256]{2,1,0:T(8,128)(2,1)S(1)} %get-tuple-element.15), channel_id=1, source_target_pairs={{0,15},{1,0},{2,1},{3,2},{4,3},{5,4},{6,5},{7,6},{8,7},{9,8},{10,9... | collective-permute-start | bytes 786440 | tf_op jit(solution)/shard_map/ppermute | solution.py:174
  6.6 9.9 %collective-permute-start = (bf16[32,16,256]{2,1,0:T(8,128)(2,1)S(1)}, bf16[32,16,256]{2,1,0:T(8,128)(2,1)S(1)}, u32[]{:S(2)}, u32[]{:S(2)}) collective-permute-start(bf16[32,16,256]{2,1,0:T(8,128)(2,1)S(1)} %get-tuple-element.16), channel_id=1, source_target_pairs={{0,1},{1,2},{2,3},{3,4},{4,5},{5,6},{6,7},{7,8},{8,9},{9,10},{10,1... | collective-permute-start | bytes 786440 | tf_op jit(solution)/shard_map/ppermute | solution.py:174
  7.4 23.3 %collective-permute-start.2 = (bf16[14,32,256]{2,1,0:T(8,128)(2,1)}, bf16[14,32,256]{2,1,0:T(8,128)(2,1)S(1)}, u32[]{:S(2)}, u32[]{:S(2)}) collective-permute-start(bf16[14,32,256]{2,1,0:T(8,128)(2,1)} %rev.4), channel_id=1, source_target_pairs={{0,15},{1,14},{2,13},{3,12},{4,11},{5,10},{6,9},{7,8},{8,7},{9,6},... | collective-permute-start | bytes 688136 | tf_op jit(solution)/shard_map/ppermute | solution.py:183
  17.5 2.0 %copy-start.1 = (bf16[3,9,256,256]{3,2,1,0:T(8,128)(2,1)S(1)}, bf16[3,9,256,256]{3,2,1,0:T(8,128)(2,1)}, u32[]{:S(2)}) copy-start(bf16[3,9,256,256]{3,2,1,0:T(8,128)(2,1)} %w.3) | copy-start | bytes 10616836
  19.5 1.4 %copy-start.3 = (bf16[3,1024,256]{2,1,0:T(8,128)(2,1)S(1)}, bf16[3,1024,256]{2,1,0:T(8,128)(2,1)}, u32[]{:S(2)}) copy-start(bf16[3,1024,256]{2,1,0:T(8,128)(2,1)} %down.3) | copy-start | bytes 4718596
  30.7 2.6 %collective-permute-start.4 = (bf16[14,16,256]{2,1,0:T(8,128)(2,1)S(1)}, bf16[14,16,256]{2,1,0:T(8,128)(2,1)S(1)}, u32[]{:S(2)}, u32[]{:S(2)}) collective-permute-start(bf16[14,16,256]{2,1,0:T(8,128)(2,1)S(1)} %get-tuple-element.17), channel_id=1, source_target_pairs={{0,15},{1,0},{2,1},{3,2},{4,3},{5,4},{6,5},{7,6},{8,7},{9,8},{10,9... | collective-permute-start | bytes 344072 | tf_op jit(solution)/shard_map/ppermute | solution.py:174
  31.0 6.9 %collective-permute-start.3 = (bf16[14,16,256]{2,1,0:T(8,128)(2,1)S(1)}, bf16[14,16,256]{2,1,0:T(8,128)(2,1)S(1)}, u32[]{:S(2)}, u32[]{:S(2)}) collective-permute-start(bf16[14,16,256]{2,1,0:T(8,128)(2,1)S(1)} %get-tuple-element.18), channel_id=1, source_target_pairs={{0,1},{1,2},{2,3},{3,4},{4,5},{5,6},{6,7},{7,8},{8,9},{9,10},{10,1... | collective-permute-start | bytes 344072 | tf_op jit(solution)/shard_map/ppermute | solution.py:174
where the time goes:
time: 46.2 us; the launch traced here: 46 us
  Pallas kernels  17.8 us (39%)
  starting transfers between devices  10.5 us (23%)
  waiting for transfers between devices  10.3 us (22%)
  local copies, waits for them, and re-layouts  7.09 us (15%)
    pallas_call x2, Pallas kernels, call(): pl.pallas_call(kernel, name=name, out_shape=tuple((jax.ShapeDtypeStruct(s...  17.8 us
    ppermute x4, waiting for transfers between devices, around(): lax.ppermute(value, 'lon', [(i, (i + step) % count) for i in range(count)])  10.3 us
    ppermute x4, starting transfers between devices, around(): lax.ppermute(value, 'lon', [(i, (i + step) % count) for i in range(count)])  6.06 us
    ppermute x1, starting transfers between devices, per_device(): lax.ppermute(strip, 'lon', [(i, count - 1 - i) for i in range(count)])  4.44 us
    unnamed x10, local copies, waits for them, and re-layouts  3.42 us
    broadcast_in_dim x6, local copies, waits for them, and re-layouts, cells_mask(): return jnp.broadcast_to(part, (part.shape[0], 128))  1.18 us
    slice x1, local copies, waits for them, and re-layouts, per_device(): right = around(own[:, :HALO], -1)  1.11 us
  transfers between devices with their start and end apart: 5, of which 3 were waited for; matrix products, arithmetic and copies ran while one was open for 6% of the time, Pallas kernels for 21%

commit v1 on v0

v1 whole, which is shorter than its diff:
```python
import functools

import jax
import jax.numpy as jnp
import numpy as np
from jax import lax
from jax.experimental import pallas as pl
from jax.experimental.pallas import tpu as pltpu
from jax.sharding import PartitionSpec as P

BF = jnp.bfloat16
F32 = jnp.float32
HALO = 16
DEEP = 14
LIMIT = 24
RSQRT2 = np.float32(0.7071067811865476)


def conv_norm(layer, shifted, width, base, chunks, w_ref, nrm):
    dil = 2 ** (layer + 1)
    weight = w_ref[layer].reshape(-1, w_ref.shape[-1])
    at = 0
    for first, count, turned in chunks:
        taps = [(a, b) for a in range(3) for b in range(3)]
        if turned:
            taps = taps[::-1]
        size = count * width
        lhs = jnp.concatenate(
            [
                shifted[b, (first - base + (a - 1) * dil) * width : (first - base + (a - 1) * dil) * width + size]
                for a, b in taps
            ],
            axis=1,
        )
        conv = jnp.dot(lhs, weight, preferred_element_type=F32)
        mean = jnp.mean(conv, axis=-1, keepdims=True)
        centred = conv - mean
        var = jnp.mean(centred * centred, axis=-1, keepdims=True)
        nrm[at : at + size] = (centred * lax.rsqrt(var + 1e-05)).astype(BF)
        at += size


def mlp(layer, shifted, width, base, first, counts, up_ref, down_ref, mask_ref, nrm, store, mask_base=0):
    at = 0
    row = first
    for count in counts:
        size = count * width
        pre = jnp.dot(nrm[at : at + size], up_ref[layer], preferred_element_type=F32)
        hidden = (0.5 * pre * (1.0 + lax.erf(pre * RSQRT2))).astype(BF)
        branch = jnp.dot(hidden, down_ref[layer], preferred_element_type=F32)
        centre = shifted[1, (row - base) * width : (row - base) * width + size].astype(F32)
        mask = mask_ref[(row - mask_base) * width : (row - mask_base) * width + size].astype(F32)
        mask = jnp.concatenate([mask, mask], axis=1)
        store(row, count, (mask * (centre + branch)).astype(BF))
        at += size
        row += count


def spread(shifted, at, values, starts, size, dil):
    for b in range(3):
        for k, start in enumerate(starts):
            lo = start + (b - 1) * dil
            shifted[b, at + k * size : at + (k + 1) * size] = values[lo : lo + size]


def clear(shifted, size):
    for b in range(3):
        shifted[b, :size] = jnp.zeros((size, shifted.shape[-1]), BF)


def keep(ref, width, base):
    def store(row, count, value):
        ref[(row - base) * width : (row - base + count) * width] = value

    return store


def wide(row, left, own, right):
    return jnp.concatenate([left[row], own[row], right[row]], axis=0)


def inner_kernel(own, mask, w, up, down, x1, x2, sh1, sh2, nrm):
    clear(sh1, 2 * 32)
    clear(sh2, 4 * 32)
    edge = jnp.zeros((HALO, own.shape[-1]), BF)
    for row in range(32):
        spread(sh1, (row + 2) * 32, jnp.concatenate([edge, own[row], edge], axis=0), [16], 32, 2)
    conv_norm(0, sh1, 32, -2, [(0, 15, False), (15, 15, False)], w, nrm)
    mlp(0, sh1, 32, -2, 0, [15, 15], up, down, mask, nrm, keep(x1, 32, 0))
    for row in range(30):
        values = jnp.concatenate([edge, x1[row * 32 : (row + 1) * 32], edge], axis=0)
        spread(sh2, (row + 4) * 32, values, [16], 32, 4)
    conv_norm(1, sh2, 32, -4, [(0, 13, False), (13, 13, False)], w, nrm)
    mlp(1, sh2, 32, -4, 0, [13, 13], up, down, mask, nrm, keep(x2, 32, 0))


def south_kernel(
    left, own, right, x1_mid, x2_mid, e1, e2, mask, w, up, down,
    x1_tail, x2_tail, out, sh1, sh2, sh3, x1, x2, nrm,
):
    clear(sh1, 2 * 32)
    clear(sh2, 4 * 32)
    clear(sh3, 8 * 32)
    for row in range(32):
        spread(sh1, (row + 2) * 32, wide(row, left, own, right), [4, 44], 16, 2)
    conv_norm(0, sh1, 32, -2, [(0, 15, False), (15, 15, False)], w, nrm)
    mlp(0, sh1, 32, -2, 0, [15, 15], up, down, e1, nrm, keep(x1, 32, 0))

    def row1(row):
        at = row * 32
        return jnp.concatenate([x1[at : at + 16], x1_mid[at + 4 : at + 28], x1[at + 16 : at + 32]], axis=0)

    for row in range(30):
        values = row1(row)
        if row >= 22:
            x1_tail[(row - 22) * 56 : (row - 21) * 56] = values
        spread(sh2, (row + 4) * 32, values, [4, 36], 16, 4)
    conv_norm(1, sh2, 32, -4, [(0, 13, False), (13, 13, False)], w, nrm)
    mlp(1, sh2, 32, -4, 0, [13, 13], up, down, e2, nrm, keep(x2, 32, 0))
    for row in range(26):
        at = row * 32
        values = jnp.concatenate([x2[at : at + 16], x2_mid[at + 8 : at + 24], x2[at + 16 : at + 32]], axis=0)
        if row >= 10:
            x2_tail[(row - 10) * 48 : (row - 9) * 48] = values
        spread(sh3, (row + 8) * 32, values, [8], 32, 8)
    conv_norm(2, sh3, 32, -8, [(0, 9, False), (9, 9, False)], w, nrm)

    def store3(row, count, value):
        out[row : row + count] = value.reshape(count, 32, 256)

    mlp(2, sh3, 32, -8, 0, [9, 9], up, down, mask, nrm, store3)


def north_kernel(
    left, own, right, north, north_left, north_right, x1_tail, x2_tail, out_south,
    m1, m2, mask, w, up, down, out, sh1, sh2, sh3, x1, x2, nrm, last, sems,
):
    first = pltpu.make_async_copy(out_south, out.at[0:18], sems.at[0])
    first.start()
    for row in range(4):
        spread(sh1, row * 56, wide(28 + row, left, own, right), [4], 56, 2)
    for row in range(14):
        spread(sh1, (row + 4) * 56, wide(row, north_left, north, north_right), [4], 56, 2)
    conv_norm(0, sh1, 56, 28, [(30, 2, False), (32, 6, True), (38, 6, True)], w, nrm)
    mlp(0, sh1, 56, 28, 30, [8, 6], up, down, m1, nrm, keep(x1, 56, 30), 30)
    for row in range(8):
        spread(sh2, row * 48, x1_tail[row * 56 : (row + 1) * 56], [4], 48, 4)
    for row in range(14):
        spread(sh2, (row + 8) * 48, x1[row * 56 : (row + 1) * 56], [4], 48, 4)
    conv_norm(1, sh2, 48, 22, [(26, 6, False), (32, 8, True)], w, nrm)
    mlp(1, sh2, 48, 22, 26, [7, 7], up, down, m2, nrm, keep(x2, 48, 26), 26)
    for row in range(16):
        spread(sh3, row * 32, x2_tail[row * 48 : (row + 1) * 48], [8], 32, 8)
    for row in range(14):
        spread(sh3, (row + 16) * 32, x2[row * 48 : (row + 1) * 48], [8], 32, 8)
    conv_norm(2, sh3, 32, 10, [(18, 7, False), (25, 7, False)], w, nrm)

    def store3(row, count, value):
        last[row - 18 : row - 18 + count] = value.reshape(count, 32, 256)

    mlp(2, sh3, 32, 10, 18, [7, 7], up, down, mask, nrm, store3)
    second = pltpu.make_async_copy(last, out.at[18:32], sems.at[1])
    second.start()
    first.wait()
    second.wait()


def cost(cells):
    return pl.CostEstimate(
        flops=2 * cells * (9 * 256 * 256 + 2 * 256 * 1024), bytes_accessed=2**20, transcendentals=cells * 1024
    )


VMEM = pl.BlockSpec(memory_space=pltpu.VMEM)
HBM = pl.BlockSpec(memory_space=pltpu.HBM)


def call(kernel, name, outs, in_specs, out_specs, scratch, cells, args):
    return pl.pallas_call(
        kernel,
        name=name,
        out_shape=tuple(jax.ShapeDtypeStruct(shape, BF) for shape in outs),
        in_specs=in_specs,
        out_specs=tuple(out_specs),
        scratch_shapes=scratch,
        compiler_params=pltpu.CompilerParams(vmem_limit_bytes=LIMIT * 2**20),
        cost_estimate=cost(cells),
    )(*args)


def taps(rows, width):
    return pltpu.VMEM((3, rows * width, 256), BF)


def flat(rows, width):
    return pltpu.VMEM((rows * width, 256), BF)


def inner_call(own, mask, w, up, down):
    return call(
        inner_kernel, "inner", [(30 * 32, 256), (26 * 32, 256)],
        [VMEM] * 5, [VMEM] * 2,
        [taps(34, 32), taps(34, 32), flat(30, 32)],
        1792, (own, mask, w, up, down),
    )


def south_call(*args):
    return call(
        south_kernel, "south", [(8 * 56, 256), (16 * 48, 256), (18, 32, 256)], [VMEM] * len(args), [VMEM] * 3,
        [taps(34, 32), taps(34, 32), taps(34, 32), flat(30, 32), flat(26, 32), flat(30, 32)],
        2368, args,
    )


def north_call(*args):
    (out,) = call(
        north_kernel, "north", [(32, 32, 256)], [VMEM] * len(args), [HBM],
        [
            taps(18, 56), taps(22, 48), taps(30, 32), flat(14, 56), flat(14, 48), flat(14, 56),
            pltpu.VMEM((14, 32, 256), BF), pltpu.SemaphoreType.DMA((2,)),
        ],
        1904, args,
    )
    return out


def around(value, step):
    count = lax.axis_size("lon")
    return lax.ppermute(value, "lon", [(i, (i + step) % count) for i in range(count)])


def per_device(own, land_sea, w, up, down):
    count = lax.axis_size("lon")
    cols = own.shape[1]
    left = around(own[:, cols - HALO :], 1)
    right = around(own[:, :HALO], -1)
    strip = own[own.shape[0] - DEEP :][::-1, ::-1]
    north = lax.ppermute(strip, "lon", [(i, count - 1 - i) for i in range(count)])

    def cells_mask(parts):
        part = jnp.concatenate(parts, axis=1) if len(parts) > 1 else parts[0]
        part = part.reshape(-1, 1)
        return jnp.broadcast_to(part, (part.shape[0], 128))

    land_sea = land_sea.astype(BF)
    at = lax.axis_index("lon") * cols
    mask = cells_mask([lax.dynamic_slice_in_dim(land_sea, at, cols, 1)])
    weights = (w, up, down)
    x1_mid, x2_mid = inner_call(own, mask, w, up, down)

    land = jnp.concatenate([land_sea, land_sea[::-1, ::-1][:DEEP]], axis=0)
    land = jnp.concatenate([land[:, -HALO:], land, land[:, :HALO]], axis=1)
    land = lax.dynamic_slice_in_dim(land, at, cols + 2 * HALO, 1)
    e1 = cells_mask([land[:30, 4:20], land[:30, 44:60]])
    e2 = cells_mask([land[:26, 8:24], land[:26, 40:56]])
    m1 = cells_mask([land[30:44, 4:60]])
    m2 = cells_mask([land[26:40, 8:56]])
    left, right, m1, m2 = lax.optimization_barrier((left, right, m1, m2))
    x1_tail, x2_tail, out_south = south_call(left, own, right, x1_mid, x2_mid, e1, e2, mask, *weights)
    north, x1_tail = lax.optimization_barrier((north, x1_tail))
    north_left = around(north[:, cols - HALO :], 1)
    north_right = around(north[:, :HALO], -1)
    return north_call(
        left, own, right, north, north_left, north_right, x1_tail, x2_tail, out_south, m1, m2, mask, *weights
    )


def solution(mesh):
    in_specs = (P("parts", "lon", None), P(), P(), P(), P())
    out_specs = P("parts", "lon", None)
    return jax.shard_map(
        per_device, mesh=mesh, in_specs=in_specs, out_specs=out_specs, check_vma=False
    )
```

time: 46.2 us -> 39.7 us (0.86)
  waiting for transfers between devices: 10.3 us -> 2.59 us
  local copies, waits for them, and re-layouts: 7.09 us -> 7.57 us
    ppermute x4, waiting for transfers between devices: 10.3 us -> 2.58 us  [around(): lax.ppermute(value, 'lon', [(i, (i + step) % count) for i in range(count)])]
    ppermute x4, starting transfers between devices: 6.06 us -> 10.1 us  [around(): lax.ppermute(value, 'lon', [(i, (i + step) % count) for i in range(count)])]
    ppermute x1, starting transfers between devices: 4.44 us -> 0.68 us  [per_device(): lax.ppermute(strip, 'lon', [(i, count - 1 - i) for i in range(count)])]
    pallas_call x2 -> x3, Pallas kernels: 17.8 us -> 18 us  [call(): pl.pallas_call(kernel, name=name, out_shape=tuple((jax.ShapeDtypeStruct(s...]
    broadcast_in_dim x6 -> x10, local copies, waits for them, and re-layouts: 1.18 us -> 1.33 us  [cells_mask(): return jnp.broadcast_to(part, (part.shape[0], 128))]
    unnamed x10 -> x14, local copies, waits for them, and re-layouts: 3.42 us -> 3.42 us
  transfers between devices with their start and end apart: 5 -> 5, of which waited for: 3 -> 1; matrix products, arithmetic and copies ran while one was open for 6% -> 8% of each run, Pallas kernels for 21% -> 29%
where the time goes in v1:
time: 39.7 us; the launch traced here: 39.5 us
  Pallas kernels  18 us (45%)
  starting transfers between devices  10.7 us (27%)
  local copies, waits for them, and re-layouts  7.57 us (19%)
  waiting for transfers between devices  2.59 us (7%)
    pallas_call x3, Pallas kernels, call(): pl.pallas_call(kernel, name=name, out_shape=tuple((jax.ShapeDtypeStruct(s...  18 us
    ppermute x4, starting transfers between devices, around(): lax.ppermute(value, 'lon', [(i, (i + step) % count) for i in range(count)])  10.1 us
    unnamed x14, local copies, waits for them, and re-layouts  3.42 us
    ppermute x4, waiting for transfers between devices, around(): lax.ppermute(value, 'lon', [(i, (i + step) % count) for i in range(count)])  2.58 us
    broadcast_in_dim x10, local copies, waits for them, and re-layouts, cells_mask(): return jnp.broadcast_to(part, (part.shape[0], 128))  1.33 us
    slice x1, local copies, waits for them, and re-layouts, per_device(): right = around(own[:, :HALO], -1)  1.22 us
  transfers between devices with their start and end apart: 5, of which 1 were waited for; matrix products, arithmetic and copies ran while one was open for 8% of the time, Pallas kernels for 29%

profile of v1, /device:TPU:0, one launch (start us, length us, event | category | flops | bytes accessed | tf_op | source)
XLA Modules:
  0.0 39.5 jit_solution(3619037968126111344)
XLA Ops:
  0.0 1.2 %fusion.5 = (bf16[32,16,256]{2,1,0:T(8,128)(2,1)S(1)}, bf16[32,16,256]{2,1,0:T(8,128)(2,1)S(1)}) fusion(bf16[32,32,256]{2,1,0:T(8,128)(2,1)} %own.5), kind=kLoop, calls=%fused_computation.14 | loop fusion | bytes 1048576 | tf_op jit(solution)/shard_map/slice | solution.py:237
  1.2 0.5 %collective-permute-start = (bf16[32,16,256]{2,1,0:T(8,128)(2,1)S(1)}, bf16[32,16,256]{2,1,0:T(8,128)(2,1)S(1)}, u32[]{:S(2)}, u32[]{:S(2)}) collective-permute-start(bf16[32,16,256]{2,1,0:T(8,128)(2,1)S(1)} %get-tuple-element.28), channel_id=1, source_target_pairs={{0,1},{1,2},{2,3},{3,4},{4,5},{5,6},{6,7},{7,8},{8,9},{9,10},{10,1... | collective-permute-start | bytes 786440 | tf_op jit(solution)/shard_map/ppermute | solution.py:230
  1.8 5.1 %collective-permute-start.1 = (bf16[32,16,256]{2,1,0:T(8,128)(2,1)S(1)}, bf16[32,16,256]{2,1,0:T(8,128)(2,1)S(1)}, u32[]{:S(2)}, u32[]{:S(2)}) collective-permute-start(bf16[32,16,256]{2,1,0:T(8,128)(2,1)S(1)} %get-tuple-element.27), channel_id=1, source_target_pairs={{0,15},{1,0},{2,1},{3,2},{4,3},{5,4},{6,5},{7,6},{8,7},{9,8},{10,9... | collective-permute-start | bytes 786440 | tf_op jit(solution)/shard_map/ppermute | solution.py:230
  6.8 0.8 %rev.4 = bf16[14,32,256]{2,1,0:T(8,128)(2,1)} reverse(bf16[14,32,256]{2,1,0:T(8,128)(2,1)S(1)} %slice-done), dimensions={0,1} | reverse | bytes 458752 | tf_op jit(solution)/shard_map/rev | solution.py:238
  7.6 0.7 %collective-permute-start.2 = (bf16[14,32,256]{2,1,0:T(8,128)(2,1)}, bf16[14,32,256]{2,1,0:T(8,128)(2,1)S(1)}, u32[]{:S(2)}, u32[]{:S(2)}) collective-permute-start(bf16[14,32,256]{2,1,0:T(8,128)(2,1)} %rev.4), channel_id=1, source_target_pairs={{0,15},{1,14},{2,13},{3,12},{4,11},{5,10},{6,9},{7,8},{8,7},{9,6},... | collective-permute-start | bytes 688136 | tf_op jit(solution)/shard_map/ppermute | solution.py:239
  8.3 0.4 %slice.48 = bf16[14,512]{1,0:T(8,128)(2,1)S(1)} reverse(bf16[14,512]{1,0:T(8,128)(2,1)S(1)} %slice.60), dimensions={0,1} | reverse | bytes 28672 | tf_op jit(solution)/shard_map/slice | solution.py:252
  8.7 0.2 fusion.2
  8.9 0.1 slice.61
  9.0 0.1 slice.62
  9.0 0.1 fusion.8
  9.1 0.1 fusion.7
  9.2 0.1 broadcast_in_dim.35
  9.3 0.1 broadcast_in_dim.37
  9.4 0.1 pad_maximum_fusion
  9.4 0.1 broadcast_in_dim.41
  9.5 0.1 pad_maximum_fusion.1
  9.6 0.1 broadcast_in_dim.43
  9.7 0.1 constant_dynamic-slice_fusion
  9.8 0.1 broadcast_in_dim.39
  9.9 0.2 broadcast_in_dim.40.mask
  10.1 2.0 %copy-done.1 = bf16[3,9,256,256]{3,2,1,0:T(8,128)(2,1)S(1)} copy-done((bf16[3,9,256,256]{3,2,1,0:T(8,128)(2,1)S(1)}, bf16[3,9,256,256]{3,2,1,0:T(8,128)(2,1)}, u32[]{:S(2)}) %copy-start.1) | copy-done | bytes 3538968
  12.1 1.4 %copy-done.4 = bf16[3,1024,256]{2,1,0:T(8,128)(2,1)S(1)} copy-done((bf16[3,1024,256]{2,1,0:T(8,128)(2,1)S(1)}, bf16[3,1024,256]{2,1,0:T(8,128)(2,1)}, u32[]{:S(2)}) %copy-start.4) | copy-done | bytes 1572888
  13.5 5.1 %inner.1 = (bf16[960,256]{1,0:T(8,128)(2,1)S(1)}, bf16[832,256]{1,0:T(8,128)(2,1)S(1)}) custom-call(bf16[32,32,256]{2,1,0:T(8,128)(2,1)S(1)} %copy-done, bf16[1024,128]{1,0:T(8,128)(2,1)S(1)} %broadcast_in_dim.40.mask, bf16[3,9,256,256]{3,2,1,0:T(8,128)(2,1)S(1)} %copy-done.1, bf16[3,256,1024]{2,1,0:T(8,128)(2,1)S(1)} %copy-done.3, ...), custom_call_target="tpu_custom_call" | custom-call | flops 3992977408 | bytes 1048576 | tf_op jit(solution)/shard_map/inner/pallas_call | solution.py:179
  18.7 0.2 broadcast_in_dim.36.m1
  18.8 0.2 broadcast_in_dim.38.m2
  19.0 0.2 broadcast_in_dim.42.e1
  19.2 0.2 broadcast_in_dim.44.e2
  19.4 6.4 %south.1 = (bf16[448,256]{1,0:T(8,128)(2,1)S(1)}, bf16[768,256]{1,0:T(8,128)(2,1)S(1)}, bf16[18,32,256]{2,1,0:T(8,128)(2,1)S(1)}) custom-call(bf16[32,16,256]{2,1,0:T(8,128)(2,1)S(1)} %collective-permute-done.left, bf16[32,32,256]{2,1,0:T(8,128)(2,1)S(1)} %copy-done, bf16[32,16,256]{2,1,0:T(8,128)(2,1)S(1)} %collective-permute-done.1.right, ...), custom_call_target="tpu_custom_call" | custom-call | flops 5276434432 | bytes 1048576 | tf_op jit(solution)/shard_map/south/pallas_call | solution.py:179
  25.9 1.7 %collective-permute-start.3 = (bf16[14,16,256]{2,1,0:T(8,128)(2,1)S(1)}, bf16[14,16,256]{2,1,0:T(8,128)(2,1)S(1)}, u32[]{:S(2)}, u32[]{:S(2)}) collective-permute-start(bf16[14,16,256]{2,1,0:T(8,128)(2,1)S(1)} %get-tuple-element.30), channel_id=1, source_target_pairs={{0,1},{1,2},{2,3},{3,4},{4,5},{5,6},{6,7},{7,8},{8,9},{9,10},{10,1... | collective-permute-start | bytes 344072 | tf_op jit(solution)/shard_map/ppermute | solution.py:230
  27.6 2.8 %collective-permute-start.4 = (bf16[14,16,256]{2,1,0:T(8,128)(2,1)S(1)}, bf16[14,16,256]{2,1,0:T(8,128)(2,1)S(1)}, u32[]{:S(2)}, u32[]{:S(2)}) collective-permute-start(bf16[14,16,256]{2,1,0:T(8,128)(2,1)S(1)} %get-tuple-element.29), channel_id=1, source_target_pairs={{0,15},{1,0},{2,1},{3,2},{4,3},{5,4},{6,5},{7,6},{8,7},{9,8},{10,9... | collective-permute-start | bytes 344072 | tf_op jit(solution)/shard_map/ppermute | solution.py:230
  30.4 2.6 %collective-permute-done.3.north_left = bf16[14,16,256]{2,1,0:T(8,128)(2,1)S(1)} collective-permute-done((bf16[14,16,256]{2,1,0:T(8,128)(2,1)S(1)}, bf16[14,16,256]{2,1,0:T(8,128)(2,1)S(1)}, u32[]{:S(2)}, u32[]{:S(2)}) %collective-permute-start.3) | collective-permute-done | bytes 114720 | tf_op jit(solution)/shard_map/ppermute | solution.py:230
  33.0 6.4 %north.1 = bf16[32,32,256]{2,1,0:T(8,128)(2,1)} custom-call(bf16[32,16,256]{2,1,0:T(8,128)(2,1)S(1)} %collective-permute-done.left, bf16[32,32,256]{2,1,0:T(8,128)(2,1)S(1)} %copy-done, bf16[32,16,256]{2,1,0:T(8,128)(2,1)S(1)} %collective-permute-done.1.right, bf16[14,32,256]{2,1,0:T(8,128)(2,1)S(1)} %collective-permute-done.2.north, ...), custom_call_target="tpu_custom_call" | custom-call | flops 4242538496 | bytes 1048576 | tf_op jit(solution)/shard_map/north/pallas_call | solution.py:179
  (21 shorter events, 0.1 us)
Async XLA Ops:
  0.0 6.8 %slice-start = ((bf16[32,32,256]{2,1,0:T(8,128)(2,1)}), bf16[14,32,256]{2,1,0:T(8,128)(2,1)S(1)}, s32[]{:S(2)}) async-start(bf16[32,32,256]{2,1,0:T(8,128)(2,1)} %own.5), calls=%async_computation | async-start | bytes 458752 | tf_op jit(solution)/shard_map/slice | solution.py:238
  0.0 10.1 %copy-start = (bf16[32,32,256]{2,1,0:T(8,128)(2,1)S(1)}, bf16[32,32,256]{2,1,0:T(8,128)(2,1)}, u32[]{:S(2)}) copy-start(bf16[32,32,256]{2,1,0:T(8,128)(2,1)} %own.5) | copy-start | bytes 1572868
  0.0 8.3 %copy-start.6 = (s32[32,512]{1,0:T(8,128)S(1)}, s32[32,512]{1,0:T(8,128)}, u32[]{:S(2)}) copy-start(s32[32,512]{1,0:T(8,128)} %param.6) | copy-start | bytes 196612
  0.0 10.1 %copy-start.3 = (bf16[3,256,1024]{2,1,0:T(8,128)(2,1)S(1)}, bf16[3,256,1024]{2,1,0:T(8,128)(2,1)}, u32[]{:S(2)}) copy-start(bf16[3,256,1024]{2,1,0:T(8,128)(2,1)} %up.5) | copy-start | bytes 4718596
  1.2 17.4 %collective-permute-start = (bf16[32,16,256]{2,1,0:T(8,128)(2,1)S(1)}, bf16[32,16,256]{2,1,0:T(8,128)(2,1)S(1)}, u32[]{:S(2)}, u32[]{:S(2)}) collective-permute-start(bf16[32,16,256]{2,1,0:T(8,128)(2,1)S(1)} %get-tuple-element.28), channel_id=1, source_target_pairs={{0,1},{1,2},{2,3},{3,4},{4,5},{5,6},{6,7},{7,8},{8,9},{9,10},{10,1... | collective-permute-start | bytes 786440 | tf_op jit(solution)/shard_map/ppermute | solution.py:230
  1.8 16.9 %collective-permute-start.1 = (bf16[32,16,256]{2,1,0:T(8,128)(2,1)S(1)}, bf16[32,16,256]{2,1,0:T(8,128)(2,1)S(1)}, u32[]{:S(2)}, u32[]{:S(2)}) collective-permute-start(bf16[32,16,256]{2,1,0:T(8,128)(2,1)S(1)} %get-tuple-element.27), channel_id=1, source_target_pairs={{0,15},{1,0},{2,1},{3,2},{4,3},{5,4},{6,5},{7,6},{8,7},{9,8},{10,9... | collective-permute-start | bytes 786440 | tf_op jit(solution)/shard_map/ppermute | solution.py:230
  7.6 18.3 %collective-permute-start.2 = (bf16[14,32,256]{2,1,0:T(8,128)(2,1)}, bf16[14,32,256]{2,1,0:T(8,128)(2,1)S(1)}, u32[]{:S(2)}, u32[]{:S(2)}) collective-permute-start(bf16[14,32,256]{2,1,0:T(8,128)(2,1)} %rev.4), channel_id=1, source_target_pairs={{0,15},{1,14},{2,13},{3,12},{4,11},{5,10},{6,9},{7,8},{8,7},{9,6},... | collective-permute-start | bytes 688136 | tf_op jit(solution)/shard_map/ppermute | solution.py:239
  10.1 2.0 %copy-start.1 = (bf16[3,9,256,256]{3,2,1,0:T(8,128)(2,1)S(1)}, bf16[3,9,256,256]{3,2,1,0:T(8,128)(2,1)}, u32[]{:S(2)}) copy-start(bf16[3,9,256,256]{3,2,1,0:T(8,128)(2,1)} %w.5) | copy-start | bytes 10616836
  12.1 1.4 %copy-start.4 = (bf16[3,1024,256]{2,1,0:T(8,128)(2,1)S(1)}, bf16[3,1024,256]{2,1,0:T(8,128)(2,1)}, u32[]{:S(2)}) copy-start(bf16[3,1024,256]{2,1,0:T(8,128)(2,1)} %down.5) | copy-start | bytes 4718596
  13.5 5.8 %copy-start.2 = (bf16[3,9,256,256]{3,2,1,0:T(8,128)(2,1)S(1)}, bf16[3,9,256,256]{3,2,1,0:T(8,128)(2,1)}, u32[]{:S(2)}) copy-start(bf16[3,9,256,256]{3,2,1,0:T(8,128)(2,1)} %w.5) | copy-start | bytes 10616836
  13.5 5.8 %copy-start.5 = (bf16[3,1024,256]{2,1,0:T(8,128)(2,1)S(1)}, bf16[3,1024,256]{2,1,0:T(8,128)(2,1)}, u32[]{:S(2)}) copy-start(bf16[3,1024,256]{2,1,0:T(8,128)(2,1)} %down.5) | copy-start | bytes 4718596
  25.9 7.1 %collective-permute-start.3 = (bf16[14,16,256]{2,1,0:T(8,128)(2,1)S(1)}, bf16[14,16,256]{2,1,0:T(8,128)(2,1)S(1)}, u32[]{:S(2)}, u32[]{:S(2)}) collective-permute-start(bf16[14,16,256]{2,1,0:T(8,128)(2,1)S(1)} %get-tuple-element.30), channel_id=1, source_target_pairs={{0,1},{1,2},{2,3},{3,4},{4,5},{5,6},{6,7},{7,8},{8,9},{9,10},{10,1... | collective-permute-start | bytes 344072 | tf_op jit(solution)/shard_map/ppermute | solution.py:230
  27.6 5.3 %collective-permute-start.4 = (bf16[14,16,256]{2,1,0:T(8,128)(2,1)S(1)}, bf16[14,16,256]{2,1,0:T(8,128)(2,1)S(1)}, u32[]{:S(2)}, u32[]{:S(2)}) collective-permute-start(bf16[14,16,256]{2,1,0:T(8,128)(2,1)S(1)} %get-tuple-element.29), channel_id=1, source_target_pairs={{0,15},{1,0},{2,1},{3,2},{4,3},{5,4},{6,5},{7,6},{8,7},{9,8},{10,9... | collective-permute-start | bytes 344072 | tf_op jit(solution)/shard_map/ppermute | solution.py:230

commit v2 on v1

--- a/solution.py
+++ b/solution.py
@@ -12,7 +12,7 @@
 F32 = jnp.float32
 HALO = 16
 DEEP = 14
-LIMIT = 24
+LIMIT = 51
 RSQRT2 = np.float32(0.7071067811865476)
 
 
@@ -75,35 +75,75 @@
     return store
 
 
+def fetch(layers, sources, targets, sems):
+    copies = [
+        [pltpu.make_async_copy(src.at[layer], dst.at[layer], sems.at[k, layer]) for k, (src, dst) in enumerate(zip(sources, targets))]
+        for layer in range(layers)
+    ]
+    for group in copies:
+        for copy in group:
+            copy.start()
+
+    def arrived(layer, *which):
+        for k in which:
+            copies[layer][k].wait()
+
+    return arrived
+
+
+def diagonal(turned):
+    rows = lax.broadcasted_iota(jnp.int32, (64, 64), 0)
+    cols = lax.broadcasted_iota(jnp.int32, (64, 64), 1)
+    return rows + cols == 63 if turned else rows == cols
+
+
+def spread_mask(land, row, turned):
+    line = jnp.where(diagonal(turned), land[row : row + 1], 0.0).astype(BF)
+    return jnp.dot(line, jnp.ones((64, 128), BF), preferred_element_type=F32).astype(BF)
+
+
 def wide(row, left, own, right):
     return jnp.concatenate([left[row], own[row], right[row]], axis=0)
 
 
-def inner_kernel(own, mask, w, up, down, x1, x2, sh1, sh2, nrm):
+def inner_kernel(own, land, w_hbm, up_hbm, down_hbm, x1, x2, mask, w, up, down, sems, sh1, sh2, nrm):
+    arrived = fetch(2, (w_hbm, up_hbm, down_hbm), (w, up, down), sems)
     clear(sh1, 2 * 32)
     clear(sh2, 4 * 32)
     edge = jnp.zeros((HALO, own.shape[-1]), BF)
     for row in range(32):
         spread(sh1, (row + 2) * 32, jnp.concatenate([edge, own[row], edge], axis=0), [16], 32, 2)
+        mask[row * 32 : (row + 1) * 32] = spread_mask(land, row, False)[16:48]
+    arrived(0, 0)
     conv_norm(0, sh1, 32, -2, [(0, 15, False), (15, 15, False)], w, nrm)
+    arrived(0, 1, 2)
     mlp(0, sh1, 32, -2, 0, [15, 15], up, down, mask, nrm, keep(x1, 32, 0))
     for row in range(30):
         values = jnp.concatenate([edge, x1[row * 32 : (row + 1) * 32], edge], axis=0)
         spread(sh2, (row + 4) * 32, values, [16], 32, 4)
+    arrived(1, 0, 1, 2)
     conv_norm(1, sh2, 32, -4, [(0, 13, False), (13, 13, False)], w, nrm)
     mlp(1, sh2, 32, -4, 0, [13, 13], up, down, mask, nrm, keep(x2, 32, 0))
 
 
 def south_kernel(
-    left, own, right, x1_mid, x2_mid, e1, e2, mask, w, up, down,
-    x1_tail, x2_tail, out, sh1, sh2, sh3, x1, x2, nrm,
+    left, own, right, x1_mid, x2_mid, land, mask, w_hbm, up_hbm, down_hbm,
+    x1_tail, x2_tail, out, w, up, down, sems, sh1, sh2, sh3, x1, x2, nrm, e1, e2,
 ):
+    arrived = fetch(3, (w_hbm, up_hbm, down_hbm), (w, up, down), sems)
     clear(sh1, 2 * 32)
     clear(sh2, 4 * 32)
     clear(sh3, 8 * 32)
     for row in range(32):
         spread(sh1, (row + 2) * 32, wide(row, left, own, right), [4, 44], 16, 2)
+    for row in range(30):
+        cells = spread_mask(land, row, False)
+        e1[row * 32 : (row + 1) * 32] = jnp.concatenate([cells[4:20], cells[44:60]], axis=0)
+        if row < 26:
+            e2[row * 32 : (row + 1) * 32] = jnp.concatenate([cells[8:24], cells[40:56]], axis=0)
+    arrived(0, 0)
     conv_norm(0, sh1, 32, -2, [(0, 15, False), (15, 15, False)], w, nrm)
+    arrived(0, 1, 2)
     mlp(0, sh1, 32, -2, 0, [15, 15], up, down, e1, nrm, keep(x1, 32, 0))
 
     def row1(row):
@@ -115,7 +155,9 @@
         if row >= 22:
             x1_tail[(row - 22) * 56 : (row - 21) * 56] = values
         spread(sh2, (row + 4) * 32, values, [4, 36], 16, 4)
+    arrived(1, 0)
     conv_norm(1, sh2, 32, -4, [(0, 13, False), (13, 13, False)], w, nrm)
+    arrived(1, 1, 2)
     mlp(1, sh2, 32, -4, 0, [13, 13], up, down, e2, nrm, keep(x2, 32, 0))
     for row in range(26):
         at = row * 32
@@ -123,41 +165,59 @@
         if row >= 10:
             x2_tail[(row - 10) * 48 : (row - 9) * 48] = values
         spread(sh3, (row + 8) * 32, values, [8], 32, 8)
+    arrived(2, 0)
     conv_norm(2, sh3, 32, -8, [(0, 9, False), (9, 9, False)], w, nrm)
 
     def store3(row, count, value):
         out[row : row + count] = value.reshape(count, 32, 256)
 
+    arrived(2, 1, 2)
     mlp(2, sh3, 32, -8, 0, [9, 9], up, down, mask, nrm, store3)
 
 
 def north_kernel(
     left, own, right, north, north_left, north_right, x1_tail, x2_tail, out_south,
-    m1, m2, mask, w, up, down, out, sh1, sh2, sh3, x1, x2, nrm, last, sems,
+    land, land_north, mask, w_hbm, up_hbm, down_hbm, out, w, up, down, w_sems, sh1, sh2, sh3, x1, x2, nrm, last, sems, m1, m2,
 ):
+    arrived = fetch(3, (w_hbm, up_hbm, down_hbm), (w, up, down), w_sems)
     first = pltpu.make_async_copy(out_south, out.at[0:18], sems.at[0])
     first.start()
+    turn = jnp.where(diagonal(True), 1.0, 0.0).astype(BF)
     for row in range(4):
         spread(sh1, row * 56, wide(28 + row, left, own, right), [4], 56, 2)
     for row in range(14):
-        spread(sh1, (row + 4) * 56, wide(row, north_left, north, north_right), [4], 56, 2)
+        source = wide(13 - row, north_right, north, north_left)
+        turned = jnp.dot(turn, source, preferred_element_type=F32).astype(BF)
+        spread(sh1, (row + 4) * 56, turned, [4], 56, 2)
+    for row in range(26, 44):
+        cells = spread_mask(land, row, False) if row < 32 else spread_mask(land_north, 45 - row, True)
+        if row >= 30:
+            m1[(row - 30) * 56 : (row - 29) * 56] = cells[4:60]
+        if row < 40:
+            m2[(row - 26) * 48 : (row - 25) * 48] = cells[8:56]
+    arrived(0, 0)
     conv_norm(0, sh1, 56, 28, [(30, 2, False), (32, 6, True), (38, 6, True)], w, nrm)
+    arrived(0, 1, 2)
     mlp(0, sh1, 56, 28, 30, [8, 6], up, down, m1, nrm, keep(x1, 56, 30), 30)
     for row in range(8):
         spread(sh2, row * 48, x1_tail[row * 56 : (row + 1) * 56], [4], 48, 4)
     for row in range(14):
         spread(sh2, (row + 8) * 48, x1[row * 56 : (row + 1) * 56], [4], 48, 4)
+    arrived(1, 0)
     conv_norm(1, sh2, 48, 22, [(26, 6, False), (32, 8, True)], w, nrm)
+    arrived(1, 1, 2)
     mlp(1, sh2, 48, 22, 26, [7, 7], up, down, m2, nrm, keep(x2, 48, 26), 26)
     for row in range(16):
         spread(sh3, row * 32, x2_tail[row * 48 : (row + 1) * 48], [8], 32, 8)
     for row in range(14):
         spread(sh3, (row + 16) * 32, x2[row * 48 : (row + 1) * 48], [8], 32, 8)
+    arrived(2, 0)
     conv_norm(2, sh3, 32, 10, [(18, 7, False), (25, 7, False)], w, nrm)
 
     def store3(row, count, value):
         last[row - 18 : row - 18 + count] = value.reshape(count, 32, 256)
 
+    arrived(2, 1, 2)
     mlp(2, sh3, 32, 10, 18, [7, 7], up, down, mask, nrm, store3)
     second = pltpu.make_async_copy(last, out.at[18:32], sems.at[1])
     second.start()
@@ -196,29 +256,35 @@
     return pltpu.VMEM((rows * width, 256), BF)
 
 
-def inner_call(own, mask, w, up, down):
+def weight_scratch(layers, *weights):
+    return [pltpu.VMEM((layers, *value.shape[1:]), BF) for value in weights] + [pltpu.SemaphoreType.DMA((3, layers))]
+
+
+def inner_call(own, land, w, up, down):
     return call(
-        inner_kernel, "inner", [(30 * 32, 256), (26 * 32, 256)],
-        [VMEM] * 5, [VMEM] * 2,
-        [taps(34, 32), taps(34, 32), flat(30, 32)],
-        1792, (own, mask, w, up, down),
+        inner_kernel, "inner", [(30 * 32, 256), (26 * 32, 256), (32 * 32, 128)],
+        [VMEM] * 2 + [HBM] * 3, [VMEM] * 3,
+        weight_scratch(2, w, up, down) + [taps(34, 32), taps(34, 32), flat(30, 32)],
+        1792, (own, land, w, up, down),
     )
 
 
 def south_call(*args):
     return call(
-        south_kernel, "south", [(8 * 56, 256), (16 * 48, 256), (18, 32, 256)], [VMEM] * len(args), [VMEM] * 3,
-        [taps(34, 32), taps(34, 32), taps(34, 32), flat(30, 32), flat(26, 32), flat(30, 32)],
+        south_kernel, "south", [(8 * 56, 256), (16 * 48, 256), (18, 32, 256)], [VMEM] * (len(args) - 3) + [HBM] * 3, [VMEM] * 3,
+        weight_scratch(3, *args[-3:]) + [taps(34, 32), taps(34, 32), taps(34, 32), flat(30, 32), flat(26, 32), flat(30, 32),
+         pltpu.VMEM((30 * 32, 128), BF), pltpu.VMEM((26 * 32, 128), BF)],
         2368, args,
     )
 
 
 def north_call(*args):
     (out,) = call(
-        north_kernel, "north", [(32, 32, 256)], [VMEM] * len(args), [HBM],
-        [
+        north_kernel, "north", [(32, 32, 256)], [VMEM] * (len(args) - 3) + [HBM] * 3, [HBM],
+        weight_scratch(3, *args[-3:]) + [
             taps(18, 56), taps(22, 48), taps(30, 32), flat(14, 56), flat(14, 48), flat(14, 56),
             pltpu.VMEM((14, 32, 256), BF), pltpu.SemaphoreType.DMA((2,)),
+            pltpu.VMEM((14 * 56, 128), BF), pltpu.VMEM((14 * 48, 128), BF),
         ],
         1904, args,
     )
@@ -235,34 +301,21 @@
     cols = own.shape[1]
     left = around(own[:, cols - HALO :], 1)
     right = around(own[:, :HALO], -1)
-    strip = own[own.shape[0] - DEEP :][::-1, ::-1]
-    north = lax.ppermute(strip, "lon", [(i, count - 1 - i) for i in range(count)])
-
-    def cells_mask(parts):
-        part = jnp.concatenate(parts, axis=1) if len(parts) > 1 else parts[0]
-        part = part.reshape(-1, 1)
-        return jnp.broadcast_to(part, (part.shape[0], 128))
-
-    land_sea = land_sea.astype(BF)
-    at = lax.axis_index("lon") * cols
-    mask = cells_mask([lax.dynamic_slice_in_dim(land_sea, at, cols, 1)])
+    north = lax.ppermute(own[own.shape[0] - DEEP :], "lon", [(i, count - 1 - i) for i in range(count)])
+
+    at = lax.axis_index("lon")
+    land = jnp.concatenate([land_sea[:, -HALO:], land_sea, land_sea[:, :HALO]], axis=1).astype(F32)
+    land_north = lax.dynamic_slice_in_dim(land[-DEEP:], (count - 1 - at) * cols, cols + 2 * HALO, 1)
+    land = lax.dynamic_slice_in_dim(land, at * cols, cols + 2 * HALO, 1)
     weights = (w, up, down)
-    x1_mid, x2_mid = inner_call(own, mask, w, up, down)
-
-    land = jnp.concatenate([land_sea, land_sea[::-1, ::-1][:DEEP]], axis=0)
-    land = jnp.concatenate([land[:, -HALO:], land, land[:, :HALO]], axis=1)
-    land = lax.dynamic_slice_in_dim(land, at, cols + 2 * HALO, 1)
-    e1 = cells_mask([land[:30, 4:20], land[:30, 44:60]])
-    e2 = cells_mask([land[:26, 8:24], land[:26, 40:56]])
-    m1 = cells_mask([land[30:44, 4:60]])
-    m2 = cells_mask([land[26:40, 8:56]])
-    left, right, m1, m2 = lax.optimization_barrier((left, right, m1, m2))
-    x1_tail, x2_tail, out_south = south_call(left, own, right, x1_mid, x2_mid, e1, e2, mask, *weights)
+    x1_mid, x2_mid, mask = inner_call(own, land, *weights)
+    left, right, land_north = lax.optimization_barrier((left, right, land_north))
+    x1_tail, x2_tail, out_south = south_call(left, own, right, x1_mid, x2_mid, land, mask, *weights)
     north, x1_tail = lax.optimization_barrier((north, x1_tail))
-    north_left = around(north[:, cols - HALO :], 1)
-    north_right = around(north[:, :HALO], -1)
+    north_left = around(north[:, :HALO], 1)
+    north_right = around(north[:, cols - HALO :], -1)
     return north_call(
-        left, own, right, north, north_left, north_right, x1_tail, x2_tail, out_south, m1, m2, mask, *weights
+        left, own, right, north, north_left, north_right, x1_tail, x2_tail, out_south, land, land_north, mask, *weights
     )
 
 

time: 39.7 us -> 44.6 us (1.12)
  Pallas kernels: 18 us -> 27.6 us
  local copies, waits for them, and re-layouts: 7.57 us -> 3.08 us
    pallas_call x3, Pallas kernels: 18 us -> 27.6 us  [call(): pl.pallas_call(kernel, name=name, out_shape=tuple((jax.ShapeDtypeStruct(s...]
    unnamed x14 -> x6, local copies, waits for them, and re-layouts: 3.42 us -> 0.01 us
    broadcast_in_dim x10 -> x0, local copies, waits for them, and re-layouts: 1.33 us -> none  [cells_mask(): return jnp.broadcast_to(part, (part.shape[0], 128))]
    slice x9 -> x4, local copies, waits for them, and re-layouts: 0.75 us -> 1.78 us  [the longest x1 0.95 us: per_device(): own[own.shape[0] - DEEP:]]
    rev x1 -> x0, local copies, waits for them, and re-layouts: 0.77 us -> none  [per_device(): strip = own[own.shape[0] - DEEP:][::-1, ::-1]]
  transfers between devices with their start and end apart: 5 -> 5, of which waited for: 1 -> 1; matrix products, arithmetic and copies ran while one was open for 8% -> 5% of each run, Pallas kernels for 29% -> 41%
where the time goes in v2:
time: 44.6 us; the launch traced here: 44.4 us
  Pallas kernels  27.6 us (62%)
  starting transfers between devices  10.8 us (24%)
  local copies, waits for them, and re-layouts  3.08 us (7%)
  waiting for transfers between devices  2.59 us (6%)
    pallas_call x3, Pallas kernels, call(): pl.pallas_call(kernel, name=name, out_shape=tuple((jax.ShapeDtypeStruct(s...  27.6 us
    ppermute x4, starting transfers between devices, around(): lax.ppermute(value, 'lon', [(i, (i + step) % count) for i in range(count)])  10.1 us
    ppermute x4, waiting for transfers between devices, around(): lax.ppermute(value, 'lon', [(i, (i + step) % count) for i in range(count)])  2.59 us
    slice x1, local copies, waits for them, and re-layouts, per_device(): right = around(own[:, :HALO], -1)  1.13 us
    slice x1, local copies, waits for them, and re-layouts, per_device(): own[own.shape[0] - DEEP:]  0.95 us
  transfers between devices with their start and end apart: 5, of which 1 were waited for; matrix products, arithmetic and copies ran while one was open for 5% of the time, Pallas kernels for 41%

profile of v2, /device:TPU:0, one launch (start us, length us, event | category | flops | bytes accessed | tf_op | source)
XLA Modules:
  0.0 44.4 jit_solution(8270276195458566311)
XLA Ops:
  0.0 0.0 copy-start
  0.0 0.0 copy-start.2
  0.0 1.1 %fusion = (bf16[32,16,256]{2,1,0:T(8,128)(2,1)S(1)}, bf16[32,16,256]{2,1,0:T(8,128)(2,1)S(1)}) fusion(bf16[32,32,256]{2,1,0:T(8,128)(2,1)} %own.5), kind=kLoop, calls=%fused_computation.3 | loop fusion | bytes 1048576 | tf_op jit(solution)/shard_map/slice | solution.py:303
  1.1 0.5 %collective-permute-start = (bf16[32,16,256]{2,1,0:T(8,128)(2,1)S(1)}, bf16[32,16,256]{2,1,0:T(8,128)(2,1)S(1)}, u32[]{:S(2)}, u32[]{:S(2)}) collective-permute-start(bf16[32,16,256]{2,1,0:T(8,128)(2,1)S(1)} %get-tuple-element.28), channel_id=1, source_target_pairs={{0,1},{1,2},{2,3},{3,4},{4,5},{5,6},{6,7},{7,8},{8,9},{9,10},{10,1... | collective-permute-start | bytes 786440 | tf_op jit(solution)/shard_map/ppermute | solution.py:296
  1.7 5.1 %collective-permute-start.1 = (bf16[32,16,256]{2,1,0:T(8,128)(2,1)S(1)}, bf16[32,16,256]{2,1,0:T(8,128)(2,1)S(1)}, u32[]{:S(2)}, u32[]{:S(2)}) collective-permute-start(bf16[32,16,256]{2,1,0:T(8,128)(2,1)S(1)} %get-tuple-element.27), channel_id=1, source_target_pairs={{0,15},{1,0},{2,1},{3,2},{4,3},{5,4},{6,5},{7,6},{8,7},{9,8},{10,9... | collective-permute-start | bytes 786440 | tf_op jit(solution)/shard_map/ppermute | solution.py:296
  6.7 1.0 %slice.29 = bf16[14,32,256]{2,1,0:T(8,128)(2,1)S(1)} slice(bf16[32,32,256]{2,1,0:T(8,128)(2,1)} %own.5), slice={[18:32], [0:32], [0:256]} | slice | bytes 458752 | tf_op jit(solution)/shard_map/slice | solution.py:304
  7.7 0.7 %collective-permute-start.2 = (bf16[14,32,256]{2,1,0:T(8,128)(2,1)S(1)}, bf16[14,32,256]{2,1,0:T(8,128)(2,1)S(1)}, u32[]{:S(2)}, u32[]{:S(2)}) collective-permute-start(bf16[14,32,256]{2,1,0:T(8,128)(2,1)S(1)} %slice.29), channel_id=1, source_target_pairs={{0,15},{1,14},{2,13},{3,12},{4,11},{5,10},{6,9},{7,8},{8,7},{9,6},... | collective-permute-start | bytes 688136 | tf_op jit(solution)/shard_map/ppermute | solution.py:304
  8.4 0.8 %fusion.2 = (s32[32,16]{1,0:T(8,128)S(1)}, s32[32,16]{1,0:T(8,128)S(1)}) fusion(s32[32,512]{1,0:T(8,128)} %param.6), kind=kLoop, calls=%fused_computation.5 | loop fusion | bytes 8192 | tf_op jit(solution)/shard_map/slice | solution.py:307
  9.2 0.0 copy-done.2
  9.2 0.1 add_convert_fusion
  9.3 0.1 constant_dynamic-slice_fusion.land
  9.4 0.1 constant_dynamic-slice_fusion.1.land_north
  9.5 0.0 copy-done
  9.5 7.3 %inner.1 = (bf16[960,256]{1,0:T(8,128)(2,1)S(1)}, bf16[832,256]{1,0:T(8,128)(2,1)S(1)}, bf16[1024,128]{1,0:T(8,128)(2,1)S(1)}) custom-call(bf16[32,32,256]{2,1,0:T(8,128)(2,1)S(1)} %copy-done, f32[32,64]{1,0:T(8,128)S(1)} %constant_dynamic-slice_fusion.land, bf16[3,9,256,256]{3,2,1,0:T(8,128)(2,1)} %w_hbm.5, bf16[3,256,1024]{2,1,0:T(8,128)(2,1)} %up_hbm.5, ...), custom_call_target="tpu_custom_call" | custom-call | flops 3992977408 | bytes 1048576 | tf_op jit(solution)/shard_map/inner/pallas_call | solution.py:239
  16.8 0.0 collective-permute-done.left
  16.8 0.0 collective-permute-done.1.right
  16.8 0.0 copy-start.1
  16.8 11.1 %south.1 = (bf16[448,256]{1,0:T(8,128)(2,1)S(1)}, bf16[768,256]{1,0:T(8,128)(2,1)S(1)}, bf16[18,32,256]{2,1,0:T(8,128)(2,1)S(1)}) custom-call(bf16[32,16,256]{2,1,0:T(8,128)(2,1)S(1)} %collective-permute-done.left, bf16[32,32,256]{2,1,0:T(8,128)(2,1)} %own.5, bf16[32,16,256]{2,1,0:T(8,128)(2,1)S(1)} %collective-permute-done.1.right, ...), custom_call_target="tpu_custom_call" | custom-call | flops 5276434432 | bytes 1048576 | tf_op jit(solution)/shard_map/south/pallas_call | solution.py:239
  27.9 0.0 collective-permute-done.2.north
  28.0 1.7 %collective-permute-start.3 = (bf16[14,16,256]{2,1,0:T(8,128)(2,1)S(1)}, bf16[14,16,256]{2,1,0:T(8,128)(2,1)S(1)}, u32[]{:S(2)}, u32[]{:S(2)}) collective-permute-start(bf16[14,16,256]{2,1,0:T(8,128)(2,1)S(1)} %get-tuple-element.30), channel_id=1, source_target_pairs={{0,1},{1,2},{2,3},{3,4},{4,5},{5,6},{6,7},{7,8},{8,9},{9,10},{10,1... | collective-permute-start | bytes 344072 | tf_op jit(solution)/shard_map/ppermute | solution.py:296
  29.7 2.8 %collective-permute-start.4 = (bf16[14,16,256]{2,1,0:T(8,128)(2,1)S(1)}, bf16[14,16,256]{2,1,0:T(8,128)(2,1)S(1)}, u32[]{:S(2)}, u32[]{:S(2)}) collective-permute-start(bf16[14,16,256]{2,1,0:T(8,128)(2,1)S(1)} %get-tuple-element.29), channel_id=1, source_target_pairs={{0,15},{1,0},{2,1},{3,2},{4,3},{5,4},{6,5},{7,6},{8,7},{9,8},{10,9... | collective-permute-start | bytes 344072 | tf_op jit(solution)/shard_map/ppermute | solution.py:296
  32.5 2.6 %collective-permute-done.3.north_left = bf16[14,16,256]{2,1,0:T(8,128)(2,1)S(1)} collective-permute-done((bf16[14,16,256]{2,1,0:T(8,128)(2,1)S(1)}, bf16[14,16,256]{2,1,0:T(8,128)(2,1)S(1)}, u32[]{:S(2)}, u32[]{:S(2)}) %collective-permute-start.3) | collective-permute-done | bytes 114720 | tf_op jit(solution)/shard_map/ppermute | solution.py:296
  35.0 0.0 collective-permute-done.4.north_right
  35.0 0.0 copy-done.1
  35.0 9.2 %north.1 = bf16[32,32,256]{2,1,0:T(8,128)(2,1)} custom-call(bf16[32,16,256]{2,1,0:T(8,128)(2,1)S(1)} %collective-permute-done.left, bf16[32,32,256]{2,1,0:T(8,128)(2,1)S(1)} %copy-done.1, bf16[32,16,256]{2,1,0:T(8,128)(2,1)S(1)} %collective-permute-done.1.right, bf16[14,32,256]{2,1,0:T(8,128)(2,1)S(1)} %collective-permute-done.2.north, ...), custom_call_target="tpu_custom_call" | custom-call | flops 4242538496 | bytes 1048576 | tf_op jit(solution)/shard_map/north/pallas_call | solution.py:239
  (2 shorter events, 0.0 us)
Async XLA Ops:
  0.0 9.5 %copy-start = (bf16[32,32,256]{2,1,0:T(8,128)(2,1)S(1)}, bf16[32,32,256]{2,1,0:T(8,128)(2,1)}, u32[]{:S(2)}) copy-start(bf16[32,32,256]{2,1,0:T(8,128)(2,1)} %own.5) | copy-start | bytes 1572868
  0.0 9.2 %copy-start.2 = (s32[32,512]{1,0:T(8,128)S(1)}, s32[32,512]{1,0:T(8,128)}, u32[]{:S(2)}) copy-start(s32[32,512]{1,0:T(8,128)} %param.6) | copy-start | bytes 196612
  1.1 15.6 %collective-permute-start = (bf16[32,16,256]{2,1,0:T(8,128)(2,1)S(1)}, bf16[32,16,256]{2,1,0:T(8,128)(2,1)S(1)}, u32[]{:S(2)}, u32[]{:S(2)}) collective-permute-start(bf16[32,16,256]{2,1,0:T(8,128)(2,1)S(1)} %get-tuple-element.28), channel_id=1, source_target_pairs={{0,1},{1,2},{2,3},{3,4},{4,5},{5,6},{6,7},{7,8},{8,9},{9,10},{10,1... | collective-permute-start | bytes 786440 | tf_op jit(solution)/shard_map/ppermute | solution.py:296
  1.7 15.1 %collective-permute-start.1 = (bf16[32,16,256]{2,1,0:T(8,128)(2,1)S(1)}, bf16[32,16,256]{2,1,0:T(8,128)(2,1)S(1)}, u32[]{:S(2)}, u32[]{:S(2)}) collective-permute-start(bf16[32,16,256]{2,1,0:T(8,128)(2,1)S(1)} %get-tuple-element.27), channel_id=1, source_target_pairs={{0,15},{1,0},{2,1},{3,2},{4,3},{5,4},{6,5},{7,6},{8,7},{9,8},{10,9... | collective-permute-start | bytes 786440 | tf_op jit(solution)/shard_map/ppermute | solution.py:296
  7.7 20.3 %collective-permute-start.2 = (bf16[14,32,256]{2,1,0:T(8,128)(2,1)S(1)}, bf16[14,32,256]{2,1,0:T(8,128)(2,1)S(1)}, u32[]{:S(2)}, u32[]{:S(2)}) collective-permute-start(bf16[14,32,256]{2,1,0:T(8,128)(2,1)S(1)} %slice.29), channel_id=1, source_target_pairs={{0,15},{1,14},{2,13},{3,12},{4,11},{5,10},{6,9},{7,8},{8,7},{9,6},... | collective-permute-start | bytes 688136 | tf_op jit(solution)/shard_map/ppermute | solution.py:304
  16.8 18.3 %copy-start.1 = (bf16[32,32,256]{2,1,0:T(8,128)(2,1)S(1)}, bf16[32,32,256]{2,1,0:T(8,128)(2,1)}, u32[]{:S(2)}) copy-start(bf16[32,32,256]{2,1,0:T(8,128)(2,1)} %own.5) | copy-start | bytes 1572868
  28.0 7.1 %collective-permute-start.3 = (bf16[14,16,256]{2,1,0:T(8,128)(2,1)S(1)}, bf16[14,16,256]{2,1,0:T(8,128)(2,1)S(1)}, u32[]{:S(2)}, u32[]{:S(2)}) collective-permute-start(bf16[14,16,256]{2,1,0:T(8,128)(2,1)S(1)} %get-tuple-element.30), channel_id=1, source_target_pairs={{0,1},{1,2},{2,3},{3,4},{4,5},{5,6},{6,7},{7,8},{8,9},{9,10},{10,1... | collective-permute-start | bytes 344072 | tf_op jit(solution)/shard_map/ppermute | solution.py:296
  29.7 5.3 %collective-permute-start.4 = (bf16[14,16,256]{2,1,0:T(8,128)(2,1)S(1)}, bf16[14,16,256]{2,1,0:T(8,128)(2,1)S(1)}, u32[]{:S(2)}, u32[]{:S(2)}) collective-permute-start(bf16[14,16,256]{2,1,0:T(8,128)(2,1)S(1)} %get-tuple-element.29), channel_id=1, source_target_pairs={{0,15},{1,0},{2,1},{3,2},{4,3},{5,4},{6,5},{7,6},{8,7},{9,8},{10,9... | collective-permute-start | bytes 344072 | tf_op jit(solution)/shard_map/ppermute | solution.py:296

commit v3 on v1

--- a/solution.py
+++ b/solution.py
@@ -12,7 +12,8 @@
 F32 = jnp.float32
 HALO = 16
 DEEP = 14
-LIMIT = 24
+LIMIT = 20
+EDGE_CELLS = 2048
 RSQRT2 = np.float32(0.7071067811865476)
 
 
@@ -75,18 +76,61 @@
     return store
 
 
+def diagonal(turned):
+    rows = lax.broadcasted_iota(jnp.int32, (64, 64), 0)
+    cols = lax.broadcasted_iota(jnp.int32, (64, 64), 1)
+    return rows + cols == 63 if turned else rows == cols
+
+
+def spread_mask(land, first, count, turned):
+    lines = jnp.where(diagonal(turned)[None], land[first : first + count][:, None, :], 0.0).astype(BF)
+    cells = jnp.dot(lines.reshape(count * 64, 64), jnp.ones((64, 128), BF), preferred_element_type=F32)
+    return cells.astype(BF).reshape(count, 64, 128)
+
+
+def window(whole, first):
+    total = whole.shape[1]
+    source = lax.broadcasted_iota(jnp.int32, (total, 64), 0)
+    target = lax.broadcasted_iota(jnp.int32, (total, 64), 1) + first
+    target = jnp.where(target < 0, target + total, target)
+    target = jnp.where(target >= total, target - total, target)
+    pick = jnp.where(source == target, 1.0, 0.0).astype(BF)
+    return jnp.dot(whole, pick, preferred_element_type=F32)
+
+
+def edges_kernel(own, left, right, top, sems):
+    copies = [
+        pltpu.make_async_copy(own.at[:, 0:HALO], left, sems.at[0]),
+        pltpu.make_async_copy(own.at[:, 32 - HALO : 32], right, sems.at[1]),
+        pltpu.make_async_copy(own.at[32 - DEEP : 32], top, sems.at[2]),
+    ]
+    for copy in copies:
+        copy.start()
+    for copy in copies:
+        copy.wait()
+
+
 def wide(row, left, own, right):
     return jnp.concatenate([left[row], own[row], right[row]], axis=0)
 
 
-def inner_kernel(own, mask, w, up, down, x1, x2, sh1, sh2, nrm):
+def first_kernel(own, land_sea, w, up, down, x1, mask, land, land_north, sh1, nrm):
+    me = lax.axis_index("lon")
+    whole = land_sea[...].astype(F32).astype(BF)
+    land[...] = window(whole, me * 32 - HALO)
+    land_north[...] = window(whole, (lax.axis_size("lon") - 1 - me) * 32 - HALO)[32 - DEEP :]
+    mask[...] = spread_mask(land, 0, 32, False)[:, 16:48].reshape(32 * 32, 128)
     clear(sh1, 2 * 32)
-    clear(sh2, 4 * 32)
     edge = jnp.zeros((HALO, own.shape[-1]), BF)
     for row in range(32):
         spread(sh1, (row + 2) * 32, jnp.concatenate([edge, own[row], edge], axis=0), [16], 32, 2)
     conv_norm(0, sh1, 32, -2, [(0, 15, False), (15, 15, False)], w, nrm)
     mlp(0, sh1, 32, -2, 0, [15, 15], up, down, mask, nrm, keep(x1, 32, 0))
+
+
+def second_kernel(x1, mask, w, up, down, x2, sh2, nrm):
+    clear(sh2, 4 * 32)
+    edge = jnp.zeros((HALO, x1.shape[-1]), BF)
     for row in range(30):
         values = jnp.concatenate([edge, x1[row * 32 : (row + 1) * 32], edge], axis=0)
         spread(sh2, (row + 4) * 32, values, [16], 32, 4)
@@ -95,14 +139,17 @@
 
 
 def south_kernel(
-    left, own, right, x1_mid, x2_mid, e1, e2, mask, w, up, down,
-    x1_tail, x2_tail, out, sh1, sh2, sh3, x1, x2, nrm,
+    left, own, right, x1_mid, x2_mid, land, mask, w, up, down,
+    x1_tail, x2_tail, out, sh1, sh2, sh3, x1, x2, nrm, e1, e2,
 ):
     clear(sh1, 2 * 32)
     clear(sh2, 4 * 32)
     clear(sh3, 8 * 32)
     for row in range(32):
         spread(sh1, (row + 2) * 32, wide(row, left, own, right), [4, 44], 16, 2)
+    cells = spread_mask(land, 0, 30, False)
+    e1[...] = jnp.concatenate([cells[:, 4:20], cells[:, 44:60]], axis=1).reshape(30 * 32, 128)
+    e2[...] = jnp.concatenate([cells[:26, 8:24], cells[:26, 40:56]], axis=1).reshape(26 * 32, 128)
     conv_norm(0, sh1, 32, -2, [(0, 15, False), (15, 15, False)], w, nrm)
     mlp(0, sh1, 32, -2, 0, [15, 15], up, down, e1, nrm, keep(x1, 32, 0))
 
@@ -133,14 +180,25 @@
 
 def north_kernel(
     left, own, right, north, north_left, north_right, x1_tail, x2_tail, out_south,
-    m1, m2, mask, w, up, down, out, sh1, sh2, sh3, x1, x2, nrm, last, sems,
+    land, land_north, mask, w, up, down, out, sh1, sh2, sh3, x1, x2, nrm, last, sems, m1, m2,
 ):
     first = pltpu.make_async_copy(out_south, out.at[0:18], sems.at[0])
     first.start()
+    turn = jnp.where(diagonal(True), 1.0, 0.0).astype(BF)
     for row in range(4):
         spread(sh1, row * 56, wide(28 + row, left, own, right), [4], 56, 2)
     for row in range(14):
-        spread(sh1, (row + 4) * 56, wide(row, north_left, north, north_right), [4], 56, 2)
+        source = wide(13 - row, north_right, north, north_left)
+        turned = jnp.dot(turn, source, preferred_element_type=F32).astype(BF)
+        spread(sh1, (row + 4) * 56, turned, [4], 56, 2)
+    near = spread_mask(land, 26, 6, False)
+    far = spread_mask(land_north, 0, 14, True)
+    for row in range(26, 44):
+        cells = near[row - 26] if row < 32 else far[45 - row]
+        if row >= 30:
+            m1[(row - 30) * 56 : (row - 29) * 56] = cells[4:60]
+        if row < 40:
+            m2[(row - 26) * 48 : (row - 25) * 48] = cells[8:56]
     conv_norm(0, sh1, 56, 28, [(30, 2, False), (32, 6, True), (38, 6, True)], w, nrm)
     mlp(0, sh1, 56, 28, 30, [8, 6], up, down, m1, nrm, keep(x1, 56, 30), 30)
     for row in range(8):
@@ -175,15 +233,15 @@
 HBM = pl.BlockSpec(memory_space=pltpu.HBM)
 
 
-def call(kernel, name, outs, in_specs, out_specs, scratch, cells, args):
+def call(kernel, name, outs, in_specs, out_specs, scratch, cells, args, limit=LIMIT):
     return pl.pallas_call(
         kernel,
         name=name,
-        out_shape=tuple(jax.ShapeDtypeStruct(shape, BF) for shape in outs),
+        out_shape=tuple(jax.ShapeDtypeStruct(*(out if isinstance(out[0], tuple) else (out, BF))) for out in outs),
         in_specs=in_specs,
         out_specs=tuple(out_specs),
         scratch_shapes=scratch,
-        compiler_params=pltpu.CompilerParams(vmem_limit_bytes=LIMIT * 2**20),
+        compiler_params=pltpu.CompilerParams(vmem_limit_bytes=limit * 2**20),
         cost_estimate=cost(cells),
     )(*args)
 
@@ -196,19 +254,32 @@
     return pltpu.VMEM((rows * width, 256), BF)
 
 
-def inner_call(own, mask, w, up, down):
+def edges_call(own):
     return call(
-        inner_kernel, "inner", [(30 * 32, 256), (26 * 32, 256)],
-        [VMEM] * 5, [VMEM] * 2,
-        [taps(34, 32), taps(34, 32), flat(30, 32)],
-        1792, (own, mask, w, up, down),
-    )
+        edges_kernel, "edges", [(32, HALO, 256), (32, HALO, 256), (DEEP, 32, 256)], [HBM], [VMEM] * 3,
+        [pltpu.SemaphoreType.DMA((3,))], EDGE_CELLS, (own,),
+    )
+
+
+def first_call(*args):
+    return call(
+        first_kernel, "first", [(30 * 32, 256), (32 * 32, 128), ((32, 64), F32), ((DEEP, 64), F32)],
+        [VMEM] * len(args), [VMEM] * 4, [taps(34, 32), flat(30, 32)], 960, args,
+    )
+
+
+def second_call(*args):
+    (x2,) = call(
+        second_kernel, "second", [(26 * 32, 256)], [VMEM] * len(args), [VMEM], [taps(34, 32), flat(26, 32)], 832, args
+    )
+    return x2
 
 
 def south_call(*args):
     return call(
         south_kernel, "south", [(8 * 56, 256), (16 * 48, 256), (18, 32, 256)], [VMEM] * len(args), [VMEM] * 3,
-        [taps(34, 32), taps(34, 32), taps(34, 32), flat(30, 32), flat(26, 32), flat(30, 32)],
+        [taps(34, 32), taps(34, 32), taps(34, 32), flat(30, 32), flat(26, 32), flat(30, 32),
+         pltpu.VMEM((30 * 32, 128), BF), pltpu.VMEM((26 * 32, 128), BF)],
         2368, args,
     )
 
@@ -219,6 +290,7 @@
         [
             taps(18, 56), taps(22, 48), taps(30, 32), flat(14, 56), flat(14, 48), flat(14, 56),
             pltpu.VMEM((14, 32, 256), BF), pltpu.SemaphoreType.DMA((2,)),
+            pltpu.VMEM((14 * 56, 128), BF), pltpu.VMEM((14 * 48, 128), BF),
         ],
         1904, args,
     )
@@ -233,36 +305,20 @@
 def per_device(own, land_sea, w, up, down):
     count = lax.axis_size("lon")
     cols = own.shape[1]
-    left = around(own[:, cols - HALO :], 1)
-    right = around(own[:, :HALO], -1)
-    strip = own[own.shape[0] - DEEP :][::-1, ::-1]
-    north = lax.ppermute(strip, "lon", [(i, count - 1 - i) for i in range(count)])
-
-    def cells_mask(parts):
-        part = jnp.concatenate(parts, axis=1) if len(parts) > 1 else parts[0]
-        part = part.reshape(-1, 1)
-        return jnp.broadcast_to(part, (part.shape[0], 128))
-
-    land_sea = land_sea.astype(BF)
-    at = lax.axis_index("lon") * cols
-    mask = cells_mask([lax.dynamic_slice_in_dim(land_sea, at, cols, 1)])
+    head, tail, top = edges_call(own)
+    left = around(tail, 1)
+    right = around(head, -1)
     weights = (w, up, down)
-    x1_mid, x2_mid = inner_call(own, mask, w, up, down)
-
-    land = jnp.concatenate([land_sea, land_sea[::-1, ::-1][:DEEP]], axis=0)
-    land = jnp.concatenate([land[:, -HALO:], land, land[:, :HALO]], axis=1)
-    land = lax.dynamic_slice_in_dim(land, at, cols + 2 * HALO, 1)
-    e1 = cells_mask([land[:30, 4:20], land[:30, 44:60]])
-    e2 = cells_mask([land[:26, 8:24], land[:26, 40:56]])
-    m1 = cells_mask([land[30:44, 4:60]])
-    m2 = cells_mask([land[26:40, 8:56]])
-    left, right, m1, m2 = lax.optimization_barrier((left, right, m1, m2))
-    x1_tail, x2_tail, out_south = south_call(left, own, right, x1_mid, x2_mid, e1, e2, mask, *weights)
+    x1_mid, mask, land, land_north = first_call(own, land_sea, *weights)
+    top, x1_mid = lax.optimization_barrier((top, x1_mid))
+    north = lax.ppermute(top, "lon", [(i, count - 1 - i) for i in range(count)])
+    x2_mid = second_call(x1_mid, mask, *weights)
+    x1_tail, x2_tail, out_south = south_call(left, own, right, x1_mid, x2_mid, land, mask, *weights)
     north, x1_tail = lax.optimization_barrier((north, x1_tail))
-    north_left = around(north[:, cols - HALO :], 1)
-    north_right = around(north[:, :HALO], -1)
+    north_left = around(north[:, :HALO], 1)
+    north_right = around(north[:, cols - HALO :], -1)
     return north_call(
-        left, own, right, north, north_left, north_right, x1_tail, x2_tail, out_south, m1, m2, mask, *weights
+        left, own, right, north, north_left, north_right, x1_tail, x2_tail, out_south, land, land_north, mask, *weights
     )
 
 

time: 39.7 us -> 38 us (0.957)
  local copies, waits for them, and re-layouts: 7.57 us -> 1.22 us
  waiting for transfers between devices: 2.59 us -> 6.92 us
  Pallas kernels: 18 us -> 19.3 us
  starting transfers between devices: 10.7 us -> 10.1 us
    ppermute x4, waiting for transfers between devices: 2.58 us -> 6.92 us  [around(): lax.ppermute(value, 'lon', [(i, (i + step) % count) for i in range(count)])]
    unnamed x14 -> x10, local copies, waits for them, and re-layouts: 3.42 us -> 1.21 us
    slice x10 -> x1, local copies, waits for them, and re-layouts: 1.97 us -> 0.02 us  [per_device(): north_right = around(north[:, cols - HALO:], -1)]
    ppermute x4, starting transfers between devices: 10.1 us -> 8.61 us  [around(): lax.ppermute(value, 'lon', [(i, (i + step) % count) for i in range(count)])]
    pallas_call x3 -> x5, Pallas kernels: 18 us -> 19.3 us  [call(): pl.pallas_call(kernel, name=name, out_shape=tuple((jax.ShapeDtypeStruct(*...]
    broadcast_in_dim x10 -> x0, local copies, waits for them, and re-layouts: 1.33 us -> none  [cells_mask(): return jnp.broadcast_to(part, (part.shape[0], 128))]
    ppermute x1, starting transfers between devices: 0.68 us -> 1.52 us  [per_device(): north = lax.ppermute(top, 'lon', [(i, count - 1 - i) for i in range(count)])]
    rev x1 -> x0, local copies, waits for them, and re-layouts: 0.77 us -> none  [per_device(): strip = own[own.shape[0] - DEEP:][::-1, ::-1]]
  transfers between devices with their start and end apart: 5 -> 5, of which waited for: 1 -> 2; matrix products, arithmetic and copies ran while one was open for 8% -> 0% of each run, Pallas kernels for 29% -> 32%
where the time goes in v3:
time: 38 us; the launch traced here: 37.8 us
  Pallas kernels  19.3 us (51%)
  starting transfers between devices  10.1 us (27%)
  waiting for transfers between devices  6.92 us (18%)
  local copies, waits for them, and re-layouts  1.22 us (3%)
    pallas_call x5, Pallas kernels, call(): pl.pallas_call(kernel, name=name, out_shape=tuple((jax.ShapeDtypeStruct(*...  19.3 us
    ppermute x4, starting transfers between devices, around(): lax.ppermute(value, 'lon', [(i, (i + step) % count) for i in range(count)])  8.61 us
    ppermute x4, waiting for transfers between devices, around(): lax.ppermute(value, 'lon', [(i, (i + step) % count) for i in range(count)])  6.92 us
    ppermute x1, starting transfers between devices, per_device(): north = lax.ppermute(top, 'lon', [(i, count - 1 - i) for i in range(count)])  1.52 us
    unnamed x10, local copies, waits for them, and re-layouts  1.21 us
  transfers between devices with their start and end apart: 5, of which 2 were waited for; matrix products, arithmetic and copies ran while one was open for 0% of the time, Pallas kernels for 32%

profile of v3, /device:TPU:0, one launch (start us, length us, event | category | flops | bytes accessed | tf_op | source)
XLA Modules:
  0.0 37.8 jit_solution(1204558191152417808)
XLA Ops:
  0.0 0.0 copy-start.2
  0.0 0.0 copy-start.1
  0.0 0.0 copy-start
  0.0 0.0 copy-start.3
  0.0 1.2 %copy-done.3 = bf16[32,32,256]{2,1,0:T(8,128)(2,1)S(1)} copy-done((bf16[32,32,256]{2,1,0:T(8,128)(2,1)S(1)}, bf16[32,32,256]{2,1,0:T(8,128)(2,1)}, u32[]{:S(2)}) %copy-start.3) | copy-done | bytes 524312
  1.2 0.0 copy-start.4
  1.2 0.4 edges.1
  1.6 0.5 %collective-permute-start = (bf16[32,16,256]{2,1,0:T(8,128)(2,1)S(1)}, bf16[32,16,256]{2,1,0:T(8,128)(2,1)S(1)}, u32[]{:S(2)}, u32[]{:S(2)}) collective-permute-start(bf16[32,16,256]{2,1,0:T(8,128)(2,1)S(1)} %get-tuple-element.19), channel_id=1, source_target_pairs={{0,1},{1,2},{2,3},{3,4},{4,5},{5,6},{6,7},{7,8},{8,9},{9,10},{10,1... | collective-permute-start | bytes 786440 | tf_op jit(solution)/shard_map/ppermute | solution.py:302
  2.1 5.1 %collective-permute-start.1 = (bf16[32,16,256]{2,1,0:T(8,128)(2,1)S(1)}, bf16[32,16,256]{2,1,0:T(8,128)(2,1)S(1)}, u32[]{:S(2)}, u32[]{:S(2)}) collective-permute-start(bf16[32,16,256]{2,1,0:T(8,128)(2,1)S(1)} %get-tuple-element.20), channel_id=1, source_target_pairs={{0,15},{1,0},{2,1},{3,2},{4,3},{5,4},{6,5},{7,6},{8,7},{9,8},{10,9... | collective-permute-start | bytes 786440 | tf_op jit(solution)/shard_map/ppermute | solution.py:302
  7.1 0.0 copy-done.2
  7.1 0.0 copy-done.1
  7.1 0.0 copy-done
  7.1 0.0 copy-done.4
  7.1 3.2 %first.1 = (bf16[960,256]{1,0:T(8,128)(2,1)S(1)}, bf16[1024,128]{1,0:T(8,128)(2,1)S(1)}, f32[32,64]{1,0:T(8,128)S(1)}, f32[14,64]{1,0:T(8,128)S(1)}) custom-call(bf16[32,32,256]{2,1,0:T(8,128)(2,1)S(1)} %copy-done.3, s32[32,512]{1,0:T(8,128)S(1)} %copy-done.4, bf16[3,9,256,256]{3,2,1,0:T(8,128)(2,1)S(1)} %copy-done, bf16[3,256,1024]{2,1,0:T(8,128)(2,1)S(1)} %copy-done.1, ...), custom_call_target="tpu_custom_call" | custom-call | flops 2139095040 | bytes 1048576 | tf_op jit(solution)/shard_map/first/pallas_call | solution.py:237
  10.3 1.5 %collective-permute-start.2 = (bf16[14,32,256]{2,1,0:T(8,128)(2,1)S(1)}, bf16[14,32,256]{2,1,0:T(8,128)(2,1)S(1)}, u32[]{:S(2)}, u32[]{:S(2)}) collective-permute-start(bf16[14,32,256]{2,1,0:T(8,128)(2,1)S(1)} %get-tuple-element.23), channel_id=1, source_target_pairs={{0,15},{1,14},{2,13},{3,12},{4,11},{5,10},{6,9},{7,8},{8,7},{9,6},... | collective-permute-start | bytes 688136 | tf_op jit(solution)/shard_map/ppermute | solution.py:314
  11.9 2.4 %second.1.x2_mid = bf16[832,256]{1,0:T(8,128)(2,1)S(1)} custom-call(bf16[960,256]{1,0:T(8,128)(2,1)S(1)} %get-tuple-element.24.x1.x1_mid, bf16[1024,128]{1,0:T(8,128)(2,1)S(1)} %get-tuple-element.25.mask, bf16[3,9,256,256]{3,2,1,0:T(8,128)(2,1)S(1)} %copy-done, bf16[3,256,1024]{2,1,0:T(8,128)(2,1)S(1)} %copy-done.1, bf16[3,1024,256]{2,1,0:T(8,128)(2,1)S(1)} %copy-done.2), custom_call_target="tpu_custom_call" | custom-call | flops 1853882368 | bytes 1048576 | tf_op jit(solution)/shard_map/second/pallas_call | solution.py:237
  14.2 0.0 collective-permute-done.left
  14.2 0.0 collective-permute-done.1.right
  14.3 6.6 %south.1 = (bf16[448,256]{1,0:T(8,128)(2,1)S(1)}, bf16[768,256]{1,0:T(8,128)(2,1)S(1)}, bf16[18,32,256]{2,1,0:T(8,128)(2,1)S(1)}) custom-call(bf16[32,16,256]{2,1,0:T(8,128)(2,1)S(1)} %collective-permute-done.left, bf16[32,32,256]{2,1,0:T(8,128)(2,1)S(1)} %copy-done.3, bf16[32,16,256]{2,1,0:T(8,128)(2,1)S(1)} %collective-permute-done.1.right, ...), custom_call_target="tpu_custom_call" | custom-call | flops 5276434432 | bytes 1048576 | tf_op jit(solution)/shard_map/south/pallas_call | solution.py:237
  20.9 0.0 collective-permute-done.2.north
  20.9 3.0 %collective-permute-start.4 = (bf16[14,16,256]{2,1,0:T(8,128)(2,1)S(1)}, bf16[14,16,256]{2,1,0:T(8,128)(2,1)S(1)}, u32[]{:S(2)}, u32[]{:S(2)}) collective-permute-start(bf16[14,16,256]{2,1,0:T(8,128)(2,1)S(1)} %get-tuple-element.33), channel_id=1, source_target_pairs={{0,15},{1,0},{2,1},{3,2},{4,3},{5,4},{6,5},{7,6},{8,7},{9,8},{10,9... | collective-permute-start | bytes 344072 | tf_op jit(solution)/shard_map/ppermute | solution.py:302
  23.9 0.0 collective-permute-start.3
  24.0 2.4 %collective-permute-done.4.north_right = bf16[14,16,256]{2,1,0:T(8,128)(2,1)S(1)} collective-permute-done((bf16[14,16,256]{2,1,0:T(8,128)(2,1)S(1)}, bf16[14,16,256]{2,1,0:T(8,128)(2,1)S(1)}, u32[]{:S(2)}, u32[]{:S(2)}) %collective-permute-start.4) | collective-permute-done | bytes 114720 | tf_op jit(solution)/shard_map/ppermute | solution.py:302
  26.3 4.5 %collective-permute-done.3.north_left = bf16[14,16,256]{2,1,0:T(8,128)(2,1)S(1)} collective-permute-done((bf16[14,16,256]{2,1,0:T(8,128)(2,1)S(1)}, bf16[14,16,256]{2,1,0:T(8,128)(2,1)S(1)}, u32[]{:S(2)}, u32[]{:S(2)}) %collective-permute-start.3) | collective-permute-done | bytes 114720 | tf_op jit(solution)/shard_map/ppermute | solution.py:302
  30.9 6.8 %north.1 = bf16[32,32,256]{2,1,0:T(8,128)(2,1)} custom-call(bf16[32,16,256]{2,1,0:T(8,128)(2,1)S(1)} %collective-permute-done.left, bf16[32,32,256]{2,1,0:T(8,128)(2,1)S(1)} %copy-done.3, bf16[32,16,256]{2,1,0:T(8,128)(2,1)S(1)} %collective-permute-done.1.right, bf16[14,32,256]{2,1,0:T(8,128)(2,1)S(1)} %collective-permute-done.2.north, ...), custom_call_target="tpu_custom_call" | custom-call | flops 4242538496 | bytes 1048576 | tf_op jit(solution)/shard_map/north/pallas_call | solution.py:237
  (1 shorter events, 0.0 us)
Async XLA Ops:
  0.0 7.1 %copy-start.2 = (bf16[3,1024,256]{2,1,0:T(8,128)(2,1)S(1)}, bf16[3,1024,256]{2,1,0:T(8,128)(2,1)}, u32[]{:S(2)}) copy-start(bf16[3,1024,256]{2,1,0:T(8,128)(2,1)} %down.7) | copy-start | bytes 4718596
  0.0 7.1 %copy-start.1 = (bf16[3,256,1024]{2,1,0:T(8,128)(2,1)S(1)}, bf16[3,256,1024]{2,1,0:T(8,128)(2,1)}, u32[]{:S(2)}) copy-start(bf16[3,256,1024]{2,1,0:T(8,128)(2,1)} %up.7) | copy-start | bytes 4718596
  0.0 7.1 %copy-start = (bf16[3,9,256,256]{3,2,1,0:T(8,128)(2,1)S(1)}, bf16[3,9,256,256]{3,2,1,0:T(8,128)(2,1)}, u32[]{:S(2)}) copy-start(bf16[3,9,256,256]{3,2,1,0:T(8,128)(2,1)} %w.7) | copy-start | bytes 10616836
  0.0 1.2 %copy-start.3 = (bf16[32,32,256]{2,1,0:T(8,128)(2,1)S(1)}, bf16[32,32,256]{2,1,0:T(8,128)(2,1)}, u32[]{:S(2)}) copy-start(bf16[32,32,256]{2,1,0:T(8,128)(2,1)} %own.7) | copy-start | bytes 1572868
  1.2 5.9 %copy-start.4 = (s32[32,512]{1,0:T(8,128)S(1)}, s32[32,512]{1,0:T(8,128)}, u32[]{:S(2)}) copy-start(s32[32,512]{1,0:T(8,128)} %land_sea.1) | copy-start | bytes 196612
  1.6 12.7 %collective-permute-start = (bf16[32,16,256]{2,1,0:T(8,128)(2,1)S(1)}, bf16[32,16,256]{2,1,0:T(8,128)(2,1)S(1)}, u32[]{:S(2)}, u32[]{:S(2)}) collective-permute-start(bf16[32,16,256]{2,1,0:T(8,128)(2,1)S(1)} %get-tuple-element.19), channel_id=1, source_target_pairs={{0,1},{1,2},{2,3},{3,4},{4,5},{5,6},{6,7},{7,8},{8,9},{9,10},{10,1... | collective-permute-start | bytes 786440 | tf_op jit(solution)/shard_map/ppermute | solution.py:302
  2.1 12.2 %collective-permute-start.1 = (bf16[32,16,256]{2,1,0:T(8,128)(2,1)S(1)}, bf16[32,16,256]{2,1,0:T(8,128)(2,1)S(1)}, u32[]{:S(2)}, u32[]{:S(2)}) collective-permute-start(bf16[32,16,256]{2,1,0:T(8,128)(2,1)S(1)} %get-tuple-element.20), channel_id=1, source_target_pairs={{0,15},{1,0},{2,1},{3,2},{4,3},{5,4},{6,5},{7,6},{8,7},{9,8},{10,9... | collective-permute-start | bytes 786440 | tf_op jit(solution)/shard_map/ppermute | solution.py:302
  10.3 10.5 %collective-permute-start.2 = (bf16[14,32,256]{2,1,0:T(8,128)(2,1)S(1)}, bf16[14,32,256]{2,1,0:T(8,128)(2,1)S(1)}, u32[]{:S(2)}, u32[]{:S(2)}) collective-permute-start(bf16[14,32,256]{2,1,0:T(8,128)(2,1)S(1)} %get-tuple-element.23), channel_id=1, source_target_pairs={{0,15},{1,14},{2,13},{3,12},{4,11},{5,10},{6,9},{7,8},{8,7},{9,6},... | collective-permute-start | bytes 688136 | tf_op jit(solution)/shard_map/ppermute | solution.py:314
  20.9 5.4 %collective-permute-start.4 = (bf16[14,16,256]{2,1,0:T(8,128)(2,1)S(1)}, bf16[14,16,256]{2,1,0:T(8,128)(2,1)S(1)}, u32[]{:S(2)}, u32[]{:S(2)}) collective-permute-start(bf16[14,16,256]{2,1,0:T(8,128)(2,1)S(1)} %get-tuple-element.33), channel_id=1, source_target_pairs={{0,15},{1,0},{2,1},{3,2},{4,3},{5,4},{6,5},{7,6},{8,7},{9,8},{10,9... | collective-permute-start | bytes 344072 | tf_op jit(solution)/shard_map/ppermute | solution.py:302
  23.9 6.9 %collective-permute-start.3 = (bf16[14,16,256]{2,1,0:T(8,128)(2,1)S(1)}, bf16[14,16,256]{2,1,0:T(8,128)(2,1)S(1)}, u32[]{:S(2)}, u32[]{:S(2)}) collective-permute-start(bf16[14,16,256]{2,1,0:T(8,128)(2,1)S(1)} %get-tuple-element.34), channel_id=1, source_target_pairs={{0,1},{1,2},{2,3},{3,4},{4,5},{5,6},{6,7},{7,8},{8,9},{9,10},{10,1... | collective-permute-start | bytes 344072 | tf_op jit(solution)/shard_map/ppermute | solution.py:302

commit v4 on v3

--- a/solution.py
+++ b/solution.py
@@ -76,10 +76,10 @@
     return store
 
 
-def diagonal(turned):
-    rows = lax.broadcasted_iota(jnp.int32, (64, 64), 0)
-    cols = lax.broadcasted_iota(jnp.int32, (64, 64), 1)
-    return rows + cols == 63 if turned else rows == cols
+def diagonal(turned, size=64):
+    rows = lax.broadcasted_iota(jnp.int32, (size, size), 0)
+    cols = lax.broadcasted_iota(jnp.int32, (size, size), 1)
+    return rows + cols == size - 1 if turned else rows == cols
 
 
 def spread_mask(land, first, count, turned):
@@ -178,40 +178,73 @@
     mlp(2, sh3, 32, -8, 0, [9, 9], up, down, mask, nrm, store3)
 
 
+def strips(cells, left, right):
+    rows = cells.shape[0]
+    return jnp.concatenate([cells[:, left : left + 16], cells[:, right : right + 16]], axis=1).reshape(rows * 32, 128)
+
+
+def fold_kernel(own, north, x1_tail, land, land_north, w, up, down, x1, x2, e1, e2, sh1, sh2, nrm, m1, m2):
+    near = spread_mask(land, 26, 6, False)
+    far = spread_mask(land_north, 0, DEEP, True)
+    cells = jnp.concatenate([near] + [far[45 - row : 46 - row] for row in range(32, 44)], axis=0)
+    m1[...] = cells[4:, 16:48].reshape(14 * 32, 128)
+    m2[...] = cells[:14, 16:48].reshape(14 * 32, 128)
+    e1[...] = strips(cells[4:], 4, 44)
+    e2[...] = strips(cells[:14], 8, 40)
+    turn = jnp.where(diagonal(True, 32), 1.0, 0.0).astype(BF)
+    edge = jnp.zeros((HALO, own.shape[-1]), BF)
+    for row in range(18):
+        if row < 4:
+            line = own[28 + row]
+        else:
+            line = jnp.dot(turn, north[17 - row], preferred_element_type=F32).astype(BF)
+        spread(sh1, row * 32, jnp.concatenate([edge, line, edge], axis=0), [16], 32, 2)
+    conv_norm(0, sh1, 32, 28, [(30, 2, False), (32, 12, True)], w, nrm)
+    mlp(0, sh1, 32, 28, 30, [7, 7], up, down, m1, nrm, keep(x1, 32, 30), 30)
+    for row in range(8):
+        spread(sh2, row * 32, x1_tail[row * 56 : (row + 1) * 56], [12], 32, 4)
+    for row in range(14):
+        values = jnp.concatenate([edge, x1[row * 32 : (row + 1) * 32], edge], axis=0)
+        spread(sh2, (row + 8) * 32, values, [16], 32, 4)
+    conv_norm(1, sh2, 32, 22, [(26, 6, False), (32, 8, True)], w, nrm)
+    mlp(1, sh2, 32, 22, 26, [7, 7], up, down, m2, nrm, keep(x2, 32, 26), 26)
+
+
 def north_kernel(
-    left, own, right, north, north_left, north_right, x1_tail, x2_tail, out_south,
-    land, land_north, mask, w, up, down, out, sh1, sh2, sh3, x1, x2, nrm, last, sems, m1, m2,
+    left, own, right, north, north_left, north_right, x1_tail, x2_tail, out_south, x1_mid, x2_mid,
+    e1, e2, mask, w, up, down, out, sh1, sh2, sh3, x1, x2, nrm, last, sems,
 ):
     first = pltpu.make_async_copy(out_south, out.at[0:18], sems.at[0])
     first.start()
+    half = lax.axis_size("lon") // 2
+    place = lax.rem(lax.axis_index("lon"), half)
     turn = jnp.where(diagonal(True), 1.0, 0.0).astype(BF)
     for row in range(4):
-        spread(sh1, row * 56, wide(28 + row, left, own, right), [4], 56, 2)
+        spread(sh1, row * 32, wide(28 + row, left, own, right), [4, 44], 16, 2)
     for row in range(14):
-        source = wide(13 - row, north_right, north, north_left)
+        at = 13 - row
+        after = jnp.where(place == 0, own[18 + at, 0:HALO], north_left[at])
+        before = jnp.where(place == half - 1, own[18 + at, 32 - HALO : 32], north_right[at])
+        source = jnp.concatenate([before, north[at], after], axis=0)
         turned = jnp.dot(turn, source, preferred_element_type=F32).astype(BF)
-        spread(sh1, (row + 4) * 56, turned, [4], 56, 2)
-    near = spread_mask(land, 26, 6, False)
-    far = spread_mask(land_north, 0, 14, True)
-    for row in range(26, 44):
-        cells = near[row - 26] if row < 32 else far[45 - row]
-        if row >= 30:
-            m1[(row - 30) * 56 : (row - 29) * 56] = cells[4:60]
-        if row < 40:
-            m2[(row - 26) * 48 : (row - 25) * 48] = cells[8:56]
-    conv_norm(0, sh1, 56, 28, [(30, 2, False), (32, 6, True), (38, 6, True)], w, nrm)
-    mlp(0, sh1, 56, 28, 30, [8, 6], up, down, m1, nrm, keep(x1, 56, 30), 30)
+        spread(sh1, (row + 4) * 32, turned, [4, 44], 16, 2)
+    conv_norm(0, sh1, 32, 28, [(30, 2, False), (32, 12, True)], w, nrm)
+    mlp(0, sh1, 32, 28, 30, [7, 7], up, down, e1, nrm, keep(x1, 32, 30), 30)
     for row in range(8):
-        spread(sh2, row * 48, x1_tail[row * 56 : (row + 1) * 56], [4], 48, 4)
+        spread(sh2, row * 32, x1_tail[row * 56 : (row + 1) * 56], [4, 36], 16, 4)
     for row in range(14):
-        spread(sh2, (row + 8) * 48, x1[row * 56 : (row + 1) * 56], [4], 48, 4)
-    conv_norm(1, sh2, 48, 22, [(26, 6, False), (32, 8, True)], w, nrm)
-    mlp(1, sh2, 48, 22, 26, [7, 7], up, down, m2, nrm, keep(x2, 48, 26), 26)
+        at = row * 32
+        values = jnp.concatenate([x1[at : at + 16], x1_mid[at + 4 : at + 28], x1[at + 16 : at + 32]], axis=0)
+        spread(sh2, (row + 8) * 32, values, [4, 36], 16, 4)
+    conv_norm(1, sh2, 32, 22, [(26, 6, False), (32, 8, True)], w, nrm)
+    mlp(1, sh2, 32, 22, 26, [7, 7], up, down, e2, nrm, keep(x2, 32, 26), 26)
     for row in range(16):
         spread(sh3, row * 32, x2_tail[row * 48 : (row + 1) * 48], [8], 32, 8)
     for row in range(14):
-        spread(sh3, (row + 16) * 32, x2[row * 48 : (row + 1) * 48], [8], 32, 8)
-    conv_norm(2, sh3, 32, 10, [(18, 7, False), (25, 7, False)], w, nrm)
+        at = row * 32
+        values = jnp.concatenate([x2[at : at + 16], x2_mid[at + 8 : at + 24], x2[at + 16 : at + 32]], axis=0)
+        spread(sh3, (row + 16) * 32, values, [8], 32, 8)
+    conv_norm(2, sh3, 32, 10, [(18, 14, False)], w, nrm)
 
     def store3(row, count, value):
         last[row - 18 : row - 18 + count] = value.reshape(count, 32, 256)
@@ -284,22 +317,31 @@
     )
 
 
+def fold_call(*args):
+    return call(
+        fold_kernel, "fold", [(14 * 32, 256), (14 * 32, 256), (14 * 32, 128), (14 * 32, 128)],
+        [VMEM] * len(args), [VMEM] * 4,
+        [taps(18, 32), taps(22, 32), flat(14, 32), pltpu.VMEM((14 * 32, 128), BF), pltpu.VMEM((14 * 32, 128), BF)],
+        896, args,
+    )
+
+
 def north_call(*args):
     (out,) = call(
         north_kernel, "north", [(32, 32, 256)], [VMEM] * len(args), [HBM],
         [
-            taps(18, 56), taps(22, 48), taps(30, 32), flat(14, 56), flat(14, 48), flat(14, 56),
+            taps(18, 32), taps(22, 32), taps(30, 32), flat(14, 32), flat(14, 32), flat(14, 32),
             pltpu.VMEM((14, 32, 256), BF), pltpu.SemaphoreType.DMA((2,)),
-            pltpu.VMEM((14 * 56, 128), BF), pltpu.VMEM((14 * 48, 128), BF),
         ],
-        1904, args,
+        1344, args,
     )
     return out
 
 
-def around(value, step):
-    count = lax.axis_size("lon")
-    return lax.ppermute(value, "lon", [(i, (i + step) % count) for i in range(count)])
+def around(value, step, ring=1):
+    count = lax.axis_size("lon") // ring
+    pairs = [(i, i // count * count + (i + step) % count) for i in range(ring * count)]
+    return lax.ppermute(value, "lon", pairs)
 
 
 def per_device(own, land_sea, w, up, down):
@@ -315,10 +357,11 @@
     x2_mid = second_call(x1_mid, mask, *weights)
     x1_tail, x2_tail, out_south = south_call(left, own, right, x1_mid, x2_mid, land, mask, *weights)
     north, x1_tail = lax.optimization_barrier((north, x1_tail))
-    north_left = around(north[:, :HALO], 1)
-    north_right = around(north[:, cols - HALO :], -1)
+    north_left = around(north[:, :HALO], 1, 2)
+    north_right = around(north[:, cols - HALO :], -1, 2)
+    y1_mid, y2_mid, e1, e2 = fold_call(own, north, x1_tail, land, land_north, *weights)
     return north_call(
-        left, own, right, north, north_left, north_right, x1_tail, x2_tail, out_south, land, land_north, mask, *weights
+        left, own, right, north, north_left, north_right, x1_tail, x2_tail, out_south, y1_mid, y2_mid, e1, e2, mask, *weights
     )
 
 

time: 38 us -> 36 us (0.947)
  waiting for transfers between devices: 6.92 us -> 0.97 us
  Pallas kernels: 19.3 us -> 23.2 us
    ppermute x4, waiting for transfers between devices: 6.92 us -> 0.97 us  [around(): return lax.ppermute(value, 'lon', pairs)]
    pallas_call x5 -> x6, Pallas kernels: 19.3 us -> 23.2 us  [call(): pl.pallas_call(kernel, name=name, out_shape=tuple((jax.ShapeDtypeStruct(*...]
  transfers between devices with their start and end apart: 5 -> 5, of which waited for: 2 -> 1; matrix products, arithmetic and copies ran while one was open for 0% -> 0% of each run, Pallas kernels for 32% -> 45%
where the time goes in v4:
time: 36 us; the launch traced here: 35.8 us
  Pallas kernels  23.2 us (64%)
  starting transfers between devices  10.2 us (28%)
  local copies, waits for them, and re-layouts  1.22 us (3%)
  waiting for transfers between devices  0.97 us (3%)
    pallas_call x6, Pallas kernels, call(): pl.pallas_call(kernel, name=name, out_shape=tuple((jax.ShapeDtypeStruct(*...  23.2 us
    ppermute x4, starting transfers between devices, around(): return lax.ppermute(value, 'lon', pairs)  8.73 us
    ppermute x1, starting transfers between devices, per_device(): north = lax.ppermute(top, 'lon', [(i, count - 1 - i) for i in range(count)])  1.52 us
    unnamed x10, local copies, waits for them, and re-layouts  1.21 us
    ppermute x4, waiting for transfers between devices, around(): return lax.ppermute(value, 'lon', pairs)  0.97 us
  transfers between devices with their start and end apart: 5, of which 1 were waited for; matrix products, arithmetic and copies ran while one was open for 0% of the time, Pallas kernels for 45%

profile of v4, /device:TPU:0, one launch (start us, length us, event | category | flops | bytes accessed | tf_op | source)
XLA Modules:
  0.0 35.8 jit_solution(5717772486091411302)
XLA Ops:
  0.0 0.0 copy-start.2
  0.0 0.0 copy-start.1
  0.0 0.0 copy-start
  0.0 0.0 copy-start.3
  0.0 1.2 %copy-done.3 = bf16[32,32,256]{2,1,0:T(8,128)(2,1)S(1)} copy-done((bf16[32,32,256]{2,1,0:T(8,128)(2,1)S(1)}, bf16[32,32,256]{2,1,0:T(8,128)(2,1)}, u32[]{:S(2)}) %copy-start.3) | copy-done | bytes 524312
  1.2 0.0 copy-start.4
  1.2 0.4 %edges.1 = (bf16[32,16,256]{2,1,0:T(8,128)(2,1)S(1)}, bf16[32,16,256]{2,1,0:T(8,128)(2,1)S(1)}, bf16[14,32,256]{2,1,0:T(8,128)(2,1)S(1)}) custom-call(bf16[32,32,256]{2,1,0:T(8,128)(2,1)S(1)} %copy-done.3), custom_call_target="tpu_custom_call" | custom-call | flops 4563402752 | bytes 1048576 | tf_op jit(solution)/shard_map/edges/pallas_call | solution.py:270
  1.6 0.5 %collective-permute-start = (bf16[32,16,256]{2,1,0:T(8,128)(2,1)S(1)}, bf16[32,16,256]{2,1,0:T(8,128)(2,1)S(1)}, u32[]{:S(2)}, u32[]{:S(2)}) collective-permute-start(bf16[32,16,256]{2,1,0:T(8,128)(2,1)S(1)} %get-tuple-element.23), channel_id=1, source_target_pairs={{0,1},{1,2},{2,3},{3,4},{4,5},{5,6},{6,7},{7,8},{8,9},{9,10},{10,1... | collective-permute-start | bytes 786440 | tf_op jit(solution)/shard_map/ppermute | solution.py:344
  2.1 5.1 %collective-permute-start.1 = (bf16[32,16,256]{2,1,0:T(8,128)(2,1)S(1)}, bf16[32,16,256]{2,1,0:T(8,128)(2,1)S(1)}, u32[]{:S(2)}, u32[]{:S(2)}) collective-permute-start(bf16[32,16,256]{2,1,0:T(8,128)(2,1)S(1)} %get-tuple-element.24), channel_id=1, source_target_pairs={{0,15},{1,0},{2,1},{3,2},{4,3},{5,4},{6,5},{7,6},{8,7},{9,8},{10,9... | collective-permute-start | bytes 786440 | tf_op jit(solution)/shard_map/ppermute | solution.py:344
  7.1 0.0 copy-done.2
  7.1 0.0 copy-done.1
  7.1 0.0 copy-done
  7.1 0.0 copy-done.4
  7.1 3.2 %first.1 = (bf16[960,256]{1,0:T(8,128)(2,1)S(1)}, bf16[1024,128]{1,0:T(8,128)(2,1)S(1)}, f32[32,64]{1,0:T(8,128)S(1)}, f32[14,64]{1,0:T(8,128)S(1)}) custom-call(bf16[32,32,256]{2,1,0:T(8,128)(2,1)S(1)} %copy-done.3, s32[32,512]{1,0:T(8,128)S(1)} %copy-done.4, bf16[3,9,256,256]{3,2,1,0:T(8,128)(2,1)S(1)} %copy-done, bf16[3,256,1024]{2,1,0:T(8,128)(2,1)S(1)} %copy-done.1, ...), custom_call_target="tpu_custom_call" | custom-call | flops 2139095040 | bytes 1048576 | tf_op jit(solution)/shard_map/first/pallas_call | solution.py:270
  10.3 1.5 %collective-permute-start.2 = (bf16[14,32,256]{2,1,0:T(8,128)(2,1)S(1)}, bf16[14,32,256]{2,1,0:T(8,128)(2,1)S(1)}, u32[]{:S(2)}, u32[]{:S(2)}) collective-permute-start(bf16[14,32,256]{2,1,0:T(8,128)(2,1)S(1)} %get-tuple-element.27), channel_id=1, source_target_pairs={{0,15},{1,14},{2,13},{3,12},{4,11},{5,10},{6,9},{7,8},{8,7},{9,6},... | collective-permute-start | bytes 688136 | tf_op jit(solution)/shard_map/ppermute | solution.py:356
  11.9 2.4 %second.1.x2_mid = bf16[832,256]{1,0:T(8,128)(2,1)S(1)} custom-call(bf16[960,256]{1,0:T(8,128)(2,1)S(1)} %get-tuple-element.28.x1.x1_mid, bf16[1024,128]{1,0:T(8,128)(2,1)S(1)} %get-tuple-element.29.mask, bf16[3,9,256,256]{3,2,1,0:T(8,128)(2,1)S(1)} %copy-done, bf16[3,256,1024]{2,1,0:T(8,128)(2,1)S(1)} %copy-done.1, bf16[3,1024,256]{2,1,0:T(8,128)(2,1)S(1)} %copy-done.2), custom_call_target="tpu_custom_call" | custom-call | flops 1853882368 | bytes 1048576 | tf_op jit(solution)/shard_map/second/pallas_call | solution.py:270
  14.2 0.0 collective-permute-done.left
  14.2 0.0 collective-permute-done.1.right
  14.3 6.6 %south.1 = (bf16[448,256]{1,0:T(8,128)(2,1)S(1)}, bf16[768,256]{1,0:T(8,128)(2,1)S(1)}, bf16[18,32,256]{2,1,0:T(8,128)(2,1)S(1)}) custom-call(bf16[32,16,256]{2,1,0:T(8,128)(2,1)S(1)} %collective-permute-done.left, bf16[32,32,256]{2,1,0:T(8,128)(2,1)S(1)} %copy-done.3, bf16[32,16,256]{2,1,0:T(8,128)(2,1)S(1)} %collective-permute-done.1.right, ...), custom_call_target="tpu_custom_call" | custom-call | flops 5276434432 | bytes 1048576 | tf_op jit(solution)/shard_map/south/pallas_call | solution.py:270
  20.9 0.0 collective-permute-done.2.north
  20.9 3.2 %collective-permute-start.4 = (bf16[14,16,256]{2,1,0:T(8,128)(2,1)S(1)}, bf16[14,16,256]{2,1,0:T(8,128)(2,1)S(1)}, u32[]{:S(2)}, u32[]{:S(2)}) collective-permute-start(bf16[14,16,256]{2,1,0:T(8,128)(2,1)S(1)} %get-tuple-element.41), channel_id=1, source_target_pairs={{0,7},{1,0},{2,1},{3,2},{4,3},{5,4},{6,5},{7,6},{8,15},{9,8},{10,9... | collective-permute-start | bytes 344072 | tf_op jit(solution)/shard_map/ppermute | solution.py:344
  24.1 0.0 collective-permute-start.3
  24.1 4.1 %fold.1 = (bf16[448,256]{1,0:T(8,128)(2,1)S(1)}, bf16[448,256]{1,0:T(8,128)(2,1)S(1)}, bf16[448,128]{1,0:T(8,128)(2,1)S(1)}, bf16[448,128]{1,0:T(8,128)(2,1)S(1)}) custom-call(bf16[32,32,256]{2,1,0:T(8,128)(2,1)S(1)} %copy-done.3, bf16[14,32,256]{2,1,0:T(8,128)(2,1)S(1)} %collective-permute-done.2.north, bf16[448,256]{1,0:T(8,128)(2,1)S(1)} %get-tuple-element.33.x1_tail, ...), custom_call_target="tpu_custom_call" | custom-call | flops 1996488704 | bytes 1048576 | tf_op jit(solution)/shard_map/fold/pallas_call | solution.py:270
  28.2 0.0 collective-permute-done.4.north_right
  28.2 1.0 %collective-permute-done.3.north_left = bf16[14,16,256]{2,1,0:T(8,128)(2,1)S(1)} collective-permute-done((bf16[14,16,256]{2,1,0:T(8,128)(2,1)S(1)}, bf16[14,16,256]{2,1,0:T(8,128)(2,1)S(1)}, u32[]{:S(2)}, u32[]{:S(2)}) %collective-permute-start.3) | collective-permute-done | bytes 114720 | tf_op jit(solution)/shard_map/ppermute | solution.py:344
  29.2 6.5 %north.1 = bf16[32,32,256]{2,1,0:T(8,128)(2,1)} custom-call(bf16[32,16,256]{2,1,0:T(8,128)(2,1)S(1)} %collective-permute-done.left, bf16[32,32,256]{2,1,0:T(8,128)(2,1)S(1)} %copy-done.3, bf16[32,16,256]{2,1,0:T(8,128)(2,1)S(1)} %collective-permute-done.1.right, bf16[14,32,256]{2,1,0:T(8,128)(2,1)S(1)} %collective-permute-done.2.north, ...), custom_call_target="tpu_custom_call" | custom-call | flops 2994733056 | bytes 1048576 | tf_op jit(solution)/shard_map/north/pallas_call | solution.py:270
  (1 shorter events, 0.0 us)
Async XLA Ops:
  0.0 7.1 %copy-start.2 = (bf16[3,1024,256]{2,1,0:T(8,128)(2,1)S(1)}, bf16[3,1024,256]{2,1,0:T(8,128)(2,1)}, u32[]{:S(2)}) copy-start(bf16[3,1024,256]{2,1,0:T(8,128)(2,1)} %down.9) | copy-start | bytes 4718596
  0.0 7.1 %copy-start.1 = (bf16[3,256,1024]{2,1,0:T(8,128)(2,1)S(1)}, bf16[3,256,1024]{2,1,0:T(8,128)(2,1)}, u32[]{:S(2)}) copy-start(bf16[3,256,1024]{2,1,0:T(8,128)(2,1)} %up.9) | copy-start | bytes 4718596
  0.0 7.1 %copy-start = (bf16[3,9,256,256]{3,2,1,0:T(8,128)(2,1)S(1)}, bf16[3,9,256,256]{3,2,1,0:T(8,128)(2,1)}, u32[]{:S(2)}) copy-start(bf16[3,9,256,256]{3,2,1,0:T(8,128)(2,1)} %w.9) | copy-start | bytes 10616836
  0.0 1.2 %copy-start.3 = (bf16[32,32,256]{2,1,0:T(8,128)(2,1)S(1)}, bf16[32,32,256]{2,1,0:T(8,128)(2,1)}, u32[]{:S(2)}) copy-start(bf16[32,32,256]{2,1,0:T(8,128)(2,1)} %own.9) | copy-start | bytes 1572868
  1.2 5.9 %copy-start.4 = (s32[32,512]{1,0:T(8,128)S(1)}, s32[32,512]{1,0:T(8,128)}, u32[]{:S(2)}) copy-start(s32[32,512]{1,0:T(8,128)} %land_sea.1) | copy-start | bytes 196612
  1.6 12.7 %collective-permute-start = (bf16[32,16,256]{2,1,0:T(8,128)(2,1)S(1)}, bf16[32,16,256]{2,1,0:T(8,128)(2,1)S(1)}, u32[]{:S(2)}, u32[]{:S(2)}) collective-permute-start(bf16[32,16,256]{2,1,0:T(8,128)(2,1)S(1)} %get-tuple-element.23), channel_id=1, source_target_pairs={{0,1},{1,2},{2,3},{3,4},{4,5},{5,6},{6,7},{7,8},{8,9},{9,10},{10,1... | collective-permute-start | bytes 786440 | tf_op jit(solution)/shard_map/ppermute | solution.py:344
  2.1 12.2 %collective-permute-start.1 = (bf16[32,16,256]{2,1,0:T(8,128)(2,1)S(1)}, bf16[32,16,256]{2,1,0:T(8,128)(2,1)S(1)}, u32[]{:S(2)}, u32[]{:S(2)}) collective-permute-start(bf16[32,16,256]{2,1,0:T(8,128)(2,1)S(1)} %get-tuple-element.24), channel_id=1, source_target_pairs={{0,15},{1,0},{2,1},{3,2},{4,3},{5,4},{6,5},{7,6},{8,7},{9,8},{10,9... | collective-permute-start | bytes 786440 | tf_op jit(solution)/shard_map/ppermute | solution.py:344
  10.3 10.5 %collective-permute-start.2 = (bf16[14,32,256]{2,1,0:T(8,128)(2,1)S(1)}, bf16[14,32,256]{2,1,0:T(8,128)(2,1)S(1)}, u32[]{:S(2)}, u32[]{:S(2)}) collective-permute-start(bf16[14,32,256]{2,1,0:T(8,128)(2,1)S(1)} %get-tuple-element.27), channel_id=1, source_target_pairs={{0,15},{1,14},{2,13},{3,12},{4,11},{5,10},{6,9},{7,8},{8,7},{9,6},... | collective-permute-start | bytes 688136 | tf_op jit(solution)/shard_map/ppermute | solution.py:356
  20.9 7.3 %collective-permute-start.4 = (bf16[14,16,256]{2,1,0:T(8,128)(2,1)S(1)}, bf16[14,16,256]{2,1,0:T(8,128)(2,1)S(1)}, u32[]{:S(2)}, u32[]{:S(2)}) collective-permute-start(bf16[14,16,256]{2,1,0:T(8,128)(2,1)S(1)} %get-tuple-element.41), channel_id=1, source_target_pairs={{0,7},{1,0},{2,1},{3,2},{4,3},{5,4},{6,5},{7,6},{8,15},{9,8},{10,9... | collective-permute-start | bytes 344072 | tf_op jit(solution)/shard_map/ppermute | solution.py:344
  24.1 5.1 %collective-permute-start.3 = (bf16[14,16,256]{2,1,0:T(8,128)(2,1)S(1)}, bf16[14,16,256]{2,1,0:T(8,128)(2,1)S(1)}, u32[]{:S(2)}, u32[]{:S(2)}) collective-permute-start(bf16[14,16,256]{2,1,0:T(8,128)(2,1)S(1)} %get-tuple-element.42), channel_id=1, source_target_pairs={{0,1},{1,2},{2,3},{3,4},{4,5},{5,6},{6,7},{7,0},{8,9},{9,10},{10,1... | collective-permute-start | bytes 344072 | tf_op jit(solution)/shard_map/ppermute | solution.py:344

commit v5 on v4

--- a/solution.py
+++ b/solution.py
@@ -114,28 +114,29 @@
     return jnp.concatenate([left[row], own[row], right[row]], axis=0)
 
 
-def first_kernel(own, land_sea, w, up, down, x1, mask, land, land_north, sh1, nrm):
+def first_kernel(own, land_sea, w, up, down, x1, mask, land, land_north, sh1, nrm, m1):
     me = lax.axis_index("lon")
     whole = land_sea[...].astype(F32).astype(BF)
     land[...] = window(whole, me * 32 - HALO)
     land_north[...] = window(whole, (lax.axis_size("lon") - 1 - me) * 32 - HALO)[32 - DEEP :]
-    mask[...] = spread_mask(land, 0, 32, False)[:, 16:48].reshape(32 * 32, 128)
-    clear(sh1, 2 * 32)
-    edge = jnp.zeros((HALO, own.shape[-1]), BF)
+    cells = spread_mask(land, 0, 32, False)
+    mask[...] = cells[:, 16:48].reshape(32 * 32, 128)
+    m1[...] = cells[:30, 20:44].reshape(30 * 24, 128)
+    clear(sh1, 2 * 24)
     for row in range(32):
-        spread(sh1, (row + 2) * 32, jnp.concatenate([edge, own[row], edge], axis=0), [16], 32, 2)
-    conv_norm(0, sh1, 32, -2, [(0, 15, False), (15, 15, False)], w, nrm)
-    mlp(0, sh1, 32, -2, 0, [15, 15], up, down, mask, nrm, keep(x1, 32, 0))
-
-
-def second_kernel(x1, mask, w, up, down, x2, sh2, nrm):
-    clear(sh2, 4 * 32)
-    edge = jnp.zeros((HALO, x1.shape[-1]), BF)
+        spread(sh1, (row + 2) * 24, own[row], [4], 24, 2)
+    conv_norm(0, sh1, 24, -2, [(0, 8, False), (8, 8, False), (16, 8, False), (24, 6, False)], w, nrm)
+    mlp(0, sh1, 24, -2, 0, [16, 14], up, down, m1, nrm, keep(x1, 24, 0))
+
+
+def second_kernel(x1, mask, w, up, down, x2, sh2, nrm, m2):
+    for row in range(26):
+        m2[row * 16 : (row + 1) * 16] = mask[row * 32 + 8 : row * 32 + 24]
+    clear(sh2, 4 * 16)
     for row in range(30):
-        values = jnp.concatenate([edge, x1[row * 32 : (row + 1) * 32], edge], axis=0)
-        spread(sh2, (row + 4) * 32, values, [16], 32, 4)
-    conv_norm(1, sh2, 32, -4, [(0, 13, False), (13, 13, False)], w, nrm)
-    mlp(1, sh2, 32, -4, 0, [13, 13], up, down, mask, nrm, keep(x2, 32, 0))
+        spread(sh2, (row + 4) * 16, x1[row * 24 : (row + 1) * 24], [4], 16, 4)
+    conv_norm(1, sh2, 16, -4, [(0, 13, False), (13, 13, False)], w, nrm)
+    mlp(1, sh2, 16, -4, 0, [26], up, down, m2, nrm, keep(x2, 16, 0))
 
 
 def south_kernel(
@@ -150,27 +151,27 @@
     cells = spread_mask(land, 0, 30, False)
     e1[...] = jnp.concatenate([cells[:, 4:20], cells[:, 44:60]], axis=1).reshape(30 * 32, 128)
     e2[...] = jnp.concatenate([cells[:26, 8:24], cells[:26, 40:56]], axis=1).reshape(26 * 32, 128)
-    conv_norm(0, sh1, 32, -2, [(0, 15, False), (15, 15, False)], w, nrm)
+    conv_norm(0, sh1, 32, -2, [(0, 8, False), (8, 8, False), (16, 7, False), (23, 7, False)], w, nrm)
     mlp(0, sh1, 32, -2, 0, [15, 15], up, down, e1, nrm, keep(x1, 32, 0))
 
     def row1(row):
         at = row * 32
-        return jnp.concatenate([x1[at : at + 16], x1_mid[at + 4 : at + 28], x1[at + 16 : at + 32]], axis=0)
+        return jnp.concatenate([x1[at : at + 16], x1_mid[row * 24 : (row + 1) * 24], x1[at + 16 : at + 32]], axis=0)
 
     for row in range(30):
         values = row1(row)
         if row >= 22:
             x1_tail[(row - 22) * 56 : (row - 21) * 56] = values
         spread(sh2, (row + 4) * 32, values, [4, 36], 16, 4)
-    conv_norm(1, sh2, 32, -4, [(0, 13, False), (13, 13, False)], w, nrm)
+    conv_norm(1, sh2, 32, -4, [(0, 7, False), (7, 7, False), (14, 6, False), (20, 6, False)], w, nrm)
     mlp(1, sh2, 32, -4, 0, [13, 13], up, down, e2, nrm, keep(x2, 32, 0))
     for row in range(26):
         at = row * 32
-        values = jnp.concatenate([x2[at : at + 16], x2_mid[at + 8 : at + 24], x2[at + 16 : at + 32]], axis=0)
+        values = jnp.concatenate([x2[at : at + 16], x2_mid[row * 16 : (row + 1) * 16], x2[at + 16 : at + 32]], axis=0)
         if row >= 10:
             x2_tail[(row - 10) * 48 : (row - 9) * 48] = values
         spread(sh3, (row + 8) * 32, values, [8], 32, 8)
-    conv_norm(2, sh3, 32, -8, [(0, 9, False), (9, 9, False)], w, nrm)
+    conv_norm(2, sh3, 32, -8, [(0, 6, False), (6, 6, False), (12, 6, False)], w, nrm)
 
     def store3(row, count, value):
         out[row : row + count] = value.reshape(count, 32, 256)
@@ -187,27 +188,25 @@
     near = spread_mask(land, 26, 6, False)
     far = spread_mask(land_north, 0, DEEP, True)
     cells = jnp.concatenate([near] + [far[45 - row : 46 - row] for row in range(32, 44)], axis=0)
-    m1[...] = cells[4:, 16:48].reshape(14 * 32, 128)
-    m2[...] = cells[:14, 16:48].reshape(14 * 32, 128)
+    m1[...] = cells[4:, 20:44].reshape(14 * 24, 128)
+    m2[...] = cells[:14, 24:40].reshape(14 * 16, 128)
     e1[...] = strips(cells[4:], 4, 44)
     e2[...] = strips(cells[:14], 8, 40)
     turn = jnp.where(diagonal(True, 32), 1.0, 0.0).astype(BF)
-    edge = jnp.zeros((HALO, own.shape[-1]), BF)
     for row in range(18):
         if row < 4:
             line = own[28 + row]
         else:
             line = jnp.dot(turn, north[17 - row], preferred_element_type=F32).astype(BF)
-        spread(sh1, row * 32, jnp.concatenate([edge, line, edge], axis=0), [16], 32, 2)
-    conv_norm(0, sh1, 32, 28, [(30, 2, False), (32, 12, True)], w, nrm)
-    mlp(0, sh1, 32, 28, 30, [7, 7], up, down, m1, nrm, keep(x1, 32, 30), 30)
+        spread(sh1, row * 24, line, [4], 24, 2)
+    conv_norm(0, sh1, 24, 28, [(30, 2, False), (32, 6, True), (38, 6, True)], w, nrm)
+    mlp(0, sh1, 24, 28, 30, [8, 6], up, down, m1, nrm, keep(x1, 24, 30), 30)
     for row in range(8):
-        spread(sh2, row * 32, x1_tail[row * 56 : (row + 1) * 56], [12], 32, 4)
+        spread(sh2, row * 16, x1_tail[row * 56 : (row + 1) * 56], [20], 16, 4)
     for row in range(14):
-        values = jnp.concatenate([edge, x1[row * 32 : (row + 1) * 32], edge], axis=0)
-        spread(sh2, (row + 8) * 32, values, [16], 32, 4)
-    conv_norm(1, sh2, 32, 22, [(26, 6, False), (32, 8, True)], w, nrm)
-    mlp(1, sh2, 32, 22, 26, [7, 7], up, down, m2, nrm, keep(x2, 32, 26), 26)
+        spread(sh2, (row + 8) * 16, x1[row * 24 : (row + 1) * 24], [4], 16, 4)
+    conv_norm(1, sh2, 16, 22, [(26, 6, False), (32, 8, True)], w, nrm)
+    mlp(1, sh2, 16, 22, 26, [7, 7], up, down, m2, nrm, keep(x2, 16, 26), 26)
 
 
 def north_kernel(
@@ -228,13 +227,13 @@
         source = jnp.concatenate([before, north[at], after], axis=0)
         turned = jnp.dot(turn, source, preferred_element_type=F32).astype(BF)
         spread(sh1, (row + 4) * 32, turned, [4, 44], 16, 2)
-    conv_norm(0, sh1, 32, 28, [(30, 2, False), (32, 12, True)], w, nrm)
+    conv_norm(0, sh1, 32, 28, [(30, 2, False), (32, 6, True), (38, 6, True)], w, nrm)
     mlp(0, sh1, 32, 28, 30, [7, 7], up, down, e1, nrm, keep(x1, 32, 30), 30)
     for row in range(8):
         spread(sh2, row * 32, x1_tail[row * 56 : (row + 1) * 56], [4, 36], 16, 4)
     for row in range(14):
         at = row * 32
-        values = jnp.concatenate([x1[at : at + 16], x1_mid[at + 4 : at + 28], x1[at + 16 : at + 32]], axis=0)
+        values = jnp.concatenate([x1[at : at + 16], x1_mid[row * 24 : (row + 1) * 24], x1[at + 16 : at + 32]], axis=0)
         spread(sh2, (row + 8) * 32, values, [4, 36], 16, 4)
     conv_norm(1, sh2, 32, 22, [(26, 6, False), (32, 8, True)], w, nrm)
     mlp(1, sh2, 32, 22, 26, [7, 7], up, down, e2, nrm, keep(x2, 32, 26), 26)
@@ -242,18 +241,23 @@
         spread(sh3, row * 32, x2_tail[row * 48 : (row + 1) * 48], [8], 32, 8)
     for row in range(14):
         at = row * 32
-        values = jnp.concatenate([x2[at : at + 16], x2_mid[at + 8 : at + 24], x2[at + 16 : at + 32]], axis=0)
+        values = jnp.concatenate([x2[at : at + 16], x2_mid[row * 16 : (row + 1) * 16], x2[at + 16 : at + 32]], axis=0)
         spread(sh3, (row + 16) * 32, values, [8], 32, 8)
-    conv_norm(2, sh3, 32, 10, [(18, 14, False)], w, nrm)
+    conv_norm(2, sh3, 32, 10, [(18, 7, False), (25, 7, False)], w, nrm)
+
+    copies = [first]
 
     def store3(row, count, value):
         last[row - 18 : row - 18 + count] = value.reshape(count, 32, 256)
+        here = pltpu.make_async_copy(
+            last.at[row - 18 : row - 18 + count], out.at[row : row + count], sems.at[len(copies)]
+        )
+        here.start()
+        copies.append(here)
 
     mlp(2, sh3, 32, 10, 18, [7, 7], up, down, mask, nrm, store3)
-    second = pltpu.make_async_copy(last, out.at[18:32], sems.at[1])
-    second.start()
-    first.wait()
-    second.wait()
+    for copy in copies:
+        copy.wait()
 
 
 def cost(cells):
@@ -296,14 +300,16 @@
 
 def first_call(*args):
     return call(
-        first_kernel, "first", [(30 * 32, 256), (32 * 32, 128), ((32, 64), F32), ((DEEP, 64), F32)],
-        [VMEM] * len(args), [VMEM] * 4, [taps(34, 32), flat(30, 32)], 960, args,
+        first_kernel, "first", [(30 * 24, 256), (32 * 32, 128), ((32, 64), F32), ((DEEP, 64), F32)],
+        [VMEM] * len(args), [VMEM] * 4,
+        [taps(34, 24), flat(30, 24), pltpu.VMEM((30 * 24, 128), BF)], 720, args,
     )
 
 
 def second_call(*args):
     (x2,) = call(
-        second_kernel, "second", [(26 * 32, 256)], [VMEM] * len(args), [VMEM], [taps(34, 32), flat(26, 32)], 832, args
+        second_kernel, "second", [(26 * 16, 256)], [VMEM] * len(args), [VMEM],
+        [taps(34, 16), flat(26, 16), pltpu.VMEM((26 * 16, 128), BF)], 416, args,
     )
     return x2
 
@@ -319,10 +325,10 @@
 
 def fold_call(*args):
     return call(
-        fold_kernel, "fold", [(14 * 32, 256), (14 * 32, 256), (14 * 32, 128), (14 * 32, 128)],
+        fold_kernel, "fold", [(14 * 24, 256), (14 * 16, 256), (14 * 32, 128), (14 * 32, 128)],
         [VMEM] * len(args), [VMEM] * 4,
-        [taps(18, 32), taps(22, 32), flat(14, 32), pltpu.VMEM((14 * 32, 128), BF), pltpu.VMEM((14 * 32, 128), BF)],
-        896, args,
+        [taps(18, 24), taps(22, 16), flat(14, 24), pltpu.VMEM((14 * 24, 128), BF), pltpu.VMEM((14 * 16, 128), BF)],
+        560, args,
     )
 
 
@@ -331,7 +337,7 @@
         north_kernel, "north", [(32, 32, 256)], [VMEM] * len(args), [HBM],
         [
             taps(18, 32), taps(22, 32), taps(30, 32), flat(14, 32), flat(14, 32), flat(14, 32),
-            pltpu.VMEM((14, 32, 256), BF), pltpu.SemaphoreType.DMA((2,)),
+            pltpu.VMEM((14, 32, 256), BF), pltpu.SemaphoreType.DMA((3,)),
         ],
         1344, args,
     )

time: 36 us -> 34.3 us (0.953)
  Pallas kernels: 23.2 us -> 18.9 us
  waiting for transfers between devices: 0.97 us -> 2.44 us
  starting transfers between devices: 10.2 us -> 11.4 us
    pallas_call x6, Pallas kernels: 23.2 us -> 18.9 us  [call(): pl.pallas_call(kernel, name=name, out_shape=tuple((jax.ShapeDtypeStruct(*...]
    ppermute x4, waiting for transfers between devices: 0.97 us -> 2.44 us  [around(): return lax.ppermute(value, 'lon', pairs)]
    ppermute x4, starting transfers between devices: 8.73 us -> 9.89 us  [around(): return lax.ppermute(value, 'lon', pairs)]
  transfers between devices with their start and end apart: 5 -> 5, of which waited for: 1 -> 1; matrix products, arithmetic and copies ran while one was open for 0% -> 0% of each run, Pallas kernels for 45% -> 38%
where the time goes in v5:
time: 34.3 us; the launch traced here: 34.2 us
  Pallas kernels  18.9 us (55%)
  starting transfers between devices  11.4 us (33%)
  waiting for transfers between devices  2.44 us (7%)
  local copies, waits for them, and re-layouts  1.22 us (4%)
    pallas_call x6, Pallas kernels, call(): pl.pallas_call(kernel, name=name, out_shape=tuple((jax.ShapeDtypeStruct(*...  18.9 us
    ppermute x4, starting transfers between devices, around(): return lax.ppermute(value, 'lon', pairs)  9.89 us
    ppermute x4, waiting for transfers between devices, around(): return lax.ppermute(value, 'lon', pairs)  2.44 us
    ppermute x1, starting transfers between devices, per_device(): north = lax.ppermute(top, 'lon', [(i, count - 1 - i) for i in range(count)])  1.53 us
    unnamed x10, local copies, waits for them, and re-layouts  1.21 us
  transfers between devices with their start and end apart: 5, of which 1 were waited for; matrix products, arithmetic and copies ran while one was open for 0% of the time, Pallas kernels for 38%

profile of v5, /device:TPU:0, one launch (start us, length us, event | category | flops | bytes accessed | tf_op | source)
XLA Modules:
  0.0 34.2 jit_solution(16428980757274740469)
XLA Ops:
  0.0 0.0 copy-start.2
  0.0 0.0 copy-start.1
  0.0 0.0 copy-start
  0.0 0.0 copy-start.3
  0.0 1.2 %copy-done.3 = bf16[32,32,256]{2,1,0:T(8,128)(2,1)S(1)} copy-done((bf16[32,32,256]{2,1,0:T(8,128)(2,1)S(1)}, bf16[32,32,256]{2,1,0:T(8,128)(2,1)}, u32[]{:S(2)}) %copy-start.3) | copy-done | bytes 524312
  1.2 0.0 copy-start.4
  1.2 0.4 %edges.1 = (bf16[32,16,256]{2,1,0:T(8,128)(2,1)S(1)}, bf16[32,16,256]{2,1,0:T(8,128)(2,1)S(1)}, bf16[14,32,256]{2,1,0:T(8,128)(2,1)S(1)}) custom-call(bf16[32,32,256]{2,1,0:T(8,128)(2,1)S(1)} %copy-done.3), custom_call_target="tpu_custom_call" | custom-call | flops 4563402752 | bytes 1048576 | tf_op jit(solution)/shard_map/edges/pallas_call | solution.py:274
  1.6 0.5 %collective-permute-start = (bf16[32,16,256]{2,1,0:T(8,128)(2,1)S(1)}, bf16[32,16,256]{2,1,0:T(8,128)(2,1)S(1)}, u32[]{:S(2)}, u32[]{:S(2)}) collective-permute-start(bf16[32,16,256]{2,1,0:T(8,128)(2,1)S(1)} %get-tuple-element.23), channel_id=1, source_target_pairs={{0,1},{1,2},{2,3},{3,4},{4,5},{5,6},{6,7},{7,8},{8,9},{9,10},{10,1... | collective-permute-start | bytes 786440 | tf_op jit(solution)/shard_map/ppermute | solution.py:350
  2.1 5.1 %collective-permute-start.1 = (bf16[32,16,256]{2,1,0:T(8,128)(2,1)S(1)}, bf16[32,16,256]{2,1,0:T(8,128)(2,1)S(1)}, u32[]{:S(2)}, u32[]{:S(2)}) collective-permute-start(bf16[32,16,256]{2,1,0:T(8,128)(2,1)S(1)} %get-tuple-element.24), channel_id=1, source_target_pairs={{0,15},{1,0},{2,1},{3,2},{4,3},{5,4},{6,5},{7,6},{8,7},{9,8},{10,9... | collective-permute-start | bytes 786440 | tf_op jit(solution)/shard_map/ppermute | solution.py:350
  7.1 0.0 copy-done.2
  7.1 0.0 copy-done.1
  7.1 0.0 copy-done
  7.1 0.0 copy-done.4
  7.1 2.4 %first.1 = (bf16[720,256]{1,0:T(8,128)(2,1)S(1)}, bf16[1024,128]{1,0:T(8,128)(2,1)S(1)}, f32[32,64]{1,0:T(8,128)S(1)}, f32[14,64]{1,0:T(8,128)S(1)}) custom-call(bf16[32,32,256]{2,1,0:T(8,128)(2,1)S(1)} %copy-done.3, s32[32,512]{1,0:T(8,128)S(1)} %copy-done.4, bf16[3,9,256,256]{3,2,1,0:T(8,128)(2,1)S(1)} %copy-done, bf16[3,256,1024]{2,1,0:T(8,128)(2,1)S(1)} %copy-done.1, ...), custom_call_target="tpu_custom_call" | custom-call | flops 1604321280 | bytes 1048576 | tf_op jit(solution)/shard_map/first/pallas_call | solution.py:274
  9.6 1.5 %collective-permute-start.2 = (bf16[14,32,256]{2,1,0:T(8,128)(2,1)S(1)}, bf16[14,32,256]{2,1,0:T(8,128)(2,1)S(1)}, u32[]{:S(2)}, u32[]{:S(2)}) collective-permute-start(bf16[14,32,256]{2,1,0:T(8,128)(2,1)S(1)} %get-tuple-element.27), channel_id=1, source_target_pairs={{0,15},{1,14},{2,13},{3,12},{4,11},{5,10},{6,9},{7,8},{8,7},{9,6},... | collective-permute-start | bytes 688136 | tf_op jit(solution)/shard_map/ppermute | solution.py:362
  11.1 1.6 %second.1.x2_mid = bf16[416,256]{1,0:T(8,128)(2,1)S(1)} custom-call(bf16[720,256]{1,0:T(8,128)(2,1)S(1)} %get-tuple-element.28.x1.x1_mid, bf16[1024,128]{1,0:T(8,128)(2,1)S(1)} %get-tuple-element.29.mask, bf16[3,9,256,256]{3,2,1,0:T(8,128)(2,1)S(1)} %copy-done, bf16[3,256,1024]{2,1,0:T(8,128)(2,1)S(1)} %copy-done.1, bf16[3,1024,256]{2,1,0:T(8,128)(2,1)S(1)} %copy-done.2), custom_call_target="tpu_custom_call" | custom-call | flops 926941184 | bytes 1048576 | tf_op jit(solution)/shard_map/second/pallas_call | solution.py:274
  12.7 0.0 collective-permute-done.left
  12.7 0.0 collective-permute-done.1.right
  12.7 6.4 %south.1 = (bf16[448,256]{1,0:T(8,128)(2,1)S(1)}, bf16[768,256]{1,0:T(8,128)(2,1)S(1)}, bf16[18,32,256]{2,1,0:T(8,128)(2,1)S(1)}) custom-call(bf16[32,16,256]{2,1,0:T(8,128)(2,1)S(1)} %collective-permute-done.left, bf16[32,32,256]{2,1,0:T(8,128)(2,1)S(1)} %copy-done.3, bf16[32,16,256]{2,1,0:T(8,128)(2,1)S(1)} %collective-permute-done.1.right, ...), custom_call_target="tpu_custom_call" | custom-call | flops 5276434432 | bytes 1048576 | tf_op jit(solution)/shard_map/south/pallas_call | solution.py:274
  19.1 0.0 collective-permute-done.2.north
  19.2 4.3 %collective-permute-start.4 = (bf16[14,16,256]{2,1,0:T(8,128)(2,1)S(1)}, bf16[14,16,256]{2,1,0:T(8,128)(2,1)S(1)}, u32[]{:S(2)}, u32[]{:S(2)}) collective-permute-start(bf16[14,16,256]{2,1,0:T(8,128)(2,1)S(1)} %get-tuple-element.41), channel_id=1, source_target_pairs={{0,7},{1,0},{2,1},{3,2},{4,3},{5,4},{6,5},{7,6},{8,15},{9,8},{10,9... | collective-permute-start | bytes 344072 | tf_op jit(solution)/shard_map/ppermute | solution.py:350
  23.5 0.0 collective-permute-start.3
  23.5 2.7 %fold.1 = (bf16[336,256]{1,0:T(8,128)(2,1)S(1)}, bf16[224,256]{1,0:T(8,128)(2,1)S(1)}, bf16[448,128]{1,0:T(8,128)(2,1)S(1)}, bf16[448,128]{1,0:T(8,128)(2,1)S(1)}) custom-call(bf16[32,32,256]{2,1,0:T(8,128)(2,1)S(1)} %copy-done.3, bf16[14,32,256]{2,1,0:T(8,128)(2,1)S(1)} %collective-permute-done.2.north, bf16[448,256]{1,0:T(8,128)(2,1)S(1)} %get-tuple-element.33.x1_tail, ...), custom_call_target="tpu_custom_call" | custom-call | flops 1247805440 | bytes 1048576 | tf_op jit(solution)/shard_map/fold/pallas_call | solution.py:274
  26.2 0.0 collective-permute-done.4.north_right
  26.2 2.4 %collective-permute-done.3.north_left = bf16[14,16,256]{2,1,0:T(8,128)(2,1)S(1)} collective-permute-done((bf16[14,16,256]{2,1,0:T(8,128)(2,1)S(1)}, bf16[14,16,256]{2,1,0:T(8,128)(2,1)S(1)}, u32[]{:S(2)}, u32[]{:S(2)}) %collective-permute-start.3) | collective-permute-done | bytes 114720 | tf_op jit(solution)/shard_map/ppermute | solution.py:350
  28.6 5.4 %north.1 = bf16[32,32,256]{2,1,0:T(8,128)(2,1)} custom-call(bf16[32,16,256]{2,1,0:T(8,128)(2,1)S(1)} %collective-permute-done.left, bf16[32,32,256]{2,1,0:T(8,128)(2,1)S(1)} %copy-done.3, bf16[32,16,256]{2,1,0:T(8,128)(2,1)S(1)} %collective-permute-done.1.right, bf16[14,32,256]{2,1,0:T(8,128)(2,1)S(1)} %collective-permute-done.2.north, ...), custom_call_target="tpu_custom_call" | custom-call | flops 2994733056 | bytes 1048576 | tf_op jit(solution)/shard_map/north/pallas_call | solution.py:274
  (1 shorter events, 0.0 us)
Async XLA Ops:
  0.0 7.1 %copy-start.2 = (bf16[3,1024,256]{2,1,0:T(8,128)(2,1)S(1)}, bf16[3,1024,256]{2,1,0:T(8,128)(2,1)}, u32[]{:S(2)}) copy-start(bf16[3,1024,256]{2,1,0:T(8,128)(2,1)} %down.9) | copy-start | bytes 4718596
  0.0 7.1 %copy-start.1 = (bf16[3,256,1024]{2,1,0:T(8,128)(2,1)S(1)}, bf16[3,256,1024]{2,1,0:T(8,128)(2,1)}, u32[]{:S(2)}) copy-start(bf16[3,256,1024]{2,1,0:T(8,128)(2,1)} %up.9) | copy-start | bytes 4718596
  0.0 7.1 %copy-start = (bf16[3,9,256,256]{3,2,1,0:T(8,128)(2,1)S(1)}, bf16[3,9,256,256]{3,2,1,0:T(8,128)(2,1)}, u32[]{:S(2)}) copy-start(bf16[3,9,256,256]{3,2,1,0:T(8,128)(2,1)} %w.9) | copy-start | bytes 10616836
  0.0 1.2 %copy-start.3 = (bf16[32,32,256]{2,1,0:T(8,128)(2,1)S(1)}, bf16[32,32,256]{2,1,0:T(8,128)(2,1)}, u32[]{:S(2)}) copy-start(bf16[32,32,256]{2,1,0:T(8,128)(2,1)} %own.9) | copy-start | bytes 1572868
  1.2 5.9 %copy-start.4 = (s32[32,512]{1,0:T(8,128)S(1)}, s32[32,512]{1,0:T(8,128)}, u32[]{:S(2)}) copy-start(s32[32,512]{1,0:T(8,128)} %land_sea.1) | copy-start | bytes 196612
  1.6 11.1 %collective-permute-start = (bf16[32,16,256]{2,1,0:T(8,128)(2,1)S(1)}, bf16[32,16,256]{2,1,0:T(8,128)(2,1)S(1)}, u32[]{:S(2)}, u32[]{:S(2)}) collective-permute-start(bf16[32,16,256]{2,1,0:T(8,128)(2,1)S(1)} %get-tuple-element.23), channel_id=1, source_target_pairs={{0,1},{1,2},{2,3},{3,4},{4,5},{5,6},{6,7},{7,8},{8,9},{9,10},{10,1... | collective-permute-start | bytes 786440 | tf_op jit(solution)/shard_map/ppermute | solution.py:350
  2.1 10.6 %collective-permute-start.1 = (bf16[32,16,256]{2,1,0:T(8,128)(2,1)S(1)}, bf16[32,16,256]{2,1,0:T(8,128)(2,1)S(1)}, u32[]{:S(2)}, u32[]{:S(2)}) collective-permute-start(bf16[32,16,256]{2,1,0:T(8,128)(2,1)S(1)} %get-tuple-element.24), channel_id=1, source_target_pairs={{0,15},{1,0},{2,1},{3,2},{4,3},{5,4},{6,5},{7,6},{8,7},{9,8},{10,9... | collective-permute-start | bytes 786440 | tf_op jit(solution)/shard_map/ppermute | solution.py:350
  9.6 9.6 %collective-permute-start.2 = (bf16[14,32,256]{2,1,0:T(8,128)(2,1)S(1)}, bf16[14,32,256]{2,1,0:T(8,128)(2,1)S(1)}, u32[]{:S(2)}, u32[]{:S(2)}) collective-permute-start(bf16[14,32,256]{2,1,0:T(8,128)(2,1)S(1)} %get-tuple-element.27), channel_id=1, source_target_pairs={{0,15},{1,14},{2,13},{3,12},{4,11},{5,10},{6,9},{7,8},{8,7},{9,6},... | collective-permute-start | bytes 688136 | tf_op jit(solution)/shard_map/ppermute | solution.py:362
  19.2 7.0 %collective-permute-start.4 = (bf16[14,16,256]{2,1,0:T(8,128)(2,1)S(1)}, bf16[14,16,256]{2,1,0:T(8,128)(2,1)S(1)}, u32[]{:S(2)}, u32[]{:S(2)}) collective-permute-start(bf16[14,16,256]{2,1,0:T(8,128)(2,1)S(1)} %get-tuple-element.41), channel_id=1, source_target_pairs={{0,7},{1,0},{2,1},{3,2},{4,3},{5,4},{6,5},{7,6},{8,15},{9,8},{10,9... | collective-permute-start | bytes 344072 | tf_op jit(solution)/shard_map/ppermute | solution.py:350
  23.5 5.1 %collective-permute-start.3 = (bf16[14,16,256]{2,1,0:T(8,128)(2,1)S(1)}, bf16[14,16,256]{2,1,0:T(8,128)(2,1)S(1)}, u32[]{:S(2)}, u32[]{:S(2)}) collective-permute-start(bf16[14,16,256]{2,1,0:T(8,128)(2,1)S(1)} %get-tuple-element.42), channel_id=1, source_target_pairs={{0,1},{1,2},{2,3},{3,4},{4,5},{5,6},{6,7},{7,0},{8,9},{9,10},{10,1... | collective-permute-start | bytes 344072 | tf_op jit(solution)/shard_map/ppermute | solution.py:350

commit v6 on v5

--- a/solution.py
+++ b/solution.py
@@ -98,20 +98,31 @@
     return jnp.dot(whole, pick, preferred_element_type=F32)
 
 
-def edges_kernel(own, left, right, top, sems):
-    copies = [
-        pltpu.make_async_copy(own.at[:, 0:HALO], left, sems.at[0]),
-        pltpu.make_async_copy(own.at[:, 32 - HALO : 32], right, sems.at[1]),
-        pltpu.make_async_copy(own.at[32 - DEEP : 32], top, sems.at[2]),
-    ]
-    for copy in copies:
-        copy.start()
-    for copy in copies:
-        copy.wait()
-
-
-def wide(row, left, own, right):
-    return jnp.concatenate([left[row], own[row], right[row]], axis=0)
+def halves(value, inner, outer):
+    odd = lax.rem(lax.axis_index("lon"), 2) == 1
+    for row in range(value.shape[0]):
+        low, high = value[row, 0:HALO], value[row, 32 - HALO : 32]
+        inner[row] = jnp.where(odd, low, high)
+        outer[row] = jnp.where(odd, high, low)
+
+
+def edges_kernel(own, inner, outer, top):
+    halves(own, inner, outer)
+    top[...] = own[32 - DEEP : 32]
+
+
+def cut_kernel(north, inner, outer):
+    halves(north, outer, inner)
+
+
+def in_order(row, inner, outer):
+    odd = lax.rem(lax.axis_index("lon"), 2) == 1
+    return jnp.where(odd, inner[row], outer[row]), jnp.where(odd, outer[row], inner[row])
+
+
+def wide(row, inner, own, outer):
+    before, after = in_order(row, inner, outer)
+    return jnp.concatenate([before, own[row], after], axis=0)
 
 
 def first_kernel(own, land_sea, w, up, down, x1, mask, land, land_north, sh1, nrm, m1):
@@ -140,14 +151,14 @@
 
 
 def south_kernel(
-    left, own, right, x1_mid, x2_mid, land, mask, w, up, down,
+    inner, own, outer, x1_mid, x2_mid, land, mask, w, up, down,
     x1_tail, x2_tail, out, sh1, sh2, sh3, x1, x2, nrm, e1, e2,
 ):
     clear(sh1, 2 * 32)
     clear(sh2, 4 * 32)
     clear(sh3, 8 * 32)
     for row in range(32):
-        spread(sh1, (row + 2) * 32, wide(row, left, own, right), [4, 44], 16, 2)
+        spread(sh1, (row + 2) * 32, wide(row, inner, own, outer), [4, 44], 16, 2)
     cells = spread_mask(land, 0, 30, False)
     e1[...] = jnp.concatenate([cells[:, 4:20], cells[:, 44:60]], axis=1).reshape(30 * 32, 128)
     e2[...] = jnp.concatenate([cells[:26, 8:24], cells[:26, 40:56]], axis=1).reshape(26 * 32, 128)
@@ -210,7 +221,7 @@
 
 
 def north_kernel(
-    left, own, right, north, north_left, north_right, x1_tail, x2_tail, out_south, x1_mid, x2_mid,
+    inner, own, outer, north, north_inner, north_outer, x1_tail, x2_tail, out_south, x1_mid, x2_mid,
     e1, e2, mask, w, up, down, out, sh1, sh2, sh3, x1, x2, nrm, last, sems,
 ):
     first = pltpu.make_async_copy(out_south, out.at[0:18], sems.at[0])
@@ -219,11 +230,12 @@
     place = lax.rem(lax.axis_index("lon"), half)
     turn = jnp.where(diagonal(True), 1.0, 0.0).astype(BF)
     for row in range(4):
-        spread(sh1, row * 32, wide(28 + row, left, own, right), [4, 44], 16, 2)
+        spread(sh1, row * 32, wide(28 + row, inner, own, outer), [4, 44], 16, 2)
     for row in range(14):
         at = 13 - row
-        after = jnp.where(place == 0, own[18 + at, 0:HALO], north_left[at])
-        before = jnp.where(place == half - 1, own[18 + at, 32 - HALO : 32], north_right[at])
+        after, before = in_order(at, north_inner, north_outer)
+        after = jnp.where(place == 0, own[18 + at, 0:HALO], after)
+        before = jnp.where(place == half - 1, own[18 + at, 32 - HALO : 32], before)
         source = jnp.concatenate([before, north[at], after], axis=0)
         turned = jnp.dot(turn, source, preferred_element_type=F32).astype(BF)
         spread(sh1, (row + 4) * 32, turned, [4, 44], 16, 2)
@@ -293,9 +305,13 @@
 
 def edges_call(own):
     return call(
-        edges_kernel, "edges", [(32, HALO, 256), (32, HALO, 256), (DEEP, 32, 256)], [HBM], [VMEM] * 3,
-        [pltpu.SemaphoreType.DMA((3,))], EDGE_CELLS, (own,),
-    )
+        edges_kernel, "edges", [(32, HALO, 256), (32, HALO, 256), (DEEP, 32, 256)], [VMEM], [VMEM] * 3, [],
+        EDGE_CELLS, (own,),
+    )
+
+
+def cut_call(north):
+    return call(cut_kernel, "cut", [(DEEP, HALO, 256)] * 2, [VMEM], [VMEM] * 2, [], 0, (north,))
 
 
 def first_call(*args):
@@ -344,30 +360,36 @@
     return out
 
 
-def around(value, step, ring=1):
+def swap_inner(value):
+    return lax.ppermute(value, "lon", [(i, i ^ 1) for i in range(lax.axis_size("lon"))])
+
+
+def swap_outer(value, ring=1):
     count = lax.axis_size("lon") // ring
-    pairs = [(i, i // count * count + (i + step) % count) for i in range(ring * count)]
-    return lax.ppermute(value, "lon", pairs)
+    return lax.ppermute(
+        value, "lon", [(i, i // count * count + (((i + 1) ^ 1) - 1) % count) for i in range(ring * count)]
+    )
 
 
 def per_device(own, land_sea, w, up, down):
     count = lax.axis_size("lon")
     cols = own.shape[1]
-    head, tail, top = edges_call(own)
-    left = around(tail, 1)
-    right = around(head, -1)
+    to_inner, to_outer, top = edges_call(own)
+    inner = swap_inner(to_inner)
+    outer = swap_outer(to_outer)
     weights = (w, up, down)
     x1_mid, mask, land, land_north = first_call(own, land_sea, *weights)
     top, x1_mid = lax.optimization_barrier((top, x1_mid))
     north = lax.ppermute(top, "lon", [(i, count - 1 - i) for i in range(count)])
     x2_mid = second_call(x1_mid, mask, *weights)
-    x1_tail, x2_tail, out_south = south_call(left, own, right, x1_mid, x2_mid, land, mask, *weights)
+    x1_tail, x2_tail, out_south = south_call(inner, own, outer, x1_mid, x2_mid, land, mask, *weights)
     north, x1_tail = lax.optimization_barrier((north, x1_tail))
-    north_left = around(north[:, :HALO], 1, 2)
-    north_right = around(north[:, cols - HALO :], -1, 2)
+    to_inner, to_outer = cut_call(north)
+    north_inner = swap_inner(to_inner)
+    north_outer = swap_outer(to_outer, 2)
     y1_mid, y2_mid, e1, e2 = fold_call(own, north, x1_tail, land, land_north, *weights)
     return north_call(
-        left, own, right, north, north_left, north_right, x1_tail, x2_tail, out_south, y1_mid, y2_mid, e1, e2, mask, *weights
+        inner, own, outer, north, north_inner, north_outer, x1_tail, x2_tail, out_south, y1_mid, y2_mid, e1, e2, mask, *weights
     )
 
 

time: 34.3 us -> 32.1 us (0.936)
  waiting for transfers between devices: 2.44 us -> 0.01 us
    ppermute x4, waiting for transfers between devices: 2.44 us -> 0.01 us  [the longest x2 0.01 us: swap_inner(): lax.ppermute(value, 'lon', [(i, i ^ 1) for i in range(lax.axis_size('lon'...]
    ppermute x4, starting transfers between devices: 9.89 us -> 10.5 us  [the longest x2 9.2 us: swap_outer(): lax.ppermute(value, 'lon', [(i, i // count * count + ((i + 1 ^ 1) - 1) %...]
    pallas_call x6 -> x7, Pallas kernels: 18.9 us -> 18.7 us  [call(): pl.pallas_call(kernel, name=name, out_shape=tuple((jax.ShapeDtypeStruct(*...]
    unnamed x10 -> x12, local copies, waits for them, and re-layouts: 1.21 us -> 1.21 us
  transfers between devices with their start and end apart: 5 -> 5, of which waited for: 1 -> 0; matrix products, arithmetic and copies ran while one was open for 0% -> 0% of each run, Pallas kernels for 38% -> 41%
where the time goes in v6:
time: 32.1 us; the launch traced here: 31.8 us
  Pallas kernels  18.7 us (58%)
  starting transfers between devices  11.7 us (36%)
  local copies, waits for them, and re-layouts  1.21 us (4%)
    pallas_call x7, Pallas kernels, call(): pl.pallas_call(kernel, name=name, out_shape=tuple((jax.ShapeDtypeStruct(*...  18.7 us
    ppermute x2, starting transfers between devices, swap_outer(): lax.ppermute(value, 'lon', [(i, i // count * count + ((i + 1 ^ 1) - 1) %...  9.2 us
    ppermute x2, starting transfers between devices, swap_inner(): lax.ppermute(value, 'lon', [(i, i ^ 1) for i in range(lax.axis_size('lon'...  1.26 us
    unnamed x12, local copies, waits for them, and re-layouts  1.21 us
    ppermute x1, starting transfers between devices, per_device(): north = lax.ppermute(top, 'lon', [(i, count - 1 - i) for i in range(count)])  1.21 us
  transfers between devices with their start and end apart: 5, of which 0 were waited for; matrix products, arithmetic and copies ran while one was open for 0% of the time, Pallas kernels for 41%

profile of v6, /device:TPU:0, one launch (start us, length us, event | category | flops | bytes accessed | tf_op | source)
XLA Modules:
  0.0 31.8 jit_solution(6588908416389816886)
XLA Ops:
  0.0 0.0 copy-start.2
  0.0 0.0 copy-start.1
  0.0 0.0 copy-start
  0.0 0.0 copy-start.3
  0.0 1.2 %copy-done.3 = bf16[32,32,256]{2,1,0:T(8,128)(2,1)S(1)} copy-done((bf16[32,32,256]{2,1,0:T(8,128)(2,1)S(1)}, bf16[32,32,256]{2,1,0:T(8,128)(2,1)}, u32[]{:S(2)}) %copy-start.3) | copy-done | bytes 524312
  1.2 0.0 copy-start.5
  1.2 0.1 edges.1
  1.3 0.5 %collective-permute-start = (bf16[32,16,256]{2,1,0:T(8,128)(2,1)S(1)}, bf16[32,16,256]{2,1,0:T(8,128)(2,1)S(1)}, u32[]{:S(2)}, u32[]{:S(2)}) collective-permute-start(bf16[32,16,256]{2,1,0:T(8,128)(2,1)S(1)} %get-tuple-element.25), channel_id=1, source_target_pairs={{0,1},{1,0},{2,3},{3,2},{4,5},{5,4},{6,7},{7,6},{8,9},{9,8},{10,11... | collective-permute-start | bytes 786440 | tf_op jit(solution)/shard_map/ppermute | solution.py:364
  1.8 5.7 %collective-permute-start.1 = (bf16[32,16,256]{2,1,0:T(8,128)(2,1)S(1)}, bf16[32,16,256]{2,1,0:T(8,128)(2,1)S(1)}, u32[]{:S(2)}, u32[]{:S(2)}) collective-permute-start(bf16[32,16,256]{2,1,0:T(8,128)(2,1)S(1)} %get-tuple-element.26), channel_id=1, source_target_pairs={{0,15},{1,2},{2,1},{3,4},{4,3},{5,6},{6,5},{7,8},{8,7},{9,10},{10,... | collective-permute-start | bytes 786440 | tf_op jit(solution)/shard_map/ppermute | solution.py:369
  7.5 0.0 copy-done.2
  7.5 0.0 copy-done.1
  7.5 0.0 copy-done
  7.5 0.0 copy-done.5
  7.5 2.4 %first.1 = (bf16[720,256]{1,0:T(8,128)(2,1)S(1)}, bf16[1024,128]{1,0:T(8,128)(2,1)S(1)}, f32[32,64]{1,0:T(8,128)S(1)}, f32[14,64]{1,0:T(8,128)S(1)}) custom-call(bf16[32,32,256]{2,1,0:T(8,128)(2,1)S(1)} %copy-done.3, s32[32,512]{1,0:T(8,128)S(1)} %copy-done.5, bf16[3,9,256,256]{3,2,1,0:T(8,128)(2,1)S(1)} %copy-done, bf16[3,256,1024]{2,1,0:T(8,128)(2,1)S(1)} %copy-done.1, ...), custom_call_target="tpu_custom_call" | custom-call | flops 1604321280 | bytes 1048576 | tf_op jit(solution)/shard_map/first/pallas_call | solution.py:286
  9.9 1.2 %collective-permute-start.2 = (bf16[14,32,256]{2,1,0:T(8,128)(2,1)S(1)}, bf16[14,32,256]{2,1,0:T(8,128)(2,1)S(1)}, u32[]{:S(2)}, u32[]{:S(2)}) collective-permute-start(bf16[14,32,256]{2,1,0:T(8,128)(2,1)S(1)} %get-tuple-element.29), channel_id=1, source_target_pairs={{0,15},{1,14},{2,13},{3,12},{4,11},{5,10},{6,9},{7,8},{8,7},{9,6},... | collective-permute-start | bytes 688136 | tf_op jit(solution)/shard_map/ppermute | solution.py:383
  11.1 1.6 %second.1.x2_mid = bf16[416,256]{1,0:T(8,128)(2,1)S(1)} custom-call(bf16[720,256]{1,0:T(8,128)(2,1)S(1)} %get-tuple-element.30.x1.x1_mid, bf16[1024,128]{1,0:T(8,128)(2,1)S(1)} %get-tuple-element.31.mask, bf16[3,9,256,256]{3,2,1,0:T(8,128)(2,1)S(1)} %copy-done, bf16[3,256,1024]{2,1,0:T(8,128)(2,1)S(1)} %copy-done.1, bf16[3,1024,256]{2,1,0:T(8,128)(2,1)S(1)} %copy-done.2), custom_call_target="tpu_custom_call" | custom-call | flops 926941184 | bytes 1048576 | tf_op jit(solution)/shard_map/second/pallas_call | solution.py:286
  12.7 0.0 collective-permute-done.inner
  12.7 0.0 collective-permute-done.1.outer
  12.7 0.0 copy-start.4
  12.7 6.5 %south.1 = (bf16[448,256]{1,0:T(8,128)(2,1)S(1)}, bf16[768,256]{1,0:T(8,128)(2,1)S(1)}, bf16[18,32,256]{2,1,0:T(8,128)(2,1)S(1)}) custom-call(bf16[32,16,256]{2,1,0:T(8,128)(2,1)S(1)} %collective-permute-done.inner, bf16[32,32,256]{2,1,0:T(8,128)(2,1)S(1)} %copy-done.3, bf16[32,16,256]{2,1,0:T(8,128)(2,1)S(1)} %collective-permute-done.1.outer, ...), custom_call_target="tpu_custom_call" | custom-call | flops 5276434432 | bytes 1048576 | tf_op jit(solution)/shard_map/south/pallas_call | solution.py:286
  19.1 0.0 collective-permute-done.2.north
  19.2 0.7 %collective-permute-start.3 = (bf16[14,16,256]{2,1,0:T(8,128)(2,1)S(1)}, bf16[14,16,256]{2,1,0:T(8,128)(2,1)S(1)}, u32[]{:S(2)}, u32[]{:S(2)}) collective-permute-start(bf16[14,16,256]{2,1,0:T(8,128)(2,1)S(1)} %get-tuple-element.35), channel_id=1, source_target_pairs={{0,1},{1,0},{2,3},{3,2},{4,5},{5,4},{6,7},{7,6},{8,9},{9,8},{10,11... | collective-permute-start | bytes 344072 | tf_op jit(solution)/shard_map/ppermute | solution.py:364
  19.9 3.5 %collective-permute-start.4 = (bf16[14,16,256]{2,1,0:T(8,128)(2,1)S(1)}, bf16[14,16,256]{2,1,0:T(8,128)(2,1)S(1)}, u32[]{:S(2)}, u32[]{:S(2)}) collective-permute-start(bf16[14,16,256]{2,1,0:T(8,128)(2,1)S(1)} %get-tuple-element.36), channel_id=1, source_target_pairs={{0,7},{1,2},{2,1},{3,4},{4,3},{5,6},{6,5},{7,0},{8,15},{9,10},{10,... | collective-permute-start | bytes 344072 | tf_op jit(solution)/shard_map/ppermute | solution.py:369
  23.5 0.0 copy-done.4
  23.5 2.7 %fold.1 = (bf16[336,256]{1,0:T(8,128)(2,1)S(1)}, bf16[224,256]{1,0:T(8,128)(2,1)S(1)}, bf16[448,128]{1,0:T(8,128)(2,1)S(1)}, bf16[448,128]{1,0:T(8,128)(2,1)S(1)}) custom-call(bf16[32,32,256]{2,1,0:T(8,128)(2,1)S(1)} %copy-done.4, bf16[14,32,256]{2,1,0:T(8,128)(2,1)S(1)} %collective-permute-done.2.north, bf16[448,256]{1,0:T(8,128)(2,1)S(1)} %get-tuple-element.37.x1_tail, ...), custom_call_target="tpu_custom_call" | custom-call | flops 1247805440 | bytes 1048576 | tf_op jit(solution)/shard_map/fold/pallas_call | solution.py:286
  26.2 0.0 collective-permute-done.3.north_inner
  26.2 0.0 collective-permute-done.4.north_outer
  26.2 5.4 %north.1 = bf16[32,32,256]{2,1,0:T(8,128)(2,1)} custom-call(bf16[32,16,256]{2,1,0:T(8,128)(2,1)S(1)} %collective-permute-done.inner, bf16[32,32,256]{2,1,0:T(8,128)(2,1)S(1)} %copy-done.4, bf16[32,16,256]{2,1,0:T(8,128)(2,1)S(1)} %collective-permute-done.1.outer, bf16[14,32,256]{2,1,0:T(8,128)(2,1)S(1)} %collective-permute-done.2.north, ...), custom_call_target="tpu_custom_call" | custom-call | flops 2994733056 | bytes 1048576 | tf_op jit(solution)/shard_map/north/pallas_call | solution.py:286
  (1 shorter events, 0.0 us)
Async XLA Ops:
  0.0 7.5 %copy-start.2 = (bf16[3,1024,256]{2,1,0:T(8,128)(2,1)S(1)}, bf16[3,1024,256]{2,1,0:T(8,128)(2,1)}, u32[]{:S(2)}) copy-start(bf16[3,1024,256]{2,1,0:T(8,128)(2,1)} %down.9) | copy-start | bytes 4718596
  0.0 7.5 %copy-start.1 = (bf16[3,256,1024]{2,1,0:T(8,128)(2,1)S(1)}, bf16[3,256,1024]{2,1,0:T(8,128)(2,1)}, u32[]{:S(2)}) copy-start(bf16[3,256,1024]{2,1,0:T(8,128)(2,1)} %up.9) | copy-start | bytes 4718596
  0.0 7.5 %copy-start = (bf16[3,9,256,256]{3,2,1,0:T(8,128)(2,1)S(1)}, bf16[3,9,256,256]{3,2,1,0:T(8,128)(2,1)}, u32[]{:S(2)}) copy-start(bf16[3,9,256,256]{3,2,1,0:T(8,128)(2,1)} %w.9) | copy-start | bytes 10616836
  0.0 1.2 %copy-start.3 = (bf16[32,32,256]{2,1,0:T(8,128)(2,1)S(1)}, bf16[32,32,256]{2,1,0:T(8,128)(2,1)}, u32[]{:S(2)}) copy-start(bf16[32,32,256]{2,1,0:T(8,128)(2,1)} %own.9) | copy-start | bytes 1572868
  1.2 6.3 %copy-start.5 = (s32[32,512]{1,0:T(8,128)S(1)}, s32[32,512]{1,0:T(8,128)}, u32[]{:S(2)}) copy-start(s32[32,512]{1,0:T(8,128)} %land_sea.1) | copy-start | bytes 196612
  1.3 11.4 %collective-permute-start = (bf16[32,16,256]{2,1,0:T(8,128)(2,1)S(1)}, bf16[32,16,256]{2,1,0:T(8,128)(2,1)S(1)}, u32[]{:S(2)}, u32[]{:S(2)}) collective-permute-start(bf16[32,16,256]{2,1,0:T(8,128)(2,1)S(1)} %get-tuple-element.25), channel_id=1, source_target_pairs={{0,1},{1,0},{2,3},{3,2},{4,5},{5,4},{6,7},{7,6},{8,9},{9,8},{10,11... | collective-permute-start | bytes 786440 | tf_op jit(solution)/shard_map/ppermute | solution.py:364
  1.8 10.9 %collective-permute-start.1 = (bf16[32,16,256]{2,1,0:T(8,128)(2,1)S(1)}, bf16[32,16,256]{2,1,0:T(8,128)(2,1)S(1)}, u32[]{:S(2)}, u32[]{:S(2)}) collective-permute-start(bf16[32,16,256]{2,1,0:T(8,128)(2,1)S(1)} %get-tuple-element.26), channel_id=1, source_target_pairs={{0,15},{1,2},{2,1},{3,4},{4,3},{5,6},{6,5},{7,8},{8,7},{9,10},{10,... | collective-permute-start | bytes 786440 | tf_op jit(solution)/shard_map/ppermute | solution.py:369
  9.9 9.3 %collective-permute-start.2 = (bf16[14,32,256]{2,1,0:T(8,128)(2,1)S(1)}, bf16[14,32,256]{2,1,0:T(8,128)(2,1)S(1)}, u32[]{:S(2)}, u32[]{:S(2)}) collective-permute-start(bf16[14,32,256]{2,1,0:T(8,128)(2,1)S(1)} %get-tuple-element.29), channel_id=1, source_target_pairs={{0,15},{1,14},{2,13},{3,12},{4,11},{5,10},{6,9},{7,8},{8,7},{9,6},... | collective-permute-start | bytes 688136 | tf_op jit(solution)/shard_map/ppermute | solution.py:383
  12.7 10.8 %copy-start.4 = (bf16[32,32,256]{2,1,0:T(8,128)(2,1)S(1)}, bf16[32,32,256]{2,1,0:T(8,128)(2,1)}, u32[]{:S(2)}) copy-start(bf16[32,32,256]{2,1,0:T(8,128)(2,1)} %own.9) | copy-start | bytes 1572868
  19.2 7.0 %collective-permute-start.3 = (bf16[14,16,256]{2,1,0:T(8,128)(2,1)S(1)}, bf16[14,16,256]{2,1,0:T(8,128)(2,1)S(1)}, u32[]{:S(2)}, u32[]{:S(2)}) collective-permute-start(bf16[14,16,256]{2,1,0:T(8,128)(2,1)S(1)} %get-tuple-element.35), channel_id=1, source_target_pairs={{0,1},{1,0},{2,3},{3,2},{4,5},{5,4},{6,7},{7,6},{8,9},{9,8},{10,11... | collective-permute-start | bytes 344072 | tf_op jit(solution)/shard_map/ppermute | solution.py:364
  19.9 6.3 %collective-permute-start.4 = (bf16[14,16,256]{2,1,0:T(8,128)(2,1)S(1)}, bf16[14,16,256]{2,1,0:T(8,128)(2,1)S(1)}, u32[]{:S(2)}, u32[]{:S(2)}) collective-permute-start(bf16[14,16,256]{2,1,0:T(8,128)(2,1)S(1)} %get-tuple-element.36), channel_id=1, source_target_pairs={{0,7},{1,2},{2,1},{3,4},{4,3},{5,6},{6,5},{7,0},{8,15},{9,10},{10,... | collective-permute-start | bytes 344072 | tf_op jit(solution)/shard_map/ppermute | solution.py:369

commit v7 on v6

--- a/solution.py
+++ b/solution.py
@@ -137,7 +137,7 @@
     for row in range(32):
         spread(sh1, (row + 2) * 24, own[row], [4], 24, 2)
     conv_norm(0, sh1, 24, -2, [(0, 8, False), (8, 8, False), (16, 8, False), (24, 6, False)], w, nrm)
-    mlp(0, sh1, 24, -2, 0, [16, 14], up, down, m1, nrm, keep(x1, 24, 0))
+    mlp(0, sh1, 24, -2, 0, [10, 10, 10], up, down, m1, nrm, keep(x1, 24, 0))
 
 
 def second_kernel(x1, mask, w, up, down, x2, sh2, nrm, m2):
@@ -147,7 +147,7 @@
     for row in range(30):
         spread(sh2, (row + 4) * 16, x1[row * 24 : (row + 1) * 24], [4], 16, 4)
     conv_norm(1, sh2, 16, -4, [(0, 13, False), (13, 13, False)], w, nrm)
-    mlp(1, sh2, 16, -4, 0, [26], up, down, m2, nrm, keep(x2, 16, 0))
+    mlp(1, sh2, 16, -4, 0, [13, 13], up, down, m2, nrm, keep(x2, 16, 0))
 
 
 def south_kernel(
@@ -247,7 +247,7 @@
         at = row * 32
         values = jnp.concatenate([x1[at : at + 16], x1_mid[row * 24 : (row + 1) * 24], x1[at + 16 : at + 32]], axis=0)
         spread(sh2, (row + 8) * 32, values, [4, 36], 16, 4)
-    conv_norm(1, sh2, 32, 22, [(26, 6, False), (32, 8, True)], w, nrm)
+    conv_norm(1, sh2, 32, 22, [(26, 6, False), (32, 4, True), (36, 4, True)], w, nrm)
     mlp(1, sh2, 32, 22, 26, [7, 7], up, down, e2, nrm, keep(x2, 32, 26), 26)
     for row in range(16):
         spread(sh3, row * 32, x2_tail[row * 48 : (row + 1) * 48], [8], 32, 8)

time: 32.1 us -> 31.9 us (level)
  transfers between devices with their start and end apart: 5 -> 5, of which waited for: 0 -> 0; matrix products, arithmetic and copies ran while one was open for 0% -> 0% of each run, Pallas kernels for 41% -> 42%
where the time goes in v7:
time: 31.9 us; the launch traced here: 31.6 us
  Pallas kernels  18.4 us (58%)
  starting transfers between devices  11.7 us (37%)
  local copies, waits for them, and re-layouts  1.21 us (4%)
    pallas_call x7, Pallas kernels, call(): pl.pallas_call(kernel, name=name, out_shape=tuple((jax.ShapeDtypeStruct(*...  18.4 us
    ppermute x2, starting transfers between devices, swap_outer(): lax.ppermute(value, 'lon', [(i, i // count * count + ((i + 1 ^ 1) - 1) %...  9.25 us
    ppermute x2, starting transfers between devices, swap_inner(): lax.ppermute(value, 'lon', [(i, i ^ 1) for i in range(lax.axis_size('lon'...  1.27 us
    unnamed x12, local copies, waits for them, and re-layouts  1.21 us
    ppermute x1, starting transfers between devices, per_device(): north = lax.ppermute(top, 'lon', [(i, count - 1 - i) for i in range(count)])  1.2 us
  transfers between devices with their start and end apart: 5, of which 0 were waited for; matrix products, arithmetic and copies ran while one was open for 0% of the time, Pallas kernels for 42%

profile of v7, /device:TPU:0, one launch (start us, length us, event | category | flops | bytes accessed | tf_op | source)
XLA Modules:
  0.0 31.6 jit_solution(6370072206007826045)
XLA Ops:
  0.0 0.0 copy-start.2
  0.0 0.0 copy-start.1
  0.0 0.0 copy-start
  0.0 0.0 copy-start.3
  0.0 1.2 %copy-done.3 = bf16[32,32,256]{2,1,0:T(8,128)(2,1)S(1)} copy-done((bf16[32,32,256]{2,1,0:T(8,128)(2,1)S(1)}, bf16[32,32,256]{2,1,0:T(8,128)(2,1)}, u32[]{:S(2)}) %copy-start.3) | copy-done | bytes 524312
  1.2 0.0 copy-start.5
  1.2 0.1 edges.1
  1.3 0.5 %collective-permute-start = (bf16[32,16,256]{2,1,0:T(8,128)(2,1)S(1)}, bf16[32,16,256]{2,1,0:T(8,128)(2,1)S(1)}, u32[]{:S(2)}, u32[]{:S(2)}) collective-permute-start(bf16[32,16,256]{2,1,0:T(8,128)(2,1)S(1)} %get-tuple-element.25), channel_id=1, source_target_pairs={{0,1},{1,0},{2,3},{3,2},{4,5},{5,4},{6,7},{7,6},{8,9},{9,8},{10,11... | collective-permute-start | bytes 786440 | tf_op jit(solution)/shard_map/ppermute | solution.py:364
  1.8 5.7 %collective-permute-start.1 = (bf16[32,16,256]{2,1,0:T(8,128)(2,1)S(1)}, bf16[32,16,256]{2,1,0:T(8,128)(2,1)S(1)}, u32[]{:S(2)}, u32[]{:S(2)}) collective-permute-start(bf16[32,16,256]{2,1,0:T(8,128)(2,1)S(1)} %get-tuple-element.26), channel_id=1, source_target_pairs={{0,15},{1,2},{2,1},{3,4},{4,3},{5,6},{6,5},{7,8},{8,7},{9,10},{10,... | collective-permute-start | bytes 786440 | tf_op jit(solution)/shard_map/ppermute | solution.py:369
  7.5 0.0 copy-done.2
  7.5 0.0 copy-done.1
  7.5 0.0 copy-done
  7.5 0.0 copy-done.5
  7.5 2.3 %first.1 = (bf16[720,256]{1,0:T(8,128)(2,1)S(1)}, bf16[1024,128]{1,0:T(8,128)(2,1)S(1)}, f32[32,64]{1,0:T(8,128)S(1)}, f32[14,64]{1,0:T(8,128)S(1)}) custom-call(bf16[32,32,256]{2,1,0:T(8,128)(2,1)S(1)} %copy-done.3, s32[32,512]{1,0:T(8,128)S(1)} %copy-done.5, bf16[3,9,256,256]{3,2,1,0:T(8,128)(2,1)S(1)} %copy-done, bf16[3,256,1024]{2,1,0:T(8,128)(2,1)S(1)} %copy-done.1, ...), custom_call_target="tpu_custom_call" | custom-call | flops 1604321280 | bytes 1048576 | tf_op jit(solution)/shard_map/first/pallas_call | solution.py:286
  9.8 1.2 %collective-permute-start.2 = (bf16[14,32,256]{2,1,0:T(8,128)(2,1)S(1)}, bf16[14,32,256]{2,1,0:T(8,128)(2,1)S(1)}, u32[]{:S(2)}, u32[]{:S(2)}) collective-permute-start(bf16[14,32,256]{2,1,0:T(8,128)(2,1)S(1)} %get-tuple-element.29), channel_id=1, source_target_pairs={{0,15},{1,14},{2,13},{3,12},{4,11},{5,10},{6,9},{7,8},{8,7},{9,6},... | collective-permute-start | bytes 688136 | tf_op jit(solution)/shard_map/ppermute | solution.py:383
  11.0 1.5 %second.1.x2_mid = bf16[416,256]{1,0:T(8,128)(2,1)S(1)} custom-call(bf16[720,256]{1,0:T(8,128)(2,1)S(1)} %get-tuple-element.30.x1.x1_mid, bf16[1024,128]{1,0:T(8,128)(2,1)S(1)} %get-tuple-element.31.mask, bf16[3,9,256,256]{3,2,1,0:T(8,128)(2,1)S(1)} %copy-done, bf16[3,256,1024]{2,1,0:T(8,128)(2,1)S(1)} %copy-done.1, bf16[3,1024,256]{2,1,0:T(8,128)(2,1)S(1)} %copy-done.2), custom_call_target="tpu_custom_call" | custom-call | flops 926941184 | bytes 1048576 | tf_op jit(solution)/shard_map/second/pallas_call | solution.py:286
  12.5 0.0 collective-permute-done.inner
  12.5 0.0 collective-permute-done.1.outer
  12.5 0.0 copy-start.4
  12.6 6.5 %south.1 = (bf16[448,256]{1,0:T(8,128)(2,1)S(1)}, bf16[768,256]{1,0:T(8,128)(2,1)S(1)}, bf16[18,32,256]{2,1,0:T(8,128)(2,1)S(1)}) custom-call(bf16[32,16,256]{2,1,0:T(8,128)(2,1)S(1)} %collective-permute-done.inner, bf16[32,32,256]{2,1,0:T(8,128)(2,1)S(1)} %copy-done.3, bf16[32,16,256]{2,1,0:T(8,128)(2,1)S(1)} %collective-permute-done.1.outer, ...), custom_call_target="tpu_custom_call" | custom-call | flops 5276434432 | bytes 1048576 | tf_op jit(solution)/shard_map/south/pallas_call | solution.py:286
  19.0 0.0 collective-permute-done.2.north
  19.1 0.7 %collective-permute-start.3 = (bf16[14,16,256]{2,1,0:T(8,128)(2,1)S(1)}, bf16[14,16,256]{2,1,0:T(8,128)(2,1)S(1)}, u32[]{:S(2)}, u32[]{:S(2)}) collective-permute-start(bf16[14,16,256]{2,1,0:T(8,128)(2,1)S(1)} %get-tuple-element.35), channel_id=1, source_target_pairs={{0,1},{1,0},{2,3},{3,2},{4,5},{5,4},{6,7},{7,6},{8,9},{9,8},{10,11... | collective-permute-start | bytes 344072 | tf_op jit(solution)/shard_map/ppermute | solution.py:364
  19.8 3.6 %collective-permute-start.4 = (bf16[14,16,256]{2,1,0:T(8,128)(2,1)S(1)}, bf16[14,16,256]{2,1,0:T(8,128)(2,1)S(1)}, u32[]{:S(2)}, u32[]{:S(2)}) collective-permute-start(bf16[14,16,256]{2,1,0:T(8,128)(2,1)S(1)} %get-tuple-element.36), channel_id=1, source_target_pairs={{0,7},{1,2},{2,1},{3,4},{4,3},{5,6},{6,5},{7,0},{8,15},{9,10},{10,... | collective-permute-start | bytes 344072 | tf_op jit(solution)/shard_map/ppermute | solution.py:369
  23.4 0.0 copy-done.4
  23.4 2.8 %fold.1 = (bf16[336,256]{1,0:T(8,128)(2,1)S(1)}, bf16[224,256]{1,0:T(8,128)(2,1)S(1)}, bf16[448,128]{1,0:T(8,128)(2,1)S(1)}, bf16[448,128]{1,0:T(8,128)(2,1)S(1)}) custom-call(bf16[32,32,256]{2,1,0:T(8,128)(2,1)S(1)} %copy-done.4, bf16[14,32,256]{2,1,0:T(8,128)(2,1)S(1)} %collective-permute-done.2.north, bf16[448,256]{1,0:T(8,128)(2,1)S(1)} %get-tuple-element.37.x1_tail, ...), custom_call_target="tpu_custom_call" | custom-call | flops 1247805440 | bytes 1048576 | tf_op jit(solution)/shard_map/fold/pallas_call | solution.py:286
  26.2 0.0 collective-permute-done.3.north_inner
  26.3 0.0 collective-permute-done.4.north_outer
  26.3 5.2 %north.1 = bf16[32,32,256]{2,1,0:T(8,128)(2,1)} custom-call(bf16[32,16,256]{2,1,0:T(8,128)(2,1)S(1)} %collective-permute-done.inner, bf16[32,32,256]{2,1,0:T(8,128)(2,1)S(1)} %copy-done.4, bf16[32,16,256]{2,1,0:T(8,128)(2,1)S(1)} %collective-permute-done.1.outer, bf16[14,32,256]{2,1,0:T(8,128)(2,1)S(1)} %collective-permute-done.2.north, ...), custom_call_target="tpu_custom_call" | custom-call | flops 2994733056 | bytes 1048576 | tf_op jit(solution)/shard_map/north/pallas_call | solution.py:286
  (1 shorter events, 0.0 us)
Async XLA Ops:
  0.0 7.5 %copy-start.2 = (bf16[3,1024,256]{2,1,0:T(8,128)(2,1)S(1)}, bf16[3,1024,256]{2,1,0:T(8,128)(2,1)}, u32[]{:S(2)}) copy-start(bf16[3,1024,256]{2,1,0:T(8,128)(2,1)} %down.9) | copy-start | bytes 4718596
  0.0 7.5 %copy-start.1 = (bf16[3,256,1024]{2,1,0:T(8,128)(2,1)S(1)}, bf16[3,256,1024]{2,1,0:T(8,128)(2,1)}, u32[]{:S(2)}) copy-start(bf16[3,256,1024]{2,1,0:T(8,128)(2,1)} %up.9) | copy-start | bytes 4718596
  0.0 7.5 %copy-start = (bf16[3,9,256,256]{3,2,1,0:T(8,128)(2,1)S(1)}, bf16[3,9,256,256]{3,2,1,0:T(8,128)(2,1)}, u32[]{:S(2)}) copy-start(bf16[3,9,256,256]{3,2,1,0:T(8,128)(2,1)} %w.9) | copy-start | bytes 10616836
  0.0 1.2 %copy-start.3 = (bf16[32,32,256]{2,1,0:T(8,128)(2,1)S(1)}, bf16[32,32,256]{2,1,0:T(8,128)(2,1)}, u32[]{:S(2)}) copy-start(bf16[32,32,256]{2,1,0:T(8,128)(2,1)} %own.9) | copy-start | bytes 1572868
  1.2 6.3 %copy-start.5 = (s32[32,512]{1,0:T(8,128)S(1)}, s32[32,512]{1,0:T(8,128)}, u32[]{:S(2)}) copy-start(s32[32,512]{1,0:T(8,128)} %land_sea.1) | copy-start | bytes 196612
  1.3 11.3 %collective-permute-start = (bf16[32,16,256]{2,1,0:T(8,128)(2,1)S(1)}, bf16[32,16,256]{2,1,0:T(8,128)(2,1)S(1)}, u32[]{:S(2)}, u32[]{:S(2)}) collective-permute-start(bf16[32,16,256]{2,1,0:T(8,128)(2,1)S(1)} %get-tuple-element.25), channel_id=1, source_target_pairs={{0,1},{1,0},{2,3},{3,2},{4,5},{5,4},{6,7},{7,6},{8,9},{9,8},{10,11... | collective-permute-start | bytes 786440 | tf_op jit(solution)/shard_map/ppermute | solution.py:364
  1.8 10.7 %collective-permute-start.1 = (bf16[32,16,256]{2,1,0:T(8,128)(2,1)S(1)}, bf16[32,16,256]{2,1,0:T(8,128)(2,1)S(1)}, u32[]{:S(2)}, u32[]{:S(2)}) collective-permute-start(bf16[32,16,256]{2,1,0:T(8,128)(2,1)S(1)} %get-tuple-element.26), channel_id=1, source_target_pairs={{0,15},{1,2},{2,1},{3,4},{4,3},{5,6},{6,5},{7,8},{8,7},{9,10},{10,... | collective-permute-start | bytes 786440 | tf_op jit(solution)/shard_map/ppermute | solution.py:369
  9.8 9.2 %collective-permute-start.2 = (bf16[14,32,256]{2,1,0:T(8,128)(2,1)S(1)}, bf16[14,32,256]{2,1,0:T(8,128)(2,1)S(1)}, u32[]{:S(2)}, u32[]{:S(2)}) collective-permute-start(bf16[14,32,256]{2,1,0:T(8,128)(2,1)S(1)} %get-tuple-element.29), channel_id=1, source_target_pairs={{0,15},{1,14},{2,13},{3,12},{4,11},{5,10},{6,9},{7,8},{8,7},{9,6},... | collective-permute-start | bytes 688136 | tf_op jit(solution)/shard_map/ppermute | solution.py:383
  12.5 10.9 %copy-start.4 = (bf16[32,32,256]{2,1,0:T(8,128)(2,1)S(1)}, bf16[32,32,256]{2,1,0:T(8,128)(2,1)}, u32[]{:S(2)}) copy-start(bf16[32,32,256]{2,1,0:T(8,128)(2,1)} %own.9) | copy-start | bytes 1572868
  19.1 7.2 %collective-permute-start.3 = (bf16[14,16,256]{2,1,0:T(8,128)(2,1)S(1)}, bf16[14,16,256]{2,1,0:T(8,128)(2,1)S(1)}, u32[]{:S(2)}, u32[]{:S(2)}) collective-permute-start(bf16[14,16,256]{2,1,0:T(8,128)(2,1)S(1)} %get-tuple-element.35), channel_id=1, source_target_pairs={{0,1},{1,0},{2,3},{3,2},{4,5},{5,4},{6,7},{7,6},{8,9},{9,8},{10,11... | collective-permute-start | bytes 344072 | tf_op jit(solution)/shard_map/ppermute | solution.py:364
  19.8 6.4 %collective-permute-start.4 = (bf16[14,16,256]{2,1,0:T(8,128)(2,1)S(1)}, bf16[14,16,256]{2,1,0:T(8,128)(2,1)S(1)}, u32[]{:S(2)}, u32[]{:S(2)}) collective-permute-start(bf16[14,16,256]{2,1,0:T(8,128)(2,1)S(1)} %get-tuple-element.36), channel_id=1, source_target_pairs={{0,7},{1,2},{2,1},{3,4},{4,3},{5,6},{6,5},{7,0},{8,15},{9,10},{10,... | collective-permute-start | bytes 344072 | tf_op jit(solution)/shard_map/ppermute | solution.py:369

commit v8 on v7

--- a/solution.py
+++ b/solution.py
@@ -50,9 +50,11 @@
         hidden = (0.5 * pre * (1.0 + lax.erf(pre * RSQRT2))).astype(BF)
         branch = jnp.dot(hidden, down_ref[layer], preferred_element_type=F32)
         centre = shifted[1, (row - base) * width : (row - base) * width + size].astype(F32)
-        mask = mask_ref[(row - mask_base) * width : (row - mask_base) * width + size].astype(F32)
-        mask = jnp.concatenate([mask, mask], axis=1)
-        store(row, count, (mask * (centre + branch)).astype(BF))
+        value = centre + branch
+        if mask_ref is not None:
+            mask = mask_ref[(row - mask_base) * width : (row - mask_base) * width + size].astype(F32)
+            value = jnp.concatenate([mask, mask], axis=1) * value
+        store(row, count, value.astype(BF))
         at += size
         row += count
 
@@ -125,24 +127,24 @@
     return jnp.concatenate([before, own[row], after], axis=0)
 
 
-def first_kernel(own, land_sea, w, up, down, x1, mask, land, land_north, sh1, nrm, m1):
+def first_kernel(own, w, up, down, x1, sh1, nrm):
+    clear(sh1, 2 * 24)
+    for row in range(32):
+        spread(sh1, (row + 2) * 24, own[row], [4], 24, 2)
+    conv_norm(0, sh1, 24, -2, [(0, 8, False), (8, 8, False), (16, 8, False), (24, 6, False)], w, nrm)
+    mlp(0, sh1, 24, -2, 0, [10, 10, 10], up, down, None, nrm, keep(x1, 24, 0))
+
+
+def second_kernel(raw, land_sea, w, up, down, x1, x2, mask, land, land_north, sh2, nrm, m2):
     me = lax.axis_index("lon")
     whole = land_sea[...].astype(F32).astype(BF)
     land[...] = window(whole, me * 32 - HALO)
     land_north[...] = window(whole, (lax.axis_size("lon") - 1 - me) * 32 - HALO)[32 - DEEP :]
     cells = spread_mask(land, 0, 32, False)
     mask[...] = cells[:, 16:48].reshape(32 * 32, 128)
-    m1[...] = cells[:30, 20:44].reshape(30 * 24, 128)
-    clear(sh1, 2 * 24)
-    for row in range(32):
-        spread(sh1, (row + 2) * 24, own[row], [4], 24, 2)
-    conv_norm(0, sh1, 24, -2, [(0, 8, False), (8, 8, False), (16, 8, False), (24, 6, False)], w, nrm)
-    mlp(0, sh1, 24, -2, 0, [10, 10, 10], up, down, m1, nrm, keep(x1, 24, 0))
-
-
-def second_kernel(x1, mask, w, up, down, x2, sh2, nrm, m2):
-    for row in range(26):
-        m2[row * 16 : (row + 1) * 16] = mask[row * 32 + 8 : row * 32 + 24]
+    m2[...] = cells[:26, 24:40].reshape(26 * 16, 128)
+    line = cells[:30, 20:44].reshape(30 * 24, 128)
+    x1[...] = raw[...] * jnp.concatenate([line, line], axis=1)
     clear(sh2, 4 * 16)
     for row in range(30):
         spread(sh2, (row + 4) * 16, x1[row * 24 : (row + 1) * 24], [4], 16, 4)
@@ -315,19 +317,19 @@
 
 
 def first_call(*args):
+    (x1,) = call(
+        first_kernel, "first", [(30 * 24, 256)], [VMEM] * len(args), [VMEM],
+        [taps(34, 24), flat(30, 24)], 720, args,
+    )
+    return x1
+
+
+def second_call(*args):
     return call(
-        first_kernel, "first", [(30 * 24, 256), (32 * 32, 128), ((32, 64), F32), ((DEEP, 64), F32)],
-        [VMEM] * len(args), [VMEM] * 4,
-        [taps(34, 24), flat(30, 24), pltpu.VMEM((30 * 24, 128), BF)], 720, args,
-    )
-
-
-def second_call(*args):
-    (x2,) = call(
-        second_kernel, "second", [(26 * 16, 256)], [VMEM] * len(args), [VMEM],
+        second_kernel, "second", [(30 * 24, 256), (26 * 16, 256), (32 * 32, 128), ((32, 64), F32), ((DEEP, 64), F32)],
+        [VMEM] * len(args), [VMEM] * 5,
         [taps(34, 16), flat(26, 16), pltpu.VMEM((26 * 16, 128), BF)], 416, args,
     )
-    return x2
 
 
 def south_call(*args):
@@ -378,10 +380,10 @@
     inner = swap_inner(to_inner)
     outer = swap_outer(to_outer)
     weights = (w, up, down)
-    x1_mid, mask, land, land_north = first_call(own, land_sea, *weights)
+    x1_mid = first_call(own, *weights)
     top, x1_mid = lax.optimization_barrier((top, x1_mid))
     north = lax.ppermute(top, "lon", [(i, count - 1 - i) for i in range(count)])
-    x2_mid = second_call(x1_mid, mask, *weights)
+    x1_mid, x2_mid, mask, land, land_north = second_call(x1_mid, land_sea, *weights)
     x1_tail, x2_tail, out_south = south_call(inner, own, outer, x1_mid, x2_mid, land, mask, *weights)
     north, x1_tail = lax.optimization_barrier((north, x1_tail))
     to_inner, to_outer = cut_call(north)

time: 31.9 us -> 31.9 us (level)
  transfers between devices with their start and end apart: 5 -> 5, of which waited for: 0 -> 0; matrix products, arithmetic and copies ran while one was open for 0% -> 0% of each run, Pallas kernels for 42% -> 41%
where the time goes in v8:
time: 31.9 us; the launch traced here: 31.6 us
  Pallas kernels  18.4 us (58%)
  starting transfers between devices  11.7 us (37%)
  local copies, waits for them, and re-layouts  1.21 us (4%)
    pallas_call x7, Pallas kernels, call(): pl.pallas_call(kernel, name=name, out_shape=tuple((jax.ShapeDtypeStruct(*...  18.4 us
    ppermute x2, starting transfers between devices, swap_outer(): lax.ppermute(value, 'lon', [(i, i // count * count + ((i + 1 ^ 1) - 1) %...  8.97 us
    ppermute x1, starting transfers between devices, per_device(): north = lax.ppermute(top, 'lon', [(i, count - 1 - i) for i in range(count)])  1.46 us
    ppermute x2, starting transfers between devices, swap_inner(): lax.ppermute(value, 'lon', [(i, i ^ 1) for i in range(lax.axis_size('lon'...  1.27 us
    unnamed x12, local copies, waits for them, and re-layouts  1.21 us
  transfers between devices with their start and end apart: 5, of which 0 were waited for; matrix products, arithmetic and copies ran while one was open for 0% of the time, Pallas kernels for 41%

profile of v8, /device:TPU:0, one launch (start us, length us, event | category | flops | bytes accessed | tf_op | source)
XLA Modules:
  0.0 31.6 jit_solution(6094728178440168279)
XLA Ops:
  0.0 0.0 copy-start.2
  0.0 0.0 copy-start.1
  0.0 0.0 copy-start.3
  0.0 1.2 %copy-done.3 = bf16[32,32,256]{2,1,0:T(8,128)(2,1)S(1)} copy-done((bf16[32,32,256]{2,1,0:T(8,128)(2,1)S(1)}, bf16[32,32,256]{2,1,0:T(8,128)(2,1)}, u32[]{:S(2)}) %copy-start.3) | copy-done | bytes 524312
  1.2 0.0 copy-start
  1.2 0.1 edges.1
  1.3 0.5 %collective-permute-start = (bf16[32,16,256]{2,1,0:T(8,128)(2,1)S(1)}, bf16[32,16,256]{2,1,0:T(8,128)(2,1)S(1)}, u32[]{:S(2)}, u32[]{:S(2)}) collective-permute-start(bf16[32,16,256]{2,1,0:T(8,128)(2,1)S(1)} %get-tuple-element.26), channel_id=1, source_target_pairs={{0,1},{1,0},{2,3},{3,2},{4,5},{5,4},{6,7},{7,6},{8,9},{9,8},{10,11... | collective-permute-start | bytes 786440 | tf_op jit(solution)/shard_map/ppermute | solution.py:366
  1.8 0.0 copy-start.5
  1.8 5.7 %collective-permute-start.1 = (bf16[32,16,256]{2,1,0:T(8,128)(2,1)S(1)}, bf16[32,16,256]{2,1,0:T(8,128)(2,1)S(1)}, u32[]{:S(2)}, u32[]{:S(2)}) collective-permute-start(bf16[32,16,256]{2,1,0:T(8,128)(2,1)S(1)} %get-tuple-element.27), channel_id=1, source_target_pairs={{0,15},{1,2},{2,1},{3,4},{4,3},{5,6},{6,5},{7,8},{8,7},{9,10},{10,... | collective-permute-start | bytes 786440 | tf_op jit(solution)/shard_map/ppermute | solution.py:371
  7.4 0.0 copy-done.2
  7.5 0.0 copy-done.1
  7.5 0.0 copy-done
  7.5 2.0 %first.1.raw = bf16[720,256]{1,0:T(8,128)(2,1)S(1)} custom-call(bf16[32,32,256]{2,1,0:T(8,128)(2,1)S(1)} %copy-done.3, bf16[3,9,256,256]{3,2,1,0:T(8,128)(2,1)S(1)} %copy-done, bf16[3,256,1024]{2,1,0:T(8,128)(2,1)S(1)} %copy-done.1, bf16[3,1024,256]{2,1,0:T(8,128)(2,1)S(1)} %copy-done.2), custom_call_target="tpu_custom_call" | custom-call | flops 1604321280 | bytes 1048576 | tf_op jit(solution)/shard_map/first/pallas_call | solution.py:288
  9.4 1.5 %collective-permute-start.2 = (bf16[14,32,256]{2,1,0:T(8,128)(2,1)S(1)}, bf16[14,32,256]{2,1,0:T(8,128)(2,1)S(1)}, u32[]{:S(2)}, u32[]{:S(2)}) collective-permute-start(bf16[14,32,256]{2,1,0:T(8,128)(2,1)S(1)} %get-tuple-element.29), channel_id=1, source_target_pairs={{0,15},{1,14},{2,13},{3,12},{4,11},{5,10},{6,9},{7,8},{8,7},{9,6},... | collective-permute-start | bytes 688136 | tf_op jit(solution)/shard_map/ppermute | solution.py:385
  10.9 0.0 copy-done.5
  10.9 1.9 %second.1 = (bf16[720,256]{1,0:T(8,128)(2,1)S(1)}, bf16[416,256]{1,0:T(8,128)(2,1)S(1)}, bf16[1024,128]{1,0:T(8,128)(2,1)S(1)}, f32[32,64]{1,0:T(8,128)S(1)}, f32[14,64]{1,0:T(8,128)S(1)}) custom-call(bf16[720,256]{1,0:T(8,128)(2,1)S(1)} %first.1.raw, s32[32,512]{1,0:T(8,128)S(1)} %copy-done.5, bf16[3,9,256,256]{3,2,1,0:T(8,128)(2,1)S(1)} %copy-done, ...), custom_call_target="tpu_custom_call" | custom-call | flops 926941184 | bytes 1048576 | tf_op jit(solution)/shard_map/second/pallas_call | solution.py:288
  12.8 0.0 collective-permute-done.inner
  12.8 0.0 collective-permute-done.1.outer
  12.8 0.0 copy-start.4
  12.8 6.5 %south.1 = (bf16[448,256]{1,0:T(8,128)(2,1)S(1)}, bf16[768,256]{1,0:T(8,128)(2,1)S(1)}, bf16[18,32,256]{2,1,0:T(8,128)(2,1)S(1)}) custom-call(bf16[32,16,256]{2,1,0:T(8,128)(2,1)S(1)} %collective-permute-done.inner, bf16[32,32,256]{2,1,0:T(8,128)(2,1)S(1)} %copy-done.3, bf16[32,16,256]{2,1,0:T(8,128)(2,1)S(1)} %collective-permute-done.1.outer, ...), custom_call_target="tpu_custom_call" | custom-call | flops 5276434432 | bytes 1048576 | tf_op jit(solution)/shard_map/south/pallas_call | solution.py:288
  19.3 0.0 collective-permute-done.2.north
  19.3 0.7 %collective-permute-start.3 = (bf16[14,16,256]{2,1,0:T(8,128)(2,1)S(1)}, bf16[14,16,256]{2,1,0:T(8,128)(2,1)S(1)}, u32[]{:S(2)}, u32[]{:S(2)}) collective-permute-start(bf16[14,16,256]{2,1,0:T(8,128)(2,1)S(1)} %get-tuple-element.37), channel_id=1, source_target_pairs={{0,1},{1,0},{2,3},{3,2},{4,5},{5,4},{6,7},{7,6},{8,9},{9,8},{10,11... | collective-permute-start | bytes 344072 | tf_op jit(solution)/shard_map/ppermute | solution.py:366
  20.1 3.3 %collective-permute-start.4 = (bf16[14,16,256]{2,1,0:T(8,128)(2,1)S(1)}, bf16[14,16,256]{2,1,0:T(8,128)(2,1)S(1)}, u32[]{:S(2)}, u32[]{:S(2)}) collective-permute-start(bf16[14,16,256]{2,1,0:T(8,128)(2,1)S(1)} %get-tuple-element.38), channel_id=1, source_target_pairs={{0,7},{1,2},{2,1},{3,4},{4,3},{5,6},{6,5},{7,0},{8,15},{9,10},{10,... | collective-permute-start | bytes 344072 | tf_op jit(solution)/shard_map/ppermute | solution.py:371
  23.4 0.0 copy-done.4
  23.4 2.7 %fold.1 = (bf16[336,256]{1,0:T(8,128)(2,1)S(1)}, bf16[224,256]{1,0:T(8,128)(2,1)S(1)}, bf16[448,128]{1,0:T(8,128)(2,1)S(1)}, bf16[448,128]{1,0:T(8,128)(2,1)S(1)}) custom-call(bf16[32,32,256]{2,1,0:T(8,128)(2,1)S(1)} %copy-done.4, bf16[14,32,256]{2,1,0:T(8,128)(2,1)S(1)} %collective-permute-done.2.north, bf16[448,256]{1,0:T(8,128)(2,1)S(1)} %get-tuple-element.39.x1_tail, ...), custom_call_target="tpu_custom_call" | custom-call | flops 1247805440 | bytes 1048576 | tf_op jit(solution)/shard_map/fold/pallas_call | solution.py:288
  26.0 0.0 collective-permute-done.3.north_inner
  26.0 0.0 collective-permute-done.4.north_outer
  26.1 5.4 %north.1 = bf16[32,32,256]{2,1,0:T(8,128)(2,1)} custom-call(bf16[32,16,256]{2,1,0:T(8,128)(2,1)S(1)} %collective-permute-done.inner, bf16[32,32,256]{2,1,0:T(8,128)(2,1)S(1)} %copy-done.4, bf16[32,16,256]{2,1,0:T(8,128)(2,1)S(1)} %collective-permute-done.1.outer, bf16[14,32,256]{2,1,0:T(8,128)(2,1)S(1)} %collective-permute-done.2.north, ...), custom_call_target="tpu_custom_call" | custom-call | flops 2994733056 | bytes 1048576 | tf_op jit(solution)/shard_map/north/pallas_call | solution.py:288
  (1 shorter events, 0.0 us)
Async XLA Ops:
  0.0 7.5 %copy-start.2 = (bf16[3,1024,256]{2,1,0:T(8,128)(2,1)S(1)}, bf16[3,1024,256]{2,1,0:T(8,128)(2,1)}, u32[]{:S(2)}) copy-start(bf16[3,1024,256]{2,1,0:T(8,128)(2,1)} %down.9) | copy-start | bytes 4718596
  0.0 7.5 %copy-start.1 = (bf16[3,256,1024]{2,1,0:T(8,128)(2,1)S(1)}, bf16[3,256,1024]{2,1,0:T(8,128)(2,1)}, u32[]{:S(2)}) copy-start(bf16[3,256,1024]{2,1,0:T(8,128)(2,1)} %up.9) | copy-start | bytes 4718596
  0.0 1.2 %copy-start.3 = (bf16[32,32,256]{2,1,0:T(8,128)(2,1)S(1)}, bf16[32,32,256]{2,1,0:T(8,128)(2,1)}, u32[]{:S(2)}) copy-start(bf16[32,32,256]{2,1,0:T(8,128)(2,1)} %own.9) | copy-start | bytes 1572868
  1.2 6.3 %copy-start = (bf16[3,9,256,256]{3,2,1,0:T(8,128)(2,1)S(1)}, bf16[3,9,256,256]{3,2,1,0:T(8,128)(2,1)}, u32[]{:S(2)}) copy-start(bf16[3,9,256,256]{3,2,1,0:T(8,128)(2,1)} %w.9) | copy-start | bytes 10616836
  1.3 11.5 %collective-permute-start = (bf16[32,16,256]{2,1,0:T(8,128)(2,1)S(1)}, bf16[32,16,256]{2,1,0:T(8,128)(2,1)S(1)}, u32[]{:S(2)}, u32[]{:S(2)}) collective-permute-start(bf16[32,16,256]{2,1,0:T(8,128)(2,1)S(1)} %get-tuple-element.26), channel_id=1, source_target_pairs={{0,1},{1,0},{2,3},{3,2},{4,5},{5,4},{6,7},{7,6},{8,9},{9,8},{10,11... | collective-permute-start | bytes 786440 | tf_op jit(solution)/shard_map/ppermute | solution.py:366
  1.8 9.1 %copy-start.5 = (s32[32,512]{1,0:T(8,128)S(1)}, s32[32,512]{1,0:T(8,128)}, u32[]{:S(2)}) copy-start(s32[32,512]{1,0:T(8,128)} %land_sea.1) | copy-start | bytes 196612
  1.8 11.0 %collective-permute-start.1 = (bf16[32,16,256]{2,1,0:T(8,128)(2,1)S(1)}, bf16[32,16,256]{2,1,0:T(8,128)(2,1)S(1)}, u32[]{:S(2)}, u32[]{:S(2)}) collective-permute-start(bf16[32,16,256]{2,1,0:T(8,128)(2,1)S(1)} %get-tuple-element.27), channel_id=1, source_target_pairs={{0,15},{1,2},{2,1},{3,4},{4,3},{5,6},{6,5},{7,8},{8,7},{9,10},{10,... | collective-permute-start | bytes 786440 | tf_op jit(solution)/shard_map/ppermute | solution.py:371
  9.4 9.8 %collective-permute-start.2 = (bf16[14,32,256]{2,1,0:T(8,128)(2,1)S(1)}, bf16[14,32,256]{2,1,0:T(8,128)(2,1)S(1)}, u32[]{:S(2)}, u32[]{:S(2)}) collective-permute-start(bf16[14,32,256]{2,1,0:T(8,128)(2,1)S(1)} %get-tuple-element.29), channel_id=1, source_target_pairs={{0,15},{1,14},{2,13},{3,12},{4,11},{5,10},{6,9},{7,8},{8,7},{9,6},... | collective-permute-start | bytes 688136 | tf_op jit(solution)/shard_map/ppermute | solution.py:385
  12.8 10.6 %copy-start.4 = (bf16[32,32,256]{2,1,0:T(8,128)(2,1)S(1)}, bf16[32,32,256]{2,1,0:T(8,128)(2,1)}, u32[]{:S(2)}) copy-start(bf16[32,32,256]{2,1,0:T(8,128)(2,1)} %own.9) | copy-start | bytes 1572868
  19.3 6.7 %collective-permute-start.3 = (bf16[14,16,256]{2,1,0:T(8,128)(2,1)S(1)}, bf16[14,16,256]{2,1,0:T(8,128)(2,1)S(1)}, u32[]{:S(2)}, u32[]{:S(2)}) collective-permute-start(bf16[14,16,256]{2,1,0:T(8,128)(2,1)S(1)} %get-tuple-element.37), channel_id=1, source_target_pairs={{0,1},{1,0},{2,3},{3,2},{4,5},{5,4},{6,7},{7,6},{8,9},{9,8},{10,11... | collective-permute-start | bytes 344072 | tf_op jit(solution)/shard_map/ppermute | solution.py:366
  20.1 6.0 %collective-permute-start.4 = (bf16[14,16,256]{2,1,0:T(8,128)(2,1)S(1)}, bf16[14,16,256]{2,1,0:T(8,128)(2,1)S(1)}, u32[]{:S(2)}, u32[]{:S(2)}) collective-permute-start(bf16[14,16,256]{2,1,0:T(8,128)(2,1)S(1)} %get-tuple-element.38), channel_id=1, source_target_pairs={{0,7},{1,2},{2,1},{3,4},{4,3},{5,6},{6,5},{7,0},{8,15},{9,10},{10,... | collective-permute-start | bytes 344072 | tf_op jit(solution)/shard_map/ppermute | solution.py:371

commit v9 on v7

--- a/solution.py
+++ b/solution.py
@@ -174,7 +174,7 @@
         if row >= 22:
             x1_tail[(row - 22) * 56 : (row - 21) * 56] = values
         spread(sh2, (row + 4) * 32, values, [4, 36], 16, 4)
-    conv_norm(1, sh2, 32, -4, [(0, 7, False), (7, 7, False), (14, 6, False), (20, 6, False)], w, nrm)
+    conv_norm(1, sh2, 32, -4, [(0, 8, False), (8, 6, False), (14, 6, False), (20, 6, False)], w, nrm)
     mlp(1, sh2, 32, -4, 0, [13, 13], up, down, e2, nrm, keep(x2, 32, 0))
     for row in range(26):
         at = row * 32
@@ -187,7 +187,7 @@
     def store3(row, count, value):
         out[row : row + count] = value.reshape(count, 32, 256)
 
-    mlp(2, sh3, 32, -8, 0, [9, 9], up, down, mask, nrm, store3)
+    mlp(2, sh3, 32, -8, 0, [12, 6], up, down, mask, nrm, store3)
 
 
 def strips(cells, left, right):
@@ -248,7 +248,7 @@
         values = jnp.concatenate([x1[at : at + 16], x1_mid[row * 24 : (row + 1) * 24], x1[at + 16 : at + 32]], axis=0)
         spread(sh2, (row + 8) * 32, values, [4, 36], 16, 4)
     conv_norm(1, sh2, 32, 22, [(26, 6, False), (32, 4, True), (36, 4, True)], w, nrm)
-    mlp(1, sh2, 32, 22, 26, [7, 7], up, down, e2, nrm, keep(x2, 32, 26), 26)
+    mlp(1, sh2, 32, 22, 26, [5, 5, 4], up, down, e2, nrm, keep(x2, 32, 26), 26)
     for row in range(16):
         spread(sh3, row * 32, x2_tail[row * 48 : (row + 1) * 48], [8], 32, 8)
     for row in range(14):
@@ -267,7 +267,7 @@
         here.start()
         copies.append(here)
 
-    mlp(2, sh3, 32, 10, 18, [7, 7], up, down, mask, nrm, store3)
+    mlp(2, sh3, 32, 10, 18, [8, 6], up, down, mask, nrm, store3)
     for copy in copies:
         copy.wait()
 

time: 31.9 us -> 31.8 us (level)
  no operation moved by 1% of the time
where the time goes in v9:
time: 31.8 us; the launch traced here: 31.6 us
  Pallas kernels  18.4 us (58%)
  starting transfers between devices  11.7 us (37%)
  local copies, waits for them, and re-layouts  1.21 us (4%)
    pallas_call x7, Pallas kernels, call(): pl.pallas_call(kernel, name=name, out_shape=tuple((jax.ShapeDtypeStruct(*...  18.4 us
    ppermute x2, starting transfers between devices, swap_outer(): lax.ppermute(value, 'lon', [(i, i // count * count + ((i + 1 ^ 1) - 1) %...  9.22 us
    ppermute x2, starting transfers between devices, swap_inner(): lax.ppermute(value, 'lon', [(i, i ^ 1) for i in range(lax.axis_size('lon'...  1.28 us
    unnamed x12, local copies, waits for them, and re-layouts  1.21 us
    ppermute x1, starting transfers between devices, per_device(): north = lax.ppermute(top, 'lon', [(i, count - 1 - i) for i in range(count)])  1.2 us
  transfers between devices with their start and end apart: 5, of which 0 were waited for; matrix products, arithmetic and copies ran while one was open for 0% of the time, Pallas kernels for 42%

profile of v9, /device:TPU:0, one launch (start us, length us, event | category | flops | bytes accessed | tf_op | source)
XLA Modules:
  0.0 31.6 jit_solution(17300603785133038856)
XLA Ops:
  0.0 0.0 copy-start.2
  0.0 0.0 copy-start.1
  0.0 0.0 copy-start
  0.0 0.0 copy-start.3
  0.0 1.2 %copy-done.3 = bf16[32,32,256]{2,1,0:T(8,128)(2,1)S(1)} copy-done((bf16[32,32,256]{2,1,0:T(8,128)(2,1)S(1)}, bf16[32,32,256]{2,1,0:T(8,128)(2,1)}, u32[]{:S(2)}) %copy-start.3) | copy-done | bytes 524312
  1.2 0.0 copy-start.5
  1.2 0.1 edges.1
  1.3 0.5 %collective-permute-start = (bf16[32,16,256]{2,1,0:T(8,128)(2,1)S(1)}, bf16[32,16,256]{2,1,0:T(8,128)(2,1)S(1)}, u32[]{:S(2)}, u32[]{:S(2)}) collective-permute-start(bf16[32,16,256]{2,1,0:T(8,128)(2,1)S(1)} %get-tuple-element.25), channel_id=1, source_target_pairs={{0,1},{1,0},{2,3},{3,2},{4,5},{5,4},{6,7},{7,6},{8,9},{9,8},{10,11... | collective-permute-start | bytes 786440 | tf_op jit(solution)/shard_map/ppermute | solution.py:364
  1.8 5.7 %collective-permute-start.1 = (bf16[32,16,256]{2,1,0:T(8,128)(2,1)S(1)}, bf16[32,16,256]{2,1,0:T(8,128)(2,1)S(1)}, u32[]{:S(2)}, u32[]{:S(2)}) collective-permute-start(bf16[32,16,256]{2,1,0:T(8,128)(2,1)S(1)} %get-tuple-element.26), channel_id=1, source_target_pairs={{0,15},{1,2},{2,1},{3,4},{4,3},{5,6},{6,5},{7,8},{8,7},{9,10},{10,... | collective-permute-start | bytes 786440 | tf_op jit(solution)/shard_map/ppermute | solution.py:369
  7.5 0.0 copy-done.2
  7.5 0.0 copy-done.1
  7.5 0.0 copy-done
  7.5 0.0 copy-done.5
  7.5 2.3 %first.1 = (bf16[720,256]{1,0:T(8,128)(2,1)S(1)}, bf16[1024,128]{1,0:T(8,128)(2,1)S(1)}, f32[32,64]{1,0:T(8,128)S(1)}, f32[14,64]{1,0:T(8,128)S(1)}) custom-call(bf16[32,32,256]{2,1,0:T(8,128)(2,1)S(1)} %copy-done.3, s32[32,512]{1,0:T(8,128)S(1)} %copy-done.5, bf16[3,9,256,256]{3,2,1,0:T(8,128)(2,1)S(1)} %copy-done, bf16[3,256,1024]{2,1,0:T(8,128)(2,1)S(1)} %copy-done.1, ...), custom_call_target="tpu_custom_call" | custom-call | flops 1604321280 | bytes 1048576 | tf_op jit(solution)/shard_map/first/pallas_call | solution.py:286
  9.8 1.2 %collective-permute-start.2 = (bf16[14,32,256]{2,1,0:T(8,128)(2,1)S(1)}, bf16[14,32,256]{2,1,0:T(8,128)(2,1)S(1)}, u32[]{:S(2)}, u32[]{:S(2)}) collective-permute-start(bf16[14,32,256]{2,1,0:T(8,128)(2,1)S(1)} %get-tuple-element.29), channel_id=1, source_target_pairs={{0,15},{1,14},{2,13},{3,12},{4,11},{5,10},{6,9},{7,8},{8,7},{9,6},... | collective-permute-start | bytes 688136 | tf_op jit(solution)/shard_map/ppermute | solution.py:383
  11.0 1.5 %second.1.x2_mid = bf16[416,256]{1,0:T(8,128)(2,1)S(1)} custom-call(bf16[720,256]{1,0:T(8,128)(2,1)S(1)} %get-tuple-element.30.x1.x1_mid, bf16[1024,128]{1,0:T(8,128)(2,1)S(1)} %get-tuple-element.31.mask, bf16[3,9,256,256]{3,2,1,0:T(8,128)(2,1)S(1)} %copy-done, bf16[3,256,1024]{2,1,0:T(8,128)(2,1)S(1)} %copy-done.1, bf16[3,1024,256]{2,1,0:T(8,128)(2,1)S(1)} %copy-done.2), custom_call_target="tpu_custom_call" | custom-call | flops 926941184 | bytes 1048576 | tf_op jit(solution)/shard_map/second/pallas_call | solution.py:286
  12.5 0.0 collective-permute-done.inner
  12.5 0.0 collective-permute-done.1.outer
  12.5 0.0 copy-start.4
  12.6 6.5 %south.1 = (bf16[448,256]{1,0:T(8,128)(2,1)S(1)}, bf16[768,256]{1,0:T(8,128)(2,1)S(1)}, bf16[18,32,256]{2,1,0:T(8,128)(2,1)S(1)}) custom-call(bf16[32,16,256]{2,1,0:T(8,128)(2,1)S(1)} %collective-permute-done.inner, bf16[32,32,256]{2,1,0:T(8,128)(2,1)S(1)} %copy-done.3, bf16[32,16,256]{2,1,0:T(8,128)(2,1)S(1)} %collective-permute-done.1.outer, ...), custom_call_target="tpu_custom_call" | custom-call | flops 5276434432 | bytes 1048576 | tf_op jit(solution)/shard_map/south/pallas_call | solution.py:286
  19.0 0.0 collective-permute-done.2.north
  19.1 0.8 %collective-permute-start.3 = (bf16[14,16,256]{2,1,0:T(8,128)(2,1)S(1)}, bf16[14,16,256]{2,1,0:T(8,128)(2,1)S(1)}, u32[]{:S(2)}, u32[]{:S(2)}) collective-permute-start(bf16[14,16,256]{2,1,0:T(8,128)(2,1)S(1)} %get-tuple-element.35), channel_id=1, source_target_pairs={{0,1},{1,0},{2,3},{3,2},{4,5},{5,4},{6,7},{7,6},{8,9},{9,8},{10,11... | collective-permute-start | bytes 344072 | tf_op jit(solution)/shard_map/ppermute | solution.py:364
  19.8 3.6 %collective-permute-start.4 = (bf16[14,16,256]{2,1,0:T(8,128)(2,1)S(1)}, bf16[14,16,256]{2,1,0:T(8,128)(2,1)S(1)}, u32[]{:S(2)}, u32[]{:S(2)}) collective-permute-start(bf16[14,16,256]{2,1,0:T(8,128)(2,1)S(1)} %get-tuple-element.36), channel_id=1, source_target_pairs={{0,7},{1,2},{2,1},{3,4},{4,3},{5,6},{6,5},{7,0},{8,15},{9,10},{10,... | collective-permute-start | bytes 344072 | tf_op jit(solution)/shard_map/ppermute | solution.py:369
  23.4 0.0 copy-done.4
  23.4 2.8 %fold.1 = (bf16[336,256]{1,0:T(8,128)(2,1)S(1)}, bf16[224,256]{1,0:T(8,128)(2,1)S(1)}, bf16[448,128]{1,0:T(8,128)(2,1)S(1)}, bf16[448,128]{1,0:T(8,128)(2,1)S(1)}) custom-call(bf16[32,32,256]{2,1,0:T(8,128)(2,1)S(1)} %copy-done.4, bf16[14,32,256]{2,1,0:T(8,128)(2,1)S(1)} %collective-permute-done.2.north, bf16[448,256]{1,0:T(8,128)(2,1)S(1)} %get-tuple-element.37.x1_tail, ...), custom_call_target="tpu_custom_call" | custom-call | flops 1247805440 | bytes 1048576 | tf_op jit(solution)/shard_map/fold/pallas_call | solution.py:286
  26.2 0.0 collective-permute-done.3.north_inner
  26.3 0.0 collective-permute-done.4.north_outer
  26.3 5.2 %north.1 = bf16[32,32,256]{2,1,0:T(8,128)(2,1)} custom-call(bf16[32,16,256]{2,1,0:T(8,128)(2,1)S(1)} %collective-permute-done.inner, bf16[32,32,256]{2,1,0:T(8,128)(2,1)S(1)} %copy-done.4, bf16[32,16,256]{2,1,0:T(8,128)(2,1)S(1)} %collective-permute-done.1.outer, bf16[14,32,256]{2,1,0:T(8,128)(2,1)S(1)} %collective-permute-done.2.north, ...), custom_call_target="tpu_custom_call" | custom-call | flops 2994733056 | bytes 1048576 | tf_op jit(solution)/shard_map/north/pallas_call | solution.py:286
  (1 shorter events, 0.0 us)
Async XLA Ops:
  0.0 7.5 %copy-start.2 = (bf16[3,1024,256]{2,1,0:T(8,128)(2,1)S(1)}, bf16[3,1024,256]{2,1,0:T(8,128)(2,1)}, u32[]{:S(2)}) copy-start(bf16[3,1024,256]{2,1,0:T(8,128)(2,1)} %down.9) | copy-start | bytes 4718596
  0.0 7.5 %copy-start.1 = (bf16[3,256,1024]{2,1,0:T(8,128)(2,1)S(1)}, bf16[3,256,1024]{2,1,0:T(8,128)(2,1)}, u32[]{:S(2)}) copy-start(bf16[3,256,1024]{2,1,0:T(8,128)(2,1)} %up.9) | copy-start | bytes 4718596
  0.0 7.5 %copy-start = (bf16[3,9,256,256]{3,2,1,0:T(8,128)(2,1)S(1)}, bf16[3,9,256,256]{3,2,1,0:T(8,128)(2,1)}, u32[]{:S(2)}) copy-start(bf16[3,9,256,256]{3,2,1,0:T(8,128)(2,1)} %w.9) | copy-start | bytes 10616836
  0.0 1.2 %copy-start.3 = (bf16[32,32,256]{2,1,0:T(8,128)(2,1)S(1)}, bf16[32,32,256]{2,1,0:T(8,128)(2,1)}, u32[]{:S(2)}) copy-start(bf16[32,32,256]{2,1,0:T(8,128)(2,1)} %own.9) | copy-start | bytes 1572868
  1.2 6.3 %copy-start.5 = (s32[32,512]{1,0:T(8,128)S(1)}, s32[32,512]{1,0:T(8,128)}, u32[]{:S(2)}) copy-start(s32[32,512]{1,0:T(8,128)} %land_sea.1) | copy-start | bytes 196612
  1.3 11.3 %collective-permute-start = (bf16[32,16,256]{2,1,0:T(8,128)(2,1)S(1)}, bf16[32,16,256]{2,1,0:T(8,128)(2,1)S(1)}, u32[]{:S(2)}, u32[]{:S(2)}) collective-permute-start(bf16[32,16,256]{2,1,0:T(8,128)(2,1)S(1)} %get-tuple-element.25), channel_id=1, source_target_pairs={{0,1},{1,0},{2,3},{3,2},{4,5},{5,4},{6,7},{7,6},{8,9},{9,8},{10,11... | collective-permute-start | bytes 786440 | tf_op jit(solution)/shard_map/ppermute | solution.py:364
  1.8 10.7 %collective-permute-start.1 = (bf16[32,16,256]{2,1,0:T(8,128)(2,1)S(1)}, bf16[32,16,256]{2,1,0:T(8,128)(2,1)S(1)}, u32[]{:S(2)}, u32[]{:S(2)}) collective-permute-start(bf16[32,16,256]{2,1,0:T(8,128)(2,1)S(1)} %get-tuple-element.26), channel_id=1, source_target_pairs={{0,15},{1,2},{2,1},{3,4},{4,3},{5,6},{6,5},{7,8},{8,7},{9,10},{10,... | collective-permute-start | bytes 786440 | tf_op jit(solution)/shard_map/ppermute | solution.py:369
  9.8 9.2 %collective-permute-start.2 = (bf16[14,32,256]{2,1,0:T(8,128)(2,1)S(1)}, bf16[14,32,256]{2,1,0:T(8,128)(2,1)S(1)}, u32[]{:S(2)}, u32[]{:S(2)}) collective-permute-start(bf16[14,32,256]{2,1,0:T(8,128)(2,1)S(1)} %get-tuple-element.29), channel_id=1, source_target_pairs={{0,15},{1,14},{2,13},{3,12},{4,11},{5,10},{6,9},{7,8},{8,7},{9,6},... | collective-permute-start | bytes 688136 | tf_op jit(solution)/shard_map/ppermute | solution.py:383
  12.5 10.9 %copy-start.4 = (bf16[32,32,256]{2,1,0:T(8,128)(2,1)S(1)}, bf16[32,32,256]{2,1,0:T(8,128)(2,1)}, u32[]{:S(2)}) copy-start(bf16[32,32,256]{2,1,0:T(8,128)(2,1)} %own.9) | copy-start | bytes 1572868
  19.1 7.2 %collective-permute-start.3 = (bf16[14,16,256]{2,1,0:T(8,128)(2,1)S(1)}, bf16[14,16,256]{2,1,0:T(8,128)(2,1)S(1)}, u32[]{:S(2)}, u32[]{:S(2)}) collective-permute-start(bf16[14,16,256]{2,1,0:T(8,128)(2,1)S(1)} %get-tuple-element.35), channel_id=1, source_target_pairs={{0,1},{1,0},{2,3},{3,2},{4,5},{5,4},{6,7},{7,6},{8,9},{9,8},{10,11... | collective-permute-start | bytes 344072 | tf_op jit(solution)/shard_map/ppermute | solution.py:364
  19.8 6.4 %collective-permute-start.4 = (bf16[14,16,256]{2,1,0:T(8,128)(2,1)S(1)}, bf16[14,16,256]{2,1,0:T(8,128)(2,1)S(1)}, u32[]{:S(2)}, u32[]{:S(2)}) collective-permute-start(bf16[14,16,256]{2,1,0:T(8,128)(2,1)S(1)} %get-tuple-element.36), channel_id=1, source_target_pairs={{0,7},{1,2},{2,1},{3,4},{4,3},{5,6},{6,5},{7,0},{8,15},{9,10},{10,... | collective-permute-start | bytes 344072 | tf_op jit(solution)/shard_map/ppermute | solution.py:369
